TPU v7x, 32 devices: a whole 2x2x4 slice. The times are simulated.
32 devices in a mesh: dp: 8 (over y, x, core), node: 4 (over z).
Axes of the slice: x: 2, y: 2, z: 4, core: 2. Of those that a mesh axis runs over, the one named last changes fastest.
Arguments:
- hidden_in: bfloat16 [8192, 8192], P(('dp', 'node')), may hold values from -6 to 6
- norm_gain: bfloat16 [8192], replicated, may hold values from 0.5 to 1.5
- weight_codes: bfloat16 [8192, 1024], P('node'), may hold values from -127 to 127
- weight_scales: float32 [8192, 4], P('node'), may hold values from 6.90534e-05 to 0.00069053395
- cotangent: bfloat16 [8192, 1024], P(('dp', 'node')), may hold values from -6 to 6
Outputs:
- values: bfloat16 [8192, 1024], P(('dp', 'node'))
- input_gradient: bfloat16 [8192, 8192], P(('dp', 'node'))
- weight_grad: float32 [8192, 1024], P(('dp', 'node'))
- gain_gradient_mean: float32 [8192], replicated
All inputs are finite; a program needn't handle non-finite values.
Results may differ from a plain program's by a relative error of at most 0.014.
Values may be sent and summed in bfloat16 or wider, within the bound.
No kernel may reach another device: no remote copies, remote signals or barrier semaphores. Data moves between devices by JAX's collectives and lax.ppermute only.
A program may use at most 256 MiB of HBM per device.

v0:
```python
import jax
import jax.numpy as jnp
from jax import lax
from jax.sharding import PartitionSpec as P

D = 8192
KV = 1024
BLOCK = 256


def quantize(blocks):
    scale = (jnp.sqrt(jnp.mean(blocks * blocks, axis=-1, keepdims=True) + 1e-06) / 3.5).astype(
        jnp.bfloat16
    )
    scale = lax.optimization_barrier(scale)
    wide = scale.astype(jnp.float32)
    codes = jnp.clip(blocks / wide, -7.0, 7.0).astype(jnp.bfloat16)
    return (codes, scale)


def restore(codes, scale):
    return codes.astype(jnp.float32) * scale.astype(jnp.float32)


def dequantize(codes, scales):
    count = codes.shape[0]
    wide = codes.astype(jnp.float32).reshape(count, KV // BLOCK, BLOCK) * scales[:, :, None]
    return wide.reshape(count, KV).astype(jnp.bfloat16)


def local(hidden_in, norm_gain, weight_codes, weight_scales, cotangent):
    data_size = lax.axis_size("dp")
    node_size = lax.axis_size("node")
    device_list = data_size * node_size
    input_broadcast = hidden_in.astype(jnp.float32)
    inverse_deviation = lax.rsqrt(
        jnp.mean(input_broadcast * input_broadcast, axis=-1, keepdims=True) + 1e-05
    )
    centered_unit_rows = input_broadcast * inverse_deviation
    gain_broadcast = norm_gain.astype(jnp.float32)
    normed_rows = (centered_unit_rows * gain_broadcast).astype(jnp.bfloat16)
    codes_all, scales_all = (
        lax.all_gather(weight_codes, "node", axis=0, tiled=True),
        lax.all_gather(weight_scales.astype(jnp.bfloat16), "node", axis=0, tiled=True).astype(
            weight_scales.dtype
        ),
    )
    weight = dequantize(codes_all, scales_all)
    values = jnp.dot(normed_rows, weight, preferred_element_type=jnp.float32).astype(jnp.bfloat16)
    normed_gradient = lax.dot_general(
        cotangent, weight, (((1,), (1,)), ((), ())), preferred_element_type=jnp.float32
    ).astype(jnp.bfloat16)
    gradient_broadcast = normed_gradient.astype(jnp.float32)
    gain_scaled_rows = gain_broadcast * gradient_broadcast
    input_gradient = (
        inverse_deviation
        * (
            gain_scaled_rows
            - centered_unit_rows
            * jnp.mean(gain_scaled_rows * centered_unit_rows, axis=-1, keepdims=True)
        )
    ).astype(jnp.bfloat16)
    gain_local_copy = jnp.sum(gradient_broadcast * centered_unit_rows, axis=0)
    gain_gradient_mean = lax.psum(gain_local_copy, ("dp", "node")) / device_list
    partial_value = lax.dot_general(
        normed_rows, cotangent, (((0,), (0,)), ((), ())), preferred_element_type=jnp.float32
    )
    rows_own = D // device_list
    codes_one, scale_one = quantize(
        partial_value.reshape(data_size, node_size, rows_own, KV // BLOCK, BLOCK)
    )
    got_codes, got_scales = (
        lax.all_to_all(codes_one, "node", split_axis=1, concat_axis=0, tiled=True),
        lax.all_to_all(scale_one, "node", split_axis=1, concat_axis=0, tiled=True),
    )
    restored = restore(got_codes, got_scales).reshape(
        node_size, data_size, rows_own, KV // BLOCK, BLOCK
    )
    node_sum = jnp.sum(restored, axis=0)
    codes_two, scale_two = quantize(node_sum)
    back_codes, back_scales = (
        lax.all_to_all(codes_two, "dp", split_axis=0, concat_axis=1, tiled=True),
        lax.all_to_all(scale_two, "dp", split_axis=0, concat_axis=1, tiled=True),
    )
    restored_two = restore(back_codes, back_scales).reshape(data_size, rows_own, KV // BLOCK, BLOCK)
    weight_grad = (jnp.sum(restored_two, axis=0) / device_list).reshape(rows_own, KV)
    return (values, input_gradient, weight_grad, gain_gradient_mean)


def solution(mesh):
    return jax.shard_map(
        local,
        mesh=mesh,
        in_specs=(
            P(("dp", "node"), None),
            P(),
            P("node", None),
            P("node", None),
            P(("dp", "node"), None),
        ),
        out_specs=(P(("dp", "node"), None), P(("dp", "node"), None), P(("dp", "node"), None), P()),
        check_vma=False,
    )
```

profile of v0, /device:TPU:0, one launch (start us, length us, event | category | flops | bytes accessed | tf_op | source)
XLA Modules:
  0.0 987.6 jit_solution(5651859773009234458)
XLA Ops:
  7.2 0.0 copy-start
  7.2 0.0 copy-start.3
  7.2 6.4 copy.61
  13.6 0.0 copy-done.3
  13.6 3.3 fusion.15
  16.9 0.0 copy-done
  16.9 14.7 %fusion.17 = f32[8192,1024]{1,0:T(8,128)} fusion(bf16[256,1024]{1,0:T(8,128)(2,1)S(1)} %copy-done, bf16[256,8192]{0,1:T(8,128)(2,1)} %copy.61, f32[8192]{0:T(1024)S(1)} %convert_element_type.113, f32[256]{0:T(256)S(1)} %add_rsqrt_fusion), kind=kOutput, calls=%fused_computation.28 | convolution fusion | flops 4303355904 | bytes 38306816 | tf_op jit(solution)/shard_map/dot_general | solution.py:65
  31.6 40.1 %reshape.146 = f32[8,4,256,4,256]{4,3,2,1,0:T(4,128)} reshape(f32[8192,1024]{1,0:T(8,128)} %fusion.17) | data formatting | bytes 67108864 | tf_op jit(solution)/shard_map/reshape | solution.py:70
  71.7 14.1 %multiply_reduce_fusion = f32[8,4,256,4]{3,2,1,0:T(8,128)} fusion(f32[8,4,256,4,256]{4,3,2,1,0:T(4,128)} %reshape.146), kind=kLoop, calls=%fused_computation.4 | loop fusion | flops 16744448 | bytes 33685504 | tf_op jit(solution)/shard_map/reduce_sum | solution.py:12
  85.8 2.8 copy.63
  88.7 0.7 fusion.20
  89.4 6.3 all-to-all-start.1
  95.7 0.9 bitcast_convert_fusion
  96.6 2.7 copy.64
  99.3 18.5 %fusion.2 = bf16[8,4,256,4,256]{4,3,2,0,1:T(4,128)(2,1)} fusion(f32[8,4,256,4,256]{4,3,2,1,0:T(4,128)} %reshape.146, f32[8,4,256,4]{3,2,0,1:T(8,128)} %copy.64), kind=kLoop, calls=%fused_computation.6 | loop fusion | flops 25165824 | bytes 50462720 | tf_op jit(solution)/shard_map/convert_element_type | solution.py:17
  117.8 0.0 copy-start.2
  117.8 0.0 all-to-all-done.1
  117.8 7.0 all-to-all-start
  124.8 0.0 all-gather.2.cloned.1.call-start
  124.8 0.7 all-gather.2.cloned.1.call-update
  125.5 0.0 copy-done.2
  125.6 637.5 %all_gather.7 = bf16[8192,4]{0,1:T(4,128)(2,1)S(1)} all-gather(bf16[2048,4]{0,1:T(4,128)(2,1)S(1)} %convert_element_type.116), channel_id=1, replica_groups=mesh['dp'=8,'node'=4] {'node'}, dimensions={0}, use_global_device_ids=true | all-gather | bytes 81920 | tf_op jit(solution)/shard_map/all_gather | solution.py:44
  763.0 2.4 copy.62
  765.5 12.8 %mul.89 = f32[8192,4,256]{2,1,0:T(4,128)} broadcast(f32[8192,4]{1,0:T(8,128)} %copy.62), dimensions={0,1} | broadcast | bytes 33685504 | tf_op jit(solution)/shard_map/mul | solution.py:27
  778.2 27.5 %copy.78 = f32[1024,8,4,256]{3,1,2,0:T(8,128)} copy(f32[1024,8,4,256]{3,2,1,0:T(4,128)} %bitcast.40) | data formatting | bytes 67108864
  805.8 2.7 copy.67
  808.5 0.0 all-to-all-done
  808.5 19.0 %fusion = f32[8,256,4,256]{3,2,1,0:T(4,128)S(1)} fusion(bf16[8,4,256,4,256]{4,3,2,0,1:T(4,128)(2,1)} %all-to-all-done, f32[4,8,256,4]{3,2,1,0:T(8,128)} %copy.67), kind=kLoop, calls=%fused_computation.1 | loop fusion | flops 23068672 | bytes 25296896 | tf_op jit(solution)/shard_map/reduce_sum | solution.py:79
  827.5 0.0 copy-start.1
  827.5 3.2 copy-done.1
  830.6 1.2 fusion.16
  831.9 0.6 fusion.21
  832.5 0.7 bitcast_convert_fusion.2
  833.2 0.4 copy.70
  833.6 3.7 all-to-all-start.3
  837.3 7.0 clamp_convert_fusion
  844.3 0.0 all-gather.2.cloned.1.call-done
  844.3 23.1 %fusion.14 = (f32[8192]{0:T(1024)S(1)}, f32[256]{0:T(256)S(1)}, f32[256,8192]{0,1:T(8,128)}) fusion(bf16[256,8192]{0,1:T(8,128)(2,1)} %copy.61, f32[256]{0:T(256)S(1)} %add_rsqrt_fusion, f32[8192]{0:T(1024)S(1)} %convert_element_type.113, bf16[256,1024]{1,0:T(8,128)(2,1)S(1)} %copy-done, f32[8192,1024]{1,0:T(8,128)} %bitcast.38, ...), kind=kOutput, calls=%fused_computation.21 | convolution fusion | flops 4338999296 | bytes 63506432 | tf_op jit(solution)/shard_map/dot_general | solution.py:50
  867.4 0.0 all-to-all-done.3
  867.4 4.8 all-to-all-start.2
  872.2 6.9 fusion.13
  879.1 6.3 copy.75
  885.5 68.0 %psum.7 = f32[8192]{0:T(1024)S(1)} all-reduce(f32[8192]{0:T(1024)S(1)} %get-tuple-element.32), channel_id=1, replica_groups=mesh['dp'=8,'node'=4] {'dp','node'}, use_global_device_ids=true, to_apply=%region_7.8 | all-reduce | flops 8192 | bytes 65536 | tf_op jit(solution)/shard_map/psum | solution.py:64
  953.5 0.6 broadcast_multiply_fusion
  954.1 19.7 %convolution_convert_fusion.1 = bf16[256,1024]{1,0:T(8,128)(2,1)} fusion(bf16[256,8192]{0,1:T(8,128)(2,1)} %copy.61, f32[8192]{0:T(1024)S(1)} %convert_element_type.113, f32[256]{0:T(256)S(1)} %add_rsqrt_fusion, f32[8192,1024]{1,0:T(8,128)} %bitcast.39, bf16[8192,1024]{1,0:T(8,128)(2,1)} %all-gather.2.cloned.1.call-done), kind=kOutput, calls=%fused_computation.27 | convolution fusion | flops 4328783872 | bytes 55084032 | tf_op jit(solution)/shard_map/dot_general | solution.py:49
  973.8 0.4 copy.72
  974.1 0.0 all-to-all-done.2
  974.1 4.7 multiply_reduce_fusion.1
  978.8 0.2 copy_multiply_fusion.1
  979.1 0.3 copy.74
  979.4 1.3 copy.76
  (6 shorter events, 0.0 us)
Async XLA Ops:
  7.2 9.8 copy-start
  7.2 6.4 copy-start.3
  89.4 28.4 %all-to-all-start.1 = ((bf16[8,4,256,4,1]{2,0,4,3,1:T(8,128)(2,1)}), bf16[8,4,256,4,1]{2,0,4,3,1:T(8,128)(2,1)S(1)}, u32[]{:S(2)}, u32[]{:S(2)}) async-start(bf16[8,4,256,4,1]{2,0,4,3,1:T(8,128)(2,1)} %bitcast.6), calls=%async_computation.1 | async-start | bytes 131072 | tf_op jit(solution)/shard_map/all_to_all | solution.py:74
  117.8 7.8 copy-start.2
  117.8 690.7 %all-to-all-start = ((bf16[8,4,256,4,256]{4,3,2,0,1:T(4,128)(2,1)}), bf16[8,4,256,4,256]{4,3,2,0,1:T(4,128)(2,1)}, u32[]{:S(2)}, u32[]{:S(2)}) async-start(bf16[8,4,256,4,256]{4,3,2,0,1:T(4,128)(2,1)} %fusion.2), calls=%async_computation | async-start | bytes 33554432 | tf_op jit(solution)/shard_map/all_to_all | solution.py:73
  124.8 719.6 %all-gather.2.cloned.1.call-start = ((), (), s32[]{:S(2)}) async-start(), calls=%async_computation.4 | async-start | bytes 20971520 | tf_op jit(solution)/shard_map/all_gather | solution.py:43
  827.5 3.2 copy-start.1
  833.6 33.8 %all-to-all-start.3 = ((bf16[8,256,4,1]{1,2,3,0:T(4,128)(2,1)}), bf16[8,256,4,1]{1,2,3,0:T(4,128)(2,1)S(1)}, u32[]{:S(2)}, u32[]{:S(2)}) async-start(bf16[8,256,4,1]{1,2,3,0:T(4,128)(2,1)} %bitcast.12), calls=%async_computation.3 | async-start | bytes 32768 | tf_op jit(solution)/shard_map/all_to_all | solution.py:83
  867.4 106.7 %all-to-all-start.2 = ((bf16[8,256,4,256]{3,2,1,0:T(4,128)(2,1)}), bf16[8,256,4,256]{3,2,1,0:T(4,128)(2,1)}, u32[]{:S(2)}, u32[]{:S(2)}) async-start(bf16[8,256,4,256]{3,2,1,0:T(4,128)(2,1)} %clamp_convert_fusion), calls=%async_computation.2 | async-start | bytes 8388608 | tf_op jit(solution)/shard_map/all_to_all | solution.py:82
Sparse Core Ops, SparseCore 0:
  127.2 586.7 all-gather.1
where the time goes:
time: 990 us; the launch traced here: 988 us
  blocking collectives  705 us (71%)
  local copies, waits for them, and re-layouts  109 us (11%)
  other arithmetic  78.6 us (8%)
  matrix products  57.4 us (6%)
  starting transfers between devices  21.9 us (2%)
  between operations  14.2 us (1%)
    all_gather x1, blocking collectives, local(): lax.all_gather(weight_scales.astype(jnp.bfloat16), 'node', axis=0, tiled=...  637 us
    psum x1, blocking collectives, local(): gain_gradient_mean = lax.psum(gain_local_copy, ('dp', 'node')) / device_list  68 us
    unnamed x12, local copies, waits for them, and re-layouts  44.8 us
    reshape x1, local copies, waits for them, and re-layouts, local(): partial_value.reshape(data_size, node_size, rows_own, KV // BLOCK, BLOCK)  40.1 us
    convert_element_type x2, other arithmetic, quantize(): codes = jnp.clip(blocks / wide, -7.0, 7.0).astype(jnp.bfloat16)  25.5 us
    dot_general x1, matrix products, local(): lax.dot_general(cotangent, weight, (((1,), (1,)), ((), ())), preferred_el...  23.1 us
  transfers between devices with their start and end apart: 5, of which 0 were waited for; matrix products, arithmetic and copies ran while one was open for 16% of the time, Pallas kernels for 0%

commit v1 on v0

v1 whole, which is shorter than its diff:
```python
import functools

import jax
import jax.numpy as jnp
from jax import lax
from jax.experimental import pallas as pl
from jax.experimental.pallas import tpu as pltpu
from jax.sharding import PartitionSpec as P

BLOCK = 256
CHUNKS = 2
F32 = jnp.float32
BF16 = jnp.bfloat16
VMEM = pl.BlockSpec(memory_space=pltpu.VMEM)
SMEM = pl.BlockSpec(memory_space=pltpu.SMEM)
PARAMS = pltpu.CompilerParams(vmem_limit_bytes=56 * 1024 * 1024)


def scaled(codes, scales):
    parts = [
        (codes[:, j * BLOCK : (j + 1) * BLOCK].astype(F32) * scales[:, j : j + 1]).astype(BF16)
        for j in range(codes.shape[1] // BLOCK)
    ]
    return jnp.concatenate(parts, axis=1)


def clipped(block):
    mean = jnp.mean(block * block, axis=-1, keepdims=True)
    limit = 7.0 * (jnp.sqrt(mean + 1e-06) * (1.0 / 3.5)).astype(BF16).astype(F32)
    return jnp.clip(block, -limit, limit)


def piece_kernel(which, codes, scales, cot, out):
    rows = codes.shape[0]
    out[:rows, :] = scaled(codes[...], scales[...])
    out[rows:, :] = cot[...]


def weight_piece(which, codes, scales, cot, rows):
    tokens, kv = cot.shape
    return pl.pallas_call(
        piece_kernel,
        grid_spec=pltpu.PrefetchScalarGridSpec(
            num_scalar_prefetch=1,
            grid=(1,),
            in_specs=[
                pl.BlockSpec((rows, kv), lambda i, w: (w[0], 0)),
                pl.BlockSpec((rows, scales.shape[1]), lambda i, w: (w[0], 0)),
                pl.BlockSpec((tokens, kv), lambda i, w: (0, 0)),
            ],
            out_specs=pl.BlockSpec((rows + tokens, kv), lambda i, w: (0, 0)),
        ),
        out_shape=jax.ShapeDtypeStruct((rows + tokens, kv), BF16),
        compiler_params=PARAMS,
        name="weight_piece",
    )(which, codes, scales, cot)


def norm_kernel(n, m, me, hidden, gain, *rest):
    outs, rstd, turned = rest[:-2], rest[-2], rest[-1]
    tokens, d = hidden.shape
    own = d // (n * m)
    part = own // CHUNKS
    wide = 512

    def square(i, total):
        h = hidden[:, pl.ds(pl.multiple_of(i * wide, wide), wide)].astype(F32)
        return total + jnp.sum(h * h, axis=-1, keepdims=True)

    total = lax.fori_loop(0, d // wide, square, jnp.zeros((tokens, 1), F32))
    inverse = lax.rsqrt(total * (1.0 / d) + 1e-05)
    rstd[...] = jnp.broadcast_to(inverse, rstd.shape)

    def turn(i, carry):
        at = pl.ds(pl.multiple_of(i * 256, 256), 256)
        x = hidden[:, at].astype(F32) * inverse * gain[:, at]
        turned[at, :] = x.astype(BF16).T
        return carry

    lax.fori_loop(0, d // 256, turn, 0)
    for s in range(n):
        to = lax.rem(me[0] + s, n)
        for k in range(CHUNKS):
            out = outs[s * CHUNKS + k]
            for a in range(m):
                start = pl.multiple_of((a * n + to) * own + k * part, part)
                out[a * part : (a + 1) * part, :] = turned[pl.ds(start, part), :]


def norm_rows(me, hidden, gain, n, m):
    tokens, d = hidden.shape
    part = jax.ShapeDtypeStruct((d // (n * CHUNKS), tokens), BF16)
    got = pl.pallas_call(
        functools.partial(norm_kernel, n, m),
        in_specs=[SMEM, VMEM, VMEM],
        out_specs=[VMEM] * (n * CHUNKS + 1),
        out_shape=[part] * (n * CHUNKS) + [jax.ShapeDtypeStruct((tokens, 128), F32)],
        scratch_shapes=[pltpu.VMEM((d, tokens), BF16)],
        compiler_params=PARAMS,
        name="norm_rows",
    )(me, hidden, gain)
    sends = [got[s * CHUNKS : (s + 1) * CHUNKS] for s in range(n)]
    return sends, got[-1]


def grad_kernel(n, *refs):
    rows, cots, out = refs[:n], refs[n : 2 * n], refs[2 * n]
    kv = out.shape[1]
    for j in range(kv // BLOCK):
        at = slice(j * BLOCK, (j + 1) * BLOCK)
        total = None
        for s in range(n):
            term = clipped(jnp.dot(rows[s][...], cots[s][:, at], preferred_element_type=F32))
            total = term if total is None else total + term
        out[:, at] = clipped(total).astype(BF16)


def node_sum(rows, cots):
    n = len(rows)
    count, tokens = rows[0].shape
    kv = cots[0].shape[1]
    tile = min(128, count)
    return pl.pallas_call(
        functools.partial(grad_kernel, n),
        grid=(count // tile,),
        in_specs=[pl.BlockSpec((tile, tokens), lambda i: (i, 0))] * n
        + [pl.BlockSpec((tokens, kv), lambda i: (0, 0))] * n,
        out_specs=pl.BlockSpec((tile, kv), lambda i: (i, 0)),
        out_shape=jax.ShapeDtypeStruct((count, kv), BF16),
        compiler_params=PARAMS,
        cost_estimate=pl.CostEstimate(
            flops=2 * n * count * tokens * kv,
            bytes_accessed=n * count * tokens * 2 + n * tokens * kv * 2 + count * kv * 2,
            transcendentals=0,
        ),
        name="node_sum",
    )(*rows, *cots)


def project(starts, hidden, gain, rstd, cot, weights, first, values, gains, mean, keep):
    at_start = first
    for array, load in weights:
        rows = array.shape[0]
        tile = min(256, rows)
        for j in range(rows // tile):
            start = pl.multiple_of(starts[at_start] + j * tile, 128)
            at = pl.ds(start, tile)
            w = load(j * tile, tile)
            g = gain[:, at]
            xhat = hidden[:, at].astype(F32) * rstd
            normed = (xhat * g).astype(BF16)
            values[...] += jnp.dot(normed, w, preferred_element_type=F32)
            grad = lax.dot_general(
                cot[...], w, (((1,), (1,)), ((), ())), preferred_element_type=F32
            ).astype(BF16)
            keep(at_start, j * tile, tile, grad)
            product = grad.astype(F32) * xhat
            gains[:, at] = jnp.sum(product, axis=0, keepdims=True)
            mean[...] += jnp.sum(product * g, axis=-1, keepdims=True)
        at_start += 1


def own_kernel(starts, hidden, gain, rstd, cot, codes, scales, values, gains, mean, grads):
    values[...] = jnp.zeros_like(values)
    mean[...] = jnp.zeros_like(mean)

    def load(first, count):
        return scaled(codes[first : first + count, :], scales[first : first + count, :])

    def keep(which, first, count, grad):
        grads[:, first : first + count] = grad

    project(starts, hidden, gain, rstd[:, :1], cot, [(codes, load)], 0, values, gains, mean, keep)


def own_part(starts, hidden, gain, rstd, cot, codes, scales):
    tokens, d = hidden.shape
    kv = cot.shape[1]
    return pl.pallas_call(
        own_kernel,
        in_specs=[SMEM] + [VMEM] * 6,
        out_specs=[VMEM] * 4,
        out_shape=[
            jax.ShapeDtypeStruct((tokens, kv), F32),
            jax.ShapeDtypeStruct((1, d), F32),
            jax.ShapeDtypeStruct((tokens, 128), F32),
            jax.ShapeDtypeStruct((tokens, codes.shape[0]), BF16),
        ],
        compiler_params=PARAMS,
        cost_estimate=pl.CostEstimate(
            flops=4 * tokens * codes.shape[0] * kv,
            bytes_accessed=12 * 1024 * 1024,
            transcendentals=0,
        ),
        name="own_part",
    )(starts, hidden, gain, rstd, cot, codes, scales)


def rest_kernel(count, starts, hidden, gain, rstd, cot, values_in, gains_in, mean_in, own_grads, *refs):
    weights, (values, gains, result, total, mean, grads) = refs[:count], refs[count:]
    total[...] = values_in[...]
    gains[...] = gains_in[...]
    mean[...] = mean_in[...]
    inverse = rstd[:, :1]
    rows = weights[0].shape[0]

    def keep(which, first, size, grad):
        at = (which - 1) * rows + first
        grads[:, at : at + size] = grad

    listed = [(w, functools.partial(lambda w, first, size: w[first : first + size, :], w)) for w in weights]
    project(starts, hidden, gain, inverse, cot, listed, 1, total, gains, mean, keep)
    values[...] = total[...].astype(BF16)
    center = mean[:, :1] * (1.0 / hidden.shape[1])

    def finish(start, size, grad):
        at = pl.ds(pl.multiple_of(start, 128), size)
        xhat = hidden[:, at].astype(F32) * inverse
        t = gain[:, at] * grad.astype(F32)
        result[:, at] = (inverse * (t - xhat * center)).astype(BF16)

    for j in range(own_grads.shape[1] // 128):
        finish(starts[0] + j * 128, 128, own_grads[:, j * 128 : (j + 1) * 128])
    for i in range(count):
        for j in range(rows // 128):
            at = i * rows + j * 128
            finish(starts[i + 1] + j * 128, 128, grads[:, at : at + 128])


def rest_part(starts, hidden, gain, rstd, cot, own, weights):
    tokens, d = hidden.shape
    kv = cot.shape[1]
    count = len(weights)
    width = count * weights[0].shape[0]
    return pl.pallas_call(
        functools.partial(rest_kernel, count),
        in_specs=[SMEM] + [VMEM] * (8 + count),
        out_specs=[VMEM] * 3,
        out_shape=[
            jax.ShapeDtypeStruct((tokens, kv), BF16),
            jax.ShapeDtypeStruct((1, d), F32),
            jax.ShapeDtypeStruct((tokens, d), BF16),
        ],
        scratch_shapes=[
            pltpu.VMEM((tokens, kv), F32),
            pltpu.VMEM((tokens, 128), F32),
            pltpu.VMEM((tokens, width), BF16),
        ],
        compiler_params=PARAMS,
        cost_estimate=pl.CostEstimate(
            flops=4 * tokens * width * kv,
            bytes_accessed=(width * kv + 3 * tokens * d) * 2,
            transcendentals=0,
        ),
        name="rest_part",
    )(starts, hidden, gain, rstd, cot, *own, *weights)


def pair_sum(parts):
    while len(parts) > 1:
        parts = [parts[i] + parts[i + 1] for i in range(0, len(parts), 2)]
    return parts[0]


def exchange_sum(value, axis, size):
    def flip(bit):
        return lax.ppermute(value, axis, [(i, i ^ bit) for i in range(size)])

    return pair_sum([value] + [flip(bit) for bit in range(1, size)])


def local(hidden, gain, codes, scales, cot):
    m, n = lax.axis_size("dp"), lax.axis_size("node")
    a, z = lax.axis_index("dp"), lax.axis_index("node")
    tokens, d = hidden.shape
    kv = cot.shape[1]
    own = d // (m * n)
    pieces = min(m, d // n // 128)
    size = d // n // pieces
    gain = gain.astype(F32).reshape(1, d)
    here = lax.rem(a, pieces)

    chain = weight_piece(here.reshape(1), codes, scales, cot, size)
    up, down = [chain], [chain]
    for s in range(1, n):
        up.append(lax.ppermute(up[-1], "node", [(i, i + 1) for i in range(s - 1, n - 1)]))
        down.append(lax.ppermute(down[-1], "node", [(i + 1, i) for i in range(n - s)]))

    sends, rstd = norm_rows(z.reshape(1), hidden, gain, n, m)
    got = [sends[0]]
    for s in range(1, n):
        shift = [(i, (i + s) % n) for i in range(n)]
        got.append([lax.ppermute(x, "node", shift) for x in sends[s]])

    starts = [z * (d // n)]
    weights, cots = [], [cot]
    odd = []
    for s in range(1, n):
        slot = jnp.where(z >= s, up[s], down[n - s])
        cots.append(slot[size:])
        mine = slot[:size]
        source = lax.rem(z + n - s, n) * (d // n)
        for bit in range(0, pieces, 2):
            part = mine
            if bit:
                part = lax.ppermute(mine, "dp", [(i, i ^ bit) for i in range(m)])
            weights.append(part)
            starts.append(source + lax.bitwise_xor(here, bit) * size)
            odd.append(
                (lax.ppermute(part, "dp", [(i, i ^ 1) for i in range(m)]), source + lax.bitwise_xor(here, bit + 1) * size)
            )
    weights += [w for w, _ in odd]
    starts = jnp.stack(starts + [at for _, at in odd]).astype(jnp.int32)

    first = own_part(starts, hidden, gain, rstd, cot, codes, scales)
    values, gains, input_gradient = rest_part(starts, hidden, gain, rstd, cot, first, weights)
    gains = exchange_sum(exchange_sum(gains, "node", n), "dp", m)
    gain_gradient_mean = gains.reshape(d) * (1.0 / (m * n))

    done = []
    for k in range(CHUNKS):
        total = node_sum([g[k] for g in got], cots)
        back = lax.all_to_all(total.reshape(m, own // CHUNKS, kv), "dp", split_axis=0, concat_axis=0, tiled=True)
        done.append(jnp.sum(back.astype(F32), axis=0) * (1.0 / (m * n)))
    weight_grad = jnp.concatenate(done, axis=0)
    return (values, input_gradient, weight_grad, gain_gradient_mean)


def solution(mesh):
    rows = P(("dp", "node"), None)
    return jax.shard_map(
        local,
        mesh=mesh,
        in_specs=(rows, P(), P("node", None), P("node", None), rows),
        out_specs=(rows, rows, rows, P()),
        check_vma=False,
    )
```

time: 990 us -> 327 us (0.33)
  blocking collectives: 705 us -> 0 us
  waiting for transfers between devices: 0.69 us -> 164 us
  local copies, waits for them, and re-layouts: 109 us -> 5.69 us
  other arithmetic: 78.6 us -> 7.78 us
  Pallas kernels: 0 us -> 64.6 us
  starting transfers between devices: 21.9 us -> 83.5 us
  matrix products: 57.4 us -> 0 us
  between operations: 14.2 us -> 1.04 us
    all_gather x1 -> x0, blocking collectives: 637 us -> none  [local(): lax.all_gather(weight_scales.astype(jnp.bfloat16), 'node', axis=0, tiled=...]
    ppermute x0 -> x43, waiting for transfers between devices: none -> 138 us  [the longest x9 59.1 us: local(): part = lax.ppermute(mine, 'dp', [(i, i ^ bit) for i in range(m)])]
    ppermute x0 -> x43, starting transfers between devices: none -> 75.4 us  [the longest x10 42.6 us: flip(): return lax.ppermute(value, axis, [(i, i ^ bit) for i in range(size)])]
    psum x1 -> x0, blocking collectives: 68 us -> none  [local(): gain_gradient_mean = lax.psum(gain_local_copy, ('dp', 'node')) / device_list]
    pallas_call x0 -> x6, Pallas kernels: none -> 64.6 us  [the longest x2 25.7 us: node_sum(): pl.pallas_call(functools.partial(grad_kernel, n), grid=(count // tile,),...]
    dot_general x3 -> x0, matrix products: 57.4 us -> none  [the longest x1 23.1 us: local(): lax.dot_general(cotangent, weight, (((1,), (1,)), ((), ())), preferred_el...]
    unnamed x12 -> x45, local copies, waits for them, and re-layouts: 44.8 us -> 2.18 us
    reshape x1 -> x0, local copies, waits for them, and re-layouts: 40.1 us -> none  [local(): partial_value.reshape(data_size, node_size, rows_own, KV // BLOCK, BLOCK)]
  transfers between devices with their start and end apart: 5 -> 45, of which waited for: 0 -> 13; matrix products, arithmetic and copies ran while one was open for 16% -> 3% of each run, Pallas kernels for 0% -> 19%
where the time goes in v1:
time: 327 us; the launch traced here: 326 us
  waiting for transfers between devices  164 us (50%)
  starting transfers between devices  83.5 us (26%)
  Pallas kernels  64.6 us (20%)
  other arithmetic  7.78 us (2%)
  local copies, waits for them, and re-layouts  5.69 us (2%)
    ppermute x9, waiting for transfers between devices, local(): part = lax.ppermute(mine, 'dp', [(i, i ^ bit) for i in range(m)])  59.1 us
    ppermute x3, waiting for transfers between devices, local(): lax.ppermute(down[-1], 'node', [(i + 1, i) for i in range(n - s)])  45.7 us
    ppermute x10, starting transfers between devices, flip(): return lax.ppermute(value, axis, [(i, i ^ bit) for i in range(size)])  42.6 us
    pallas_call x2, Pallas kernels, node_sum(): pl.pallas_call(functools.partial(grad_kernel, n), grid=(count // tile,),...  25.7 us
    all_to_all x2, waiting for transfers between devices, local(): lax.all_to_all(total.reshape(m, own // CHUNKS, kv), 'dp', split_axis=0, c...  25.5 us
    ppermute x6, waiting for transfers between devices, local(): got.append([lax.ppermute(x, 'node', shift) for x in sends[s]])  20.8 us
    pallas_call x1, Pallas kernels, rest_part(): pl.pallas_call(functools.partial(rest_kernel, count), in_specs=[SMEM] + [...  18.4 us
    ppermute x10, waiting for transfers between devices, flip(): return lax.ppermute(value, axis, [(i, i ^ bit) for i in range(size)])  12.8 us
  transfers between devices with their start and end apart: 45, of which 13 were waited for; matrix products, arithmetic and copies ran while one was open for 3% of the time, Pallas kernels for 19%

profile of v1, /device:TPU:0, one launch (start us, length us, event | category | flops | bytes accessed | tf_op | source)
XLA Modules:
  0.0 326.5 jit_solution(5364174550118664399)
XLA Ops:
  0.6 2.1 copy.9.scales
  2.7 2.5 weight_piece.1
  5.2 1.3 collective-permute-start.1
  6.5 5.6 %collective-permute-start = (bf16[512,1024]{1,0:T(8,128)(2,1)}, bf16[512,1024]{1,0:T(8,128)(2,1)S(1)}, u32[]{:S(2)}, u32[]{:S(2)}) collective-permute-start(bf16[512,1024]{1,0:T(8,128)(2,1)} %weight_piece.1), channel_id=1, source_target_pairs={{0,1},{1,2},{2,3},{4,5},{5,6},{6,7},{8,9},{9,10},{10,11},{12,13},{... | collective-permute-start | bytes 3145736 | tf_op jit(solution)/shard_map/ppermute | solution.py:286
  12.1 21.4 %collective-permute-done.1 = bf16[512,1024]{1,0:T(8,128)(2,1)S(1)} collective-permute-done((bf16[512,1024]{1,0:T(8,128)(2,1)}, bf16[512,1024]{1,0:T(8,128)(2,1)S(1)}, u32[]{:S(2)}, u32[]{:S(2)}) %collective-permute-start.1) | collective-permute-done | bytes 1048608 | tf_op jit(solution)/shard_map/ppermute | solution.py:287
  33.5 1.3 collective-permute-start.2
  34.8 0.7 collective-permute-start.7
  35.5 24.3 %collective-permute-done.2 = bf16[512,1024]{1,0:T(8,128)(2,1)} collective-permute-done((bf16[512,1024]{1,0:T(8,128)(2,1)S(1)}, bf16[512,1024]{1,0:T(8,128)(2,1)}, u32[]{:S(2)}, u32[]{:S(2)}) %collective-permute-start.2) | collective-permute-done | bytes 1048608 | tf_op jit(solution)/shard_map/ppermute | solution.py:287
  59.8 1.3 collective-permute-start.3
  61.1 1.3 broadcast_select_fusion.1
  62.4 1.1 fusion.1
  63.5 2.3 collective-permute-start.10
  65.8 0.5 collective-permute-start.9
  66.3 0.7 collective-permute-start.8
  67.0 1.6 collective-permute-start.11
  68.7 11.0 %collective-permute-done.10.refs_7_ = bf16[256,1024]{1,0:T(8,128)(2,1)} collective-permute-done((bf16[256,1024]{1,0:T(8,128)(2,1)}, bf16[256,1024]{1,0:T(8,128)(2,1)}, u32[]{:S(2)}, u32[]{:S(2)}) %collective-permute-start.10) | collective-permute-done | bytes 524320 | tf_op jit(solution)/shard_map/ppermute | solution.py:306
  79.6 8.5 %collective-permute-done.9.refs_6_ = bf16[256,1024]{1,0:T(8,128)(2,1)} collective-permute-done((bf16[256,1024]{1,0:T(8,128)(2,1)}, bf16[256,1024]{1,0:T(8,128)(2,1)}, u32[]{:S(2)}, u32[]{:S(2)}) %collective-permute-start.9) | collective-permute-done | bytes 524320 | tf_op jit(solution)/shard_map/ppermute | solution.py:306
  88.2 0.5 collective-permute-start.21
  88.7 1.3 broadcast_select_fusion.2
  90.1 0.9 fusion.2
  91.0 0.5 collective-permute-start.15
  91.5 1.7 collective-permute-start.6
  93.2 0.7 collective-permute-start.5
  94.0 1.0 collective-permute-start.4
  95.1 0.9 fusion
  96.1 1.8 collective-permute-start.14
  97.9 9.3 %collective-permute-done.6.refs_3_ = bf16[256,1024]{1,0:T(8,128)(2,1)S(1)} collective-permute-done((bf16[256,1024]{1,0:T(8,128)(2,1)S(1)}, bf16[256,1024]{1,0:T(8,128)(2,1)S(1)}, u32[]{:S(2)}, u32[]{:S(2)}) %collective-permute-start.6) | collective-permute-done | bytes 524320 | tf_op jit(solution)/shard_map/ppermute | solution.py:306
  107.2 1.0 collective-permute-start.13
  108.2 10.3 %collective-permute-done.5.refs_2_ = bf16[256,1024]{1,0:T(8,128)(2,1)S(1)} collective-permute-done((bf16[256,1024]{1,0:T(8,128)(2,1)S(1)}, bf16[256,1024]{1,0:T(8,128)(2,1)S(1)}, u32[]{:S(2)}, u32[]{:S(2)}) %collective-permute-start.5) | collective-permute-done | bytes 524320 | tf_op jit(solution)/shard_map/ppermute | solution.py:306
  118.5 1.0 collective-permute-start.12
  119.5 0.5 collective-permute-start.17
  120.0 9.8 %collective-permute-done.14.refs_11_ = bf16[256,1024]{1,0:T(8,128)(2,1)} collective-permute-done((bf16[256,1024]{1,0:T(8,128)(2,1)S(1)}, bf16[256,1024]{1,0:T(8,128)(2,1)}, u32[]{:S(2)}, u32[]{:S(2)}) %collective-permute-start.14) | collective-permute-done | bytes 524320 | tf_op jit(solution)/shard_map/ppermute | solution.py:306
  129.8 10.3 %collective-permute-done.13.refs_10_ = bf16[256,1024]{1,0:T(8,128)(2,1)} collective-permute-done((bf16[256,1024]{1,0:T(8,128)(2,1)S(1)}, bf16[256,1024]{1,0:T(8,128)(2,1)}, u32[]{:S(2)}, u32[]{:S(2)}) %collective-permute-start.13) | collective-permute-done | bytes 524320 | tf_op jit(solution)/shard_map/ppermute | solution.py:306
  140.1 0.5 collective-permute-start.25
  140.7 0.7 reshape.34
  141.4 9.5 %norm_rows.1 = (bf16[1024,256]{1,0:T(8,128)(2,1)}, bf16[1024,256]{1,0:T(8,128)(2,1)}, bf16[1024,256]{1,0:T(8,128)(2,1)}, bf16[1024,256]{1,0:T(8,128)(2,1)}, bf16...) custom-call(s32[1]{0:T(128)} %bitcast.26.me, ...), custom_call_target="tpu_custom_call" | custom-call | tf_op jit(solution)/shard_map/norm_rows/pallas_call | solution.py:93
  151.0 0.7 stack.103.starts
  151.7 8.5 %own_part.1 = (f32[256,1024]{1,0:T(8,128)}, f32[1,8192]{1,0:T(1,128)}, f32[256,128]{1,0:T(8,128)}, bf16[256,2048]{1,0:T(8,128)(2,1)}) custom-call(s32[25]{0:T(128)} %stack.103.starts, bf16[256,8192]{1,0:T(8,128)(2,1)} %hidden.5, f32[1,8192]{1,0:T(1,128)} %bitcast.34, f32[256,128]{1,0:T(8,128)} %get-tuple-element.20.rstd, bf16[256,1024]{1,0:T(8,128)(2,1)} %refs_4_.3, ...), custom_call_target="tpu_custom_call" | custom-call | flops 2147483648 | bytes 12582912 | tf_op jit(solution)/shard_map/own_part/pallas_call | solution.py:179
  160.2 2.2 collective-permute-start.27
  162.4 2.4 collective-permute-start.29
  164.9 2.4 collective-permute-start.31
  167.3 18.4 %rest_part.1 = (bf16[256,1024]{1,0:T(8,128)(2,1)}, f32[1,8192]{1,0:T(1,128)}, bf16[256,8192]{1,0:T(8,128)(2,1)}) custom-call(s32[25]{0:T(128)} %stack.103.starts, bf16[256,8192]{1,0:T(8,128)(2,1)} %hidden.5, f32[1,8192]{1,0:T(1,128)} %bitcast.35, f32[256,128]{1,0:T(8,128)} %get-tuple-element.20.rstd, bf16[256,1024]{1,0:T(8,128)(2,1)} %refs_4_.3, ...), custom_call_target="tpu_custom_call" | custom-call | flops 6442450944 | bytes 25165824 | tf_op jit(solution)/shard_map/rest_part/pallas_call | solution.py:235
  185.8 1.8 collective-permute-start.35
  187.6 11.8 %collective-permute-done.28.refs_2_ = bf16[1024,256]{1,0:T(8,128)(2,1)S(1)} collective-permute-done((bf16[1024,256]{1,0:T(8,128)(2,1)S(1)}, bf16[1024,256]{1,0:T(8,128)(2,1)S(1)}, u32[]{:S(2)}, u32[]{:S(2)}) %collective-permute-start.28) | collective-permute-done | bytes 524320 | tf_op jit(solution)/shard_map/ppermute | solution.py:293
  199.4 35.1 %collective-permute-start.33 = (f32[1,8192]{1,0:T(1,128)}, f32[1,8192]{1,0:T(1,128)S(1)}, u32[]{:S(2)}, u32[]{:S(2)}) collective-permute-start(f32[1,8192]{1,0:T(1,128)} %get-tuple-element.35), channel_id=1, source_target_pairs={{0,1},{1,0},{2,3},{3,2},{4,5},{5,4},{6,7},{7,6},{8,9},{9,8},{10,11... | collective-permute-start | bytes 98312 | tf_op jit(solution)/shard_map/ppermute | solution.py:267
  234.5 12.8 %node_sum.2 = bf16[1024,1024]{1,0:T(8,128)(2,1)} custom-call(bf16[1024,256]{1,0:T(8,128)(2,1)} %get-tuple-element.27.refs_0_, bf16[1024,256]{1,0:T(8,128)(2,1)} %copy-done.18, bf16[1024,256]{1,0:T(8,128)(2,1)} %copy-done.19, bf16[1024,256]{1,0:T(8,128)(2,1)} %copy-done.20, bf16[256,1024]{1,0:T(8,128)(2,1)} %refs_4_.3, ...), custom_call_target="tpu_custom_call" | custom-call | flops 2147483648 | bytes 6291456 | tf_op jit(solution)/shard_map/node_sum/pallas_call | solution.py:123
  247.3 3.7 %all-to-all-start = ((bf16[8,128,1024]{2,1,0:T(8,128)(2,1)}), bf16[8,128,1024]{2,1,0:T(8,128)(2,1)S(1)}, u32[]{:S(2)}, u32[]{:S(2)}) async-start(bf16[8,128,1024]{2,1,0:T(8,128)(2,1)} %bitcast.31), calls=%async_computation | async-start | bytes 4194304 | tf_op jit(solution)/shard_map/all_to_all | solution.py:323
  251.1 0.8 collective-permute-start.32
  252.0 2.3 collective-permute-start.42
  254.3 0.6 collective-permute-start.41
  254.9 1.4 collective-permute-start.40
  256.3 0.3 collective-permute-start.39
  256.6 9.0 %collective-permute-done.32.refs_3_ = bf16[1024,256]{1,0:T(8,128)(2,1)S(1)} collective-permute-done((bf16[1024,256]{1,0:T(8,128)(2,1)S(1)}, bf16[1024,256]{1,0:T(8,128)(2,1)S(1)}, u32[]{:S(2)}, u32[]{:S(2)}) %collective-permute-start.32) | collective-permute-done | bytes 524320 | tf_op jit(solution)/shard_map/ppermute | solution.py:293
  265.6 0.6 collective-permute-start.38
  266.2 11.8 %collective-permute-done.42 = f32[1,8192]{1,0:T(1,128)S(1)} collective-permute-done((f32[1,8192]{1,0:T(1,128)S(1)}, f32[1,8192]{1,0:T(1,128)S(1)}, u32[]{:S(2)}, u32[]{:S(2)}) %collective-permute-start.42) | collective-permute-done | bytes 32800 | tf_op jit(solution)/shard_map/ppermute | solution.py:267
  278.0 0.5 collective-permute-start.37
  278.5 1.0 collective-permute-done.41
  279.5 12.8 %node_sum.3 = bf16[1024,1024]{1,0:T(8,128)(2,1)} custom-call(bf16[1024,256]{1,0:T(8,128)(2,1)} %get-tuple-element.31.refs_0_, bf16[1024,256]{1,0:T(8,128)(2,1)} %collective-permute-done.30.refs_1_, bf16[1024,256]{1,0:T(8,128)(2,1)} %collective-permute-done.31.refs_2_, bf16[1024,256]{1,0:T(8,128)(2,1)} %copy-done.21, bf16[256,1024]{1,0:T(8,128)(2,1)} %refs_4_.3, ...), custom_call_target="tpu_custom_call" | custom-call | flops 2147483648 | bytes 6291456 | tf_op jit(solution)/shard_map/node_sum/pallas_call | solution.py:123
  292.3 4.4 %all-to-all-start.1 = ((bf16[8,128,1024]{2,1,0:T(8,128)(2,1)}), bf16[8,128,1024]{2,1,0:T(8,128)(2,1)}, u32[]{:S(2)}, u32[]{:S(2)}) async-start(bf16[8,128,1024]{2,1,0:T(8,128)(2,1)} %bitcast.32), calls=%async_computation.1 | async-start | bytes 4194304 | tf_op jit(solution)/shard_map/all_to_all | solution.py:323
  296.7 0.7 add_multiply_fusion
  297.5 0.3 convert_reduce_fusion.1
  297.9 25.5 %all-to-all-done.1 = bf16[8,128,1024]{2,1,0:T(8,128)(2,1)} async-done(((bf16[8,128,1024]{2,1,0:T(8,128)(2,1)}), bf16[8,128,1024]{2,1,0:T(8,128)(2,1)}, u32[]{:S(2)}, u32[]{:S(2)}) %all-to-all-start.1) | async-done | bytes 2097184 | tf_op jit(solution)/shard_map/all_to_all | solution.py:323
  323.3 2.0 convert_reduce_fusion
  325.4 1.0 pad_maximum_fusion
  (92 shorter events, 0.8 us)
Async XLA Ops:
  5.2 28.3 %collective-permute-start.1 = (bf16[512,1024]{1,0:T(8,128)(2,1)}, bf16[512,1024]{1,0:T(8,128)(2,1)S(1)}, u32[]{:S(2)}, u32[]{:S(2)}) collective-permute-start(bf16[512,1024]{1,0:T(8,128)(2,1)} %weight_piece.1), channel_id=1, source_target_pairs={{1,0},{2,1},{3,2},{5,4},{6,5},{7,6},{9,8},{10,9},{11,10},{13,12},{... | collective-permute-start | bytes 3145736 | tf_op jit(solution)/shard_map/ppermute | solution.py:287
  6.5 28.3 %collective-permute-start = (bf16[512,1024]{1,0:T(8,128)(2,1)}, bf16[512,1024]{1,0:T(8,128)(2,1)S(1)}, u32[]{:S(2)}, u32[]{:S(2)}) collective-permute-start(bf16[512,1024]{1,0:T(8,128)(2,1)} %weight_piece.1), channel_id=1, source_target_pairs={{0,1},{1,2},{2,3},{4,5},{5,6},{6,7},{8,9},{9,10},{10,11},{12,13},{... | collective-permute-start | bytes 3145736 | tf_op jit(solution)/shard_map/ppermute | solution.py:286
  33.5 26.3 %collective-permute-start.2 = (bf16[512,1024]{1,0:T(8,128)(2,1)S(1)}, bf16[512,1024]{1,0:T(8,128)(2,1)}, u32[]{:S(2)}, u32[]{:S(2)}) collective-permute-start(bf16[512,1024]{1,0:T(8,128)(2,1)S(1)} %collective-permute-done.1), channel_id=1, source_target_pairs={{1,0},{2,1},{5,4},{6,5},{9,8},{10,9},{13,12},{14,13},{17,16},{18,1... | collective-permute-start | bytes 3145736 | tf_op jit(solution)/shard_map/ppermute | solution.py:287
  34.8 26.3 %collective-permute-start.7 = (bf16[512,1024]{1,0:T(8,128)(2,1)S(1)}, bf16[512,1024]{1,0:T(8,128)(2,1)S(1)}, u32[]{:S(2)}, u32[]{:S(2)}) collective-permute-start(bf16[512,1024]{1,0:T(8,128)(2,1)S(1)} %collective-permute-done), channel_id=1, source_target_pairs={{1,2},{2,3},{5,6},{6,7},{9,10},{10,11},{13,14},{14,15},{17,18},{18... | collective-permute-start | bytes 3145736 | tf_op jit(solution)/shard_map/ppermute | solution.py:286
  59.8 28.9 %collective-permute-start.3 = (bf16[512,1024]{1,0:T(8,128)(2,1)}, bf16[512,1024]{1,0:T(8,128)(2,1)}, u32[]{:S(2)}, u32[]{:S(2)}) collective-permute-start(bf16[512,1024]{1,0:T(8,128)(2,1)} %collective-permute-done.2), channel_id=1, source_target_pairs={{1,0},{5,4},{9,8},{13,12},{17,16},{21,20},{25,24},{29,28}} | collective-permute-start | bytes 3145736 | tf_op jit(solution)/shard_map/ppermute | solution.py:287
  63.5 16.1 %collective-permute-start.10 = (bf16[256,1024]{1,0:T(8,128)(2,1)}, bf16[256,1024]{1,0:T(8,128)(2,1)}, u32[]{:S(2)}, u32[]{:S(2)}) collective-permute-start(bf16[256,1024]{1,0:T(8,128)(2,1)} %get-tuple-element.39.refs_4_), channel_id=1, source_target_pairs={{0,24},{4,28},{8,16},{12,20},{16,8},{20,12},{24,0},{28,4},{1,25},{... | collective-permute-start | bytes 1572872 | tf_op jit(solution)/shard_map/ppermute | solution.py:306
  65.8 22.4 %collective-permute-start.9 = (bf16[256,1024]{1,0:T(8,128)(2,1)}, bf16[256,1024]{1,0:T(8,128)(2,1)}, u32[]{:S(2)}, u32[]{:S(2)}) collective-permute-start(bf16[256,1024]{1,0:T(8,128)(2,1)} %get-tuple-element.39.refs_4_), channel_id=1, source_target_pairs={{0,16},{4,20},{8,24},{12,28},{16,0},{20,4},{24,8},{28,12},{1,17},{... | collective-permute-start | bytes 1572872 | tf_op jit(solution)/shard_map/ppermute | solution.py:306
  66.3 21.9 %collective-permute-start.8 = (bf16[256,1024]{1,0:T(8,128)(2,1)}, bf16[256,1024]{1,0:T(8,128)(2,1)}, u32[]{:S(2)}, u32[]{:S(2)}) collective-permute-start(bf16[256,1024]{1,0:T(8,128)(2,1)} %get-tuple-element.39.refs_4_), channel_id=1, source_target_pairs={{0,8},{4,12},{8,0},{12,4},{16,24},{20,28},{24,16},{28,20},{1,9},{5... | collective-permute-start | bytes 1572872 | tf_op jit(solution)/shard_map/ppermute | solution.py:306
  67.0 24.5 %collective-permute-start.11 = (bf16[512,1024]{1,0:T(8,128)(2,1)S(1)}, bf16[512,1024]{1,0:T(8,128)(2,1)}, u32[]{:S(2)}, u32[]{:S(2)}) collective-permute-start(bf16[512,1024]{1,0:T(8,128)(2,1)S(1)} %collective-permute-done.7), channel_id=1, source_target_pairs={{2,3},{6,7},{10,11},{14,15},{18,19},{22,23},{26,27},{30,31}} | collective-permute-start | bytes 3145736 | tf_op jit(solution)/shard_map/ppermute | solution.py:286
  79.6 11.3 %collective-permute-start.19 = (bf16[256,1024]{1,0:T(8,128)(2,1)}, bf16[256,1024]{1,0:T(8,128)(2,1)S(1)}, u32[]{:S(2)}, u32[]{:S(2)}) collective-permute-start(bf16[256,1024]{1,0:T(8,128)(2,1)} %get-tuple-element.39.refs_4_), channel_id=1, source_target_pairs={{0,4},{4,0},{8,12},{12,8},{16,20},{20,16},{24,28},{28,24},{1,5},{5... | collective-permute-start | bytes 1572872 | tf_op jit(solution)/shard_map/ppermute | solution.py:310
  88.2 5.1 %collective-permute-start.22 = (bf16[256,1024]{1,0:T(8,128)(2,1)}, bf16[256,1024]{1,0:T(8,128)(2,1)S(1)}, u32[]{:S(2)}, u32[]{:S(2)}) collective-permute-start(bf16[256,1024]{1,0:T(8,128)(2,1)} %collective-permute-done.10.refs_7_), channel_id=1, source_target_pairs={{0,4},{4,0},{8,12},{12,8},{16,20},{20,16},{24,28},{28,24},{1,5},{5... | collective-permute-start | bytes 1572872 | tf_op jit(solution)/shard_map/ppermute | solution.py:310
  88.2 5.8 %collective-permute-start.21 = (bf16[256,1024]{1,0:T(8,128)(2,1)}, bf16[256,1024]{1,0:T(8,128)(2,1)S(1)}, u32[]{:S(2)}, u32[]{:S(2)}) collective-permute-start(bf16[256,1024]{1,0:T(8,128)(2,1)} %collective-permute-done.9.refs_6_), channel_id=1, source_target_pairs={{0,4},{4,0},{8,12},{12,8},{16,20},{20,16},{24,28},{28,24},{1,5},{5... | collective-permute-start | bytes 1572872 | tf_op jit(solution)/shard_map/ppermute | solution.py:310
  88.7 7.3 %collective-permute-start.20 = (bf16[256,1024]{1,0:T(8,128)(2,1)}, bf16[256,1024]{1,0:T(8,128)(2,1)S(1)}, u32[]{:S(2)}, u32[]{:S(2)}) collective-permute-start(bf16[256,1024]{1,0:T(8,128)(2,1)} %collective-permute-done.8.refs_5_), channel_id=1, source_target_pairs={{0,4},{4,0},{8,12},{12,8},{16,20},{20,16},{24,28},{28,24},{1,5},{5... | collective-permute-start | bytes 1572872 | tf_op jit(solution)/shard_map/ppermute | solution.py:310
  90.9 5.0 %copy-start = (bf16[256,1024]{1,0:T(8,128)(2,1)}, bf16[256,1024]{1,0:T(8,128)(2,1)S(1)}, u32[]{:S(2)}) copy-start(bf16[256,1024]{1,0:T(8,128)(2,1)S(1)} %get-tuple-element.41.refs_0_) | copy-start | bytes 1572868
  90.9 5.0 %copy-start.4 = (bf16[256,1024]{1,0:T(8,128)(2,1)}, bf16[256,1024]{1,0:T(8,128)(2,1)S(1)}, u32[]{:S(2)}) copy-start(bf16[256,1024]{1,0:T(8,128)(2,1)S(1)} %collective-permute-done.19.refs_16_) | copy-start | bytes 1572868
  90.9 49.8 %copy-start.3 = (bf16[8192]{0:T(1024)(128)(2,1)S(1)}, bf16[8192]{0:T(1024)(128)(2,1)}, u32[]{:S(2)}) copy-start(bf16[8192]{0:T(1024)(128)(2,1)} %param.6) | copy-start | bytes 49156
  91.0 5.1 %collective-permute-start.15 = (bf16[256,1024]{1,0:T(8,128)(2,1)S(1)}, bf16[256,1024]{1,0:T(8,128)(2,1)S(1)}, u32[]{:S(2)}, u32[]{:S(2)}) collective-permute-start(bf16[256,1024]{1,0:T(8,128)(2,1)S(1)} %get-tuple-element.41.refs_0_), channel_id=1, source_target_pairs={{0,4},{4,0},{8,12},{12,8},{16,20},{20,16},{24,28},{28,24},{1,5},{5... | collective-permute-start | bytes 1572872 | tf_op jit(solution)/shard_map/ppermute | solution.py:310
  91.5 15.7 %collective-permute-start.6 = (bf16[256,1024]{1,0:T(8,128)(2,1)S(1)}, bf16[256,1024]{1,0:T(8,128)(2,1)S(1)}, u32[]{:S(2)}, u32[]{:S(2)}) collective-permute-start(bf16[256,1024]{1,0:T(8,128)(2,1)S(1)} %get-tuple-element.41.refs_0_), channel_id=1, source_target_pairs={{0,24},{4,28},{8,16},{12,20},{16,8},{20,12},{24,0},{28,4},{1,25},{... | collective-permute-start | bytes 1572872 | tf_op jit(solution)/shard_map/ppermute | solution.py:306
  93.2 25.3 %collective-permute-start.5 = (bf16[256,1024]{1,0:T(8,128)(2,1)S(1)}, bf16[256,1024]{1,0:T(8,128)(2,1)S(1)}, u32[]{:S(2)}, u32[]{:S(2)}) collective-permute-start(bf16[256,1024]{1,0:T(8,128)(2,1)S(1)} %get-tuple-element.41.refs_0_), channel_id=1, source_target_pairs={{0,16},{4,20},{8,24},{12,28},{16,0},{20,4},{24,8},{28,12},{1,17},{... | collective-permute-start | bytes 1572872 | tf_op jit(solution)/shard_map/ppermute | solution.py:306
  94.0 25.5 %collective-permute-start.4 = (bf16[256,1024]{1,0:T(8,128)(2,1)S(1)}, bf16[256,1024]{1,0:T(8,128)(2,1)}, u32[]{:S(2)}, u32[]{:S(2)}) collective-permute-start(bf16[256,1024]{1,0:T(8,128)(2,1)S(1)} %get-tuple-element.41.refs_0_), channel_id=1, source_target_pairs={{0,8},{4,12},{8,0},{12,4},{16,24},{20,28},{24,16},{28,20},{1,9},{5... | collective-permute-start | bytes 1572872 | tf_op jit(solution)/shard_map/ppermute | solution.py:306
  96.0 55.0 %copy-start.1 = (bf16[256,1024]{1,0:T(8,128)(2,1)}, bf16[256,1024]{1,0:T(8,128)(2,1)S(1)}, u32[]{:S(2)}) copy-start(bf16[256,1024]{1,0:T(8,128)(2,1)S(1)} %get-tuple-element.37.refs_8_) | copy-start | bytes 1572868
  96.0 44.1 %copy-start.7 = (bf16[256,1024]{1,0:T(8,128)(2,1)}, bf16[256,1024]{1,0:T(8,128)(2,1)S(1)}, u32[]{:S(2)}) copy-start(bf16[256,1024]{1,0:T(8,128)(2,1)S(1)} %collective-permute-done.20.refs_17_) | copy-start | bytes 1572868
  96.0 23.5 %collective-permute-start.23 = (bf16[256,1024]{1,0:T(8,128)(2,1)S(1)}, bf16[256,1024]{1,0:T(8,128)(2,1)S(1)}, u32[]{:S(2)}, u32[]{:S(2)}) collective-permute-start(bf16[256,1024]{1,0:T(8,128)(2,1)S(1)} %get-tuple-element.37.refs_8_), channel_id=1, source_target_pairs={{0,4},{4,0},{8,12},{12,8},{16,20},{20,16},{24,28},{28,24},{1,5},{5... | collective-permute-start | bytes 1572872 | tf_op jit(solution)/shard_map/ppermute | solution.py:310
  96.1 54.8 %copy-start.8 = (bf16[256,1024]{1,0:T(8,128)(2,1)}, bf16[256,1024]{1,0:T(8,128)(2,1)S(1)}, u32[]{:S(2)}) copy-start(bf16[256,1024]{1,0:T(8,128)(2,1)S(1)} %collective-permute-done.15.refs_12_) | copy-start | bytes 1572868
  96.1 33.7 %collective-permute-start.14 = (bf16[256,1024]{1,0:T(8,128)(2,1)S(1)}, bf16[256,1024]{1,0:T(8,128)(2,1)}, u32[]{:S(2)}, u32[]{:S(2)}) collective-permute-start(bf16[256,1024]{1,0:T(8,128)(2,1)S(1)} %get-tuple-element.37.refs_8_), channel_id=1, source_target_pairs={{0,24},{4,28},{8,16},{12,20},{16,8},{20,12},{24,0},{28,4},{1,25},{... | collective-permute-start | bytes 1572872 | tf_op jit(solution)/shard_map/ppermute | solution.py:306
  107.2 43.7 %copy-start.9 = (bf16[256,1024]{1,0:T(8,128)(2,1)}, bf16[256,1024]{1,0:T(8,128)(2,1)S(1)}, u32[]{:S(2)}) copy-start(bf16[256,1024]{1,0:T(8,128)(2,1)S(1)} %collective-permute-done.6.refs_3_) | copy-start | bytes 1572868
  107.2 32.9 %collective-permute-start.13 = (bf16[256,1024]{1,0:T(8,128)(2,1)S(1)}, bf16[256,1024]{1,0:T(8,128)(2,1)}, u32[]{:S(2)}, u32[]{:S(2)}) collective-permute-start(bf16[256,1024]{1,0:T(8,128)(2,1)S(1)} %get-tuple-element.37.refs_8_), channel_id=1, source_target_pairs={{0,16},{4,20},{8,24},{12,28},{16,0},{20,4},{24,8},{28,12},{1,17},{... | collective-permute-start | bytes 1572872 | tf_op jit(solution)/shard_map/ppermute | solution.py:306
  118.5 32.5 %copy-start.10 = (bf16[256,1024]{1,0:T(8,128)(2,1)}, bf16[256,1024]{1,0:T(8,128)(2,1)S(1)}, u32[]{:S(2)}) copy-start(bf16[256,1024]{1,0:T(8,128)(2,1)S(1)} %collective-permute-done.5.refs_2_) | copy-start | bytes 1572868
  118.5 21.6 %collective-permute-start.12 = (bf16[256,1024]{1,0:T(8,128)(2,1)S(1)}, bf16[256,1024]{1,0:T(8,128)(2,1)}, u32[]{:S(2)}, u32[]{:S(2)}) collective-permute-start(bf16[256,1024]{1,0:T(8,128)(2,1)S(1)} %get-tuple-element.37.refs_8_), channel_id=1, source_target_pairs={{0,8},{4,12},{8,0},{12,4},{16,24},{20,28},{24,16},{28,20},{1,9},{5... | collective-permute-start | bytes 1572872 | tf_op jit(solution)/shard_map/ppermute | solution.py:306
  119.5 21.1 %collective-permute-start.18 = (bf16[256,1024]{1,0:T(8,128)(2,1)S(1)}, bf16[256,1024]{1,0:T(8,128)(2,1)S(1)}, u32[]{:S(2)}, u32[]{:S(2)}) collective-permute-start(bf16[256,1024]{1,0:T(8,128)(2,1)S(1)} %collective-permute-done.6.refs_3_), channel_id=1, source_target_pairs={{0,4},{4,0},{8,12},{12,8},{16,20},{20,16},{24,28},{28,24},{1,5},{5... | collective-permute-start | bytes 1572872 | tf_op jit(solution)/shard_map/ppermute | solution.py:310
  119.5 31.5 %copy-start.11 = (bf16[256,1024]{1,0:T(8,128)(2,1)}, bf16[256,1024]{1,0:T(8,128)(2,1)S(1)}, u32[]{:S(2)}) copy-start(bf16[256,1024]{1,0:T(8,128)(2,1)S(1)} %collective-permute-done.23.refs_20_) | copy-start | bytes 1572868
  119.5 40.7 %collective-permute-start.17 = (bf16[256,1024]{1,0:T(8,128)(2,1)S(1)}, bf16[256,1024]{1,0:T(8,128)(2,1)}, u32[]{:S(2)}, u32[]{:S(2)}) collective-permute-start(bf16[256,1024]{1,0:T(8,128)(2,1)S(1)} %collective-permute-done.5.refs_2_), channel_id=1, source_target_pairs={{0,4},{4,0},{8,12},{12,8},{16,20},{20,16},{24,28},{28,24},{1,5},{5... | collective-permute-start | bytes 1572872 | tf_op jit(solution)/shard_map/ppermute | solution.py:310
  129.8 32.5 %collective-permute-start.16 = (bf16[256,1024]{1,0:T(8,128)(2,1)}, bf16[256,1024]{1,0:T(8,128)(2,1)}, u32[]{:S(2)}, u32[]{:S(2)}) collective-permute-start(bf16[256,1024]{1,0:T(8,128)(2,1)} %collective-permute-done.4.refs_1_), channel_id=1, source_target_pairs={{0,4},{4,0},{8,12},{12,8},{16,20},{20,16},{24,28},{28,24},{1,5},{5... | collective-permute-start | bytes 1572872 | tf_op jit(solution)/shard_map/ppermute | solution.py:310
  140.1 22.3 %collective-permute-start.26 = (bf16[256,1024]{1,0:T(8,128)(2,1)}, bf16[256,1024]{1,0:T(8,128)(2,1)}, u32[]{:S(2)}, u32[]{:S(2)}) collective-permute-start(bf16[256,1024]{1,0:T(8,128)(2,1)} %collective-permute-done.14.refs_11_), channel_id=1, source_target_pairs={{0,4},{4,0},{8,12},{12,8},{16,20},{20,16},{24,28},{28,24},{1,5},{5... | collective-permute-start | bytes 1572872 | tf_op jit(solution)/shard_map/ppermute | solution.py:310
  140.1 24.7 %collective-permute-start.25 = (bf16[256,1024]{1,0:T(8,128)(2,1)}, bf16[256,1024]{1,0:T(8,128)(2,1)}, u32[]{:S(2)}, u32[]{:S(2)}) collective-permute-start(bf16[256,1024]{1,0:T(8,128)(2,1)} %collective-permute-done.13.refs_10_), channel_id=1, source_target_pairs={{0,4},{4,0},{8,12},{12,8},{16,20},{20,16},{24,28},{28,24},{1,5},{5... | collective-permute-start | bytes 1572872 | tf_op jit(solution)/shard_map/ppermute | solution.py:310
  140.6 10.4 %copy-start.12 = (bf16[256,1024]{1,0:T(8,128)(2,1)}, bf16[256,1024]{1,0:T(8,128)(2,1)S(1)}, u32[]{:S(2)}) copy-start(bf16[256,1024]{1,0:T(8,128)(2,1)S(1)} %collective-permute-done.18.refs_15_) | copy-start | bytes 1572868
  140.6 24.3 %collective-permute-start.24 = (bf16[256,1024]{1,0:T(8,128)(2,1)}, bf16[256,1024]{1,0:T(8,128)(2,1)}, u32[]{:S(2)}, u32[]{:S(2)}) collective-permute-start(bf16[256,1024]{1,0:T(8,128)(2,1)} %collective-permute-done.12.refs_9_), channel_id=1, source_target_pairs={{0,4},{4,0},{8,12},{12,8},{16,20},{20,16},{24,28},{28,24},{1,5},{5... | collective-permute-start | bytes 1572872 | tf_op jit(solution)/shard_map/ppermute | solution.py:310
  151.7 8.5 %copy-start.17 = (bf16[1024,256]{1,0:T(8,128)(2,1)S(1)}, bf16[1024,256]{1,0:T(8,128)(2,1)}, u32[]{:S(2)}) copy-start(bf16[1024,256]{1,0:T(8,128)(2,1)} %get-tuple-element.28) | copy-start | bytes 1572868
  151.7 10.7 %copy-start.16 = (bf16[1024,256]{1,0:T(8,128)(2,1)S(1)}, bf16[1024,256]{1,0:T(8,128)(2,1)}, u32[]{:S(2)}) copy-start(bf16[1024,256]{1,0:T(8,128)(2,1)} %get-tuple-element.29) | copy-start | bytes 1572868
  151.7 10.7 %copy-start.15 = (bf16[1024,256]{1,0:T(8,128)(2,1)S(1)}, bf16[1024,256]{1,0:T(8,128)(2,1)}, u32[]{:S(2)}) copy-start(bf16[1024,256]{1,0:T(8,128)(2,1)} %get-tuple-element.30) | copy-start | bytes 1572868
  151.7 13.2 %copy-start.14 = (bf16[1024,256]{1,0:T(8,128)(2,1)S(1)}, bf16[1024,256]{1,0:T(8,128)(2,1)}, u32[]{:S(2)}) copy-start(bf16[1024,256]{1,0:T(8,128)(2,1)} %get-tuple-element.33) | copy-start | bytes 1572868
  160.2 25.6 %collective-permute-start.27 = (bf16[1024,256]{1,0:T(8,128)(2,1)S(1)}, bf16[1024,256]{1,0:T(8,128)(2,1)S(1)}, u32[]{:S(2)}, u32[]{:S(2)}) collective-permute-start(bf16[1024,256]{1,0:T(8,128)(2,1)S(1)} %copy-done.17), channel_id=1, source_target_pairs={{0,1},{1,2},{2,3},{3,0},{4,5},{5,6},{6,7},{7,4},{8,9},{9,10},{10,1... | collective-permute-start | bytes 1572872 | tf_op jit(solution)/shard_map/ppermute | solution.py:293
  162.4 37.0 %collective-permute-start.28 = (bf16[1024,256]{1,0:T(8,128)(2,1)S(1)}, bf16[1024,256]{1,0:T(8,128)(2,1)S(1)}, u32[]{:S(2)}, u32[]{:S(2)}) collective-permute-start(bf16[1024,256]{1,0:T(8,128)(2,1)S(1)} %copy-done.16), channel_id=1, source_target_pairs={{0,2},{1,3},{2,0},{3,1},{4,6},{5,7},{6,4},{7,5},{8,10},{9,11},{10,... | collective-permute-start | bytes 1572872 | tf_op jit(solution)/shard_map/ppermute | solution.py:293
  162.4 37.0 %collective-permute-start.29 = (bf16[1024,256]{1,0:T(8,128)(2,1)S(1)}, bf16[1024,256]{1,0:T(8,128)(2,1)S(1)}, u32[]{:S(2)}, u32[]{:S(2)}) collective-permute-start(bf16[1024,256]{1,0:T(8,128)(2,1)S(1)} %copy-done.15), channel_id=1, source_target_pairs={{0,3},{1,0},{2,1},{3,2},{4,7},{5,4},{6,5},{7,6},{8,11},{9,8},{10,9... | collective-permute-start | bytes 1572872 | tf_op jit(solution)/shard_map/ppermute | solution.py:293
  164.8 90.1 %collective-permute-start.30 = (bf16[1024,256]{1,0:T(8,128)(2,1)}, bf16[1024,256]{1,0:T(8,128)(2,1)}, u32[]{:S(2)}, u32[]{:S(2)}) collective-permute-start(bf16[1024,256]{1,0:T(8,128)(2,1)} %get-tuple-element.32), channel_id=1, source_target_pairs={{0,1},{1,2},{2,3},{3,0},{4,5},{5,6},{6,7},{7,4},{8,9},{9,10},{10,1... | collective-permute-start | bytes 1572872 | tf_op jit(solution)/shard_map/ppermute | solution.py:293
  164.9 91.4 %collective-permute-start.31 = (bf16[1024,256]{1,0:T(8,128)(2,1)S(1)}, bf16[1024,256]{1,0:T(8,128)(2,1)}, u32[]{:S(2)}, u32[]{:S(2)}) collective-permute-start(bf16[1024,256]{1,0:T(8,128)(2,1)S(1)} %copy-done.14), channel_id=1, source_target_pairs={{0,2},{1,3},{2,0},{3,1},{4,6},{5,7},{6,4},{7,5},{8,10},{9,11},{10,... | collective-permute-start | bytes 1572872 | tf_op jit(solution)/shard_map/ppermute | solution.py:293
  185.8 48.7 %copy-start.18 = (bf16[1024,256]{1,0:T(8,128)(2,1)}, bf16[1024,256]{1,0:T(8,128)(2,1)S(1)}, u32[]{:S(2)}) copy-start(bf16[1024,256]{1,0:T(8,128)(2,1)S(1)} %collective-permute-done.27.refs_1_) | copy-start | bytes 1572868
  185.8 65.3 %collective-permute-start.35 = (f32[1,8192]{1,0:T(1,128)}, f32[1,8192]{1,0:T(1,128)S(1)}, u32[]{:S(2)}, u32[]{:S(2)}) collective-permute-start(f32[1,8192]{1,0:T(1,128)} %get-tuple-element.35), channel_id=1, source_target_pairs={{0,3},{1,2},{2,1},{3,0},{4,7},{5,6},{6,5},{7,4},{8,11},{9,10},{10,... | collective-permute-start | bytes 98312 | tf_op jit(solution)/shard_map/ppermute | solution.py:267
  199.4 35.1 %copy-start.19 = (bf16[1024,256]{1,0:T(8,128)(2,1)}, bf16[1024,256]{1,0:T(8,128)(2,1)S(1)}, u32[]{:S(2)}) copy-start(bf16[1024,256]{1,0:T(8,128)(2,1)S(1)} %collective-permute-done.28.refs_2_) | copy-start | bytes 1572868
  199.4 52.5 %collective-permute-start.34 = (f32[1,8192]{1,0:T(1,128)}, f32[1,8192]{1,0:T(1,128)S(1)}, u32[]{:S(2)}, u32[]{:S(2)}) collective-permute-start(f32[1,8192]{1,0:T(1,128)} %get-tuple-element.35), channel_id=1, source_target_pairs={{0,2},{1,3},{2,0},{3,1},{4,6},{5,7},{6,4},{7,5},{8,10},{9,11},{10,... | collective-permute-start | bytes 98312 | tf_op jit(solution)/shard_map/ppermute | solution.py:267
  199.4 35.1 %copy-start.20 = (bf16[1024,256]{1,0:T(8,128)(2,1)}, bf16[1024,256]{1,0:T(8,128)(2,1)S(1)}, u32[]{:S(2)}) copy-start(bf16[1024,256]{1,0:T(8,128)(2,1)S(1)} %collective-permute-done.29.refs_3_) | copy-start | bytes 1572868
  199.4 52.5 %collective-permute-start.33 = (f32[1,8192]{1,0:T(1,128)}, f32[1,8192]{1,0:T(1,128)S(1)}, u32[]{:S(2)}, u32[]{:S(2)}) collective-permute-start(f32[1,8192]{1,0:T(1,128)} %get-tuple-element.35), channel_id=1, source_target_pairs={{0,1},{1,0},{2,3},{3,2},{4,5},{5,4},{6,7},{7,6},{8,9},{9,8},{10,11... | collective-permute-start | bytes 98312 | tf_op jit(solution)/shard_map/ppermute | solution.py:267
  247.3 4.5 %copy-start.2 = (f32[1,8192]{1,0:T(1,128)S(1)}, f32[1,8192]{1,0:T(1,128)}, u32[]{:S(2)}) copy-start(f32[1,8192]{1,0:T(1,128)} %get-tuple-element.35) | copy-start | bytes 98308
  247.3 45.0 %all-to-all-start = ((bf16[8,128,1024]{2,1,0:T(8,128)(2,1)}), bf16[8,128,1024]{2,1,0:T(8,128)(2,1)S(1)}, u32[]{:S(2)}, u32[]{:S(2)}) async-start(bf16[8,128,1024]{2,1,0:T(8,128)(2,1)} %bitcast.31), calls=%async_computation | async-start | bytes 4194304 | tf_op jit(solution)/shard_map/all_to_all | solution.py:323
  251.1 14.5 %collective-permute-start.32 = (bf16[1024,256]{1,0:T(8,128)(2,1)S(1)}, bf16[1024,256]{1,0:T(8,128)(2,1)S(1)}, u32[]{:S(2)}, u32[]{:S(2)}) collective-permute-start(bf16[1024,256]{1,0:T(8,128)(2,1)S(1)} %copy-done.13), channel_id=1, source_target_pairs={{0,3},{1,0},{2,1},{3,2},{4,7},{5,4},{6,5},{7,6},{8,11},{9,8},{10,9... | collective-permute-start | bytes 1572872 | tf_op jit(solution)/shard_map/ppermute | solution.py:293
  252.0 26.0 %collective-permute-start.42 = (f32[1,8192]{1,0:T(1,128)S(1)}, f32[1,8192]{1,0:T(1,128)S(1)}, u32[]{:S(2)}, u32[]{:S(2)}) collective-permute-start(f32[1,8192]{1,0:T(1,128)S(1)} %add_add_fusion), channel_id=1, source_target_pairs={{0,28},{4,24},{8,20},{12,16},{16,12},{20,8},{24,4},{28,0},{1,29},{... | collective-permute-start | bytes 98312 | tf_op jit(solution)/shard_map/ppermute | solution.py:267
  254.3 25.2 %collective-permute-start.41 = (f32[1,8192]{1,0:T(1,128)S(1)}, f32[1,8192]{1,0:T(1,128)S(1)}, u32[]{:S(2)}, u32[]{:S(2)}) collective-permute-start(f32[1,8192]{1,0:T(1,128)S(1)} %add_add_fusion), channel_id=1, source_target_pairs={{0,24},{4,28},{8,16},{12,20},{16,8},{20,12},{24,0},{28,4},{1,25},{... | collective-permute-start | bytes 98312 | tf_op jit(solution)/shard_map/ppermute | solution.py:267
  254.9 41.8 %collective-permute-start.40 = (f32[1,8192]{1,0:T(1,128)S(1)}, f32[1,8192]{1,0:T(1,128)S(1)}, u32[]{:S(2)}, u32[]{:S(2)}) collective-permute-start(f32[1,8192]{1,0:T(1,128)S(1)} %add_add_fusion), channel_id=1, source_target_pairs={{0,20},{4,16},{8,28},{12,24},{16,4},{20,0},{24,12},{28,8},{1,21},{... | collective-permute-start | bytes 98312 | tf_op jit(solution)/shard_map/ppermute | solution.py:267
  256.3 40.4 %collective-permute-start.39 = (f32[1,8192]{1,0:T(1,128)S(1)}, f32[1,8192]{1,0:T(1,128)S(1)}, u32[]{:S(2)}, u32[]{:S(2)}) collective-permute-start(f32[1,8192]{1,0:T(1,128)S(1)} %add_add_fusion), channel_id=1, source_target_pairs={{0,16},{4,20},{8,24},{12,28},{16,0},{20,4},{24,8},{28,12},{1,17},{... | collective-permute-start | bytes 98312 | tf_op jit(solution)/shard_map/ppermute | solution.py:267
  265.6 13.9 %copy-start.21 = (bf16[1024,256]{1,0:T(8,128)(2,1)}, bf16[1024,256]{1,0:T(8,128)(2,1)S(1)}, u32[]{:S(2)}) copy-start(bf16[1024,256]{1,0:T(8,128)(2,1)S(1)} %collective-permute-done.32.refs_3_) | copy-start | bytes 1572868
  265.6 31.1 %collective-permute-start.38 = (f32[1,8192]{1,0:T(1,128)S(1)}, f32[1,8192]{1,0:T(1,128)S(1)}, u32[]{:S(2)}, u32[]{:S(2)}) collective-permute-start(f32[1,8192]{1,0:T(1,128)S(1)} %add_add_fusion), channel_id=1, source_target_pairs={{0,12},{4,8},{8,4},{12,0},{16,28},{20,24},{24,20},{28,16},{1,13},{... | collective-permute-start | bytes 98312 | tf_op jit(solution)/shard_map/ppermute | solution.py:267
  278.0 18.7 %collective-permute-start.37 = (f32[1,8192]{1,0:T(1,128)S(1)}, f32[1,8192]{1,0:T(1,128)S(1)}, u32[]{:S(2)}, u32[]{:S(2)}) collective-permute-start(f32[1,8192]{1,0:T(1,128)S(1)} %add_add_fusion), channel_id=1, source_target_pairs={{0,8},{4,12},{8,0},{12,4},{16,24},{20,28},{24,16},{28,20},{1,9},{5... | collective-permute-start | bytes 98312 | tf_op jit(solution)/shard_map/ppermute | solution.py:267
  279.5 17.2 %collective-permute-start.36 = (f32[1,8192]{1,0:T(1,128)S(1)}, f32[1,8192]{1,0:T(1,128)S(1)}, u32[]{:S(2)}, u32[]{:S(2)}) collective-permute-start(f32[1,8192]{1,0:T(1,128)S(1)} %add_add_fusion), channel_id=1, source_target_pairs={{0,4},{4,0},{8,12},{12,8},{16,20},{20,16},{24,28},{28,24},{1,5},{5... | collective-permute-start | bytes 98312 | tf_op jit(solution)/shard_map/ppermute | solution.py:267
  292.3 31.0 %all-to-all-start.1 = ((bf16[8,128,1024]{2,1,0:T(8,128)(2,1)}), bf16[8,128,1024]{2,1,0:T(8,128)(2,1)}, u32[]{:S(2)}, u32[]{:S(2)}) async-start(bf16[8,128,1024]{2,1,0:T(8,128)(2,1)} %bitcast.32), calls=%async_computation.1 | async-start | bytes 4194304 | tf_op jit(solution)/shard_map/all_to_all | solution.py:323
  (3 other events, 8.5 us)

commit v2 on v1

v2 whole, which is shorter than its diff:
```python
import functools

import jax
import jax.numpy as jnp
from jax import lax
from jax.experimental import pallas as pl
from jax.experimental.pallas import tpu as pltpu
from jax.sharding import PartitionSpec as P

BLOCK = 256
CUTS = (2, 2, 2, 2)
F32 = jnp.float32
BF16 = jnp.bfloat16
VMEM = pl.BlockSpec(memory_space=pltpu.VMEM)
SMEM = pl.BlockSpec(memory_space=pltpu.SMEM)
CHEAP = pl.CostEstimate(flops=1000, bytes_accessed=1000, transcendentals=0)
PARAMS = pltpu.CompilerParams(vmem_limit_bytes=56 * 1024 * 1024)


def cuts(own):
    unit = own // sum(CUTS)
    sizes = [unit * c for c in CUTS]
    sizes = [x for x in sizes if x]
    return [(sum(sizes[:k]), size) for k, size in enumerate(sizes)]


def scaled(codes, scales):
    parts = [
        (codes[:, j * BLOCK : (j + 1) * BLOCK].astype(F32) * scales[:, j : j + 1]).astype(BF16)
        for j in range(codes.shape[1] // BLOCK)
    ]
    return jnp.concatenate(parts, axis=1)


def clipped(block):
    mean = jnp.sum(block * block, axis=-1, keepdims=True) * (1.0 / BLOCK) + 1e-06
    limit = 7.0 * (mean * lax.rsqrt(mean) * (1.0 / 3.5)).astype(BF16).astype(F32)
    return jnp.clip(block, -limit, limit)


def piece_kernel(which, codes, scales, cot, out):
    tokens = cot.shape[0]
    out[:tokens, :] = cot[...]
    out[tokens:, :] = scaled(codes[...], scales[...].T)


def weight_piece(which, codes, scales, cot, rows):
    tokens, kv = cot.shape
    return pl.pallas_call(
        piece_kernel,
        grid_spec=pltpu.PrefetchScalarGridSpec(
            num_scalar_prefetch=1,
            grid=(1,),
            in_specs=[
                pl.BlockSpec((rows, kv), lambda i, w: (w[0], 0)),
                pl.BlockSpec((scales.shape[0], rows), lambda i, w: (0, w[0])),
                pl.BlockSpec((tokens, kv), lambda i, w: (0, 0)),
            ],
            out_specs=pl.BlockSpec((tokens + rows, kv), lambda i, w: (0, 0)),
        ),
        out_shape=jax.ShapeDtypeStruct((tokens + rows, kv), BF16),
        compiler_params=PARAMS,
        cost_estimate=CHEAP,
        name="weight_piece",
    )(which, codes, scales, cot)


def norm_kernel(n, m, hidden, gain, after, *rest):
    outs, rstd, turned = rest[:-2], rest[-2], rest[-1]
    tokens, d = hidden.shape
    own = d // (n * m)
    wide = 512

    def square(i, total):
        h = hidden[:, pl.ds(pl.multiple_of(i * wide, wide), wide)].astype(F32)
        return total + jnp.sum(h * h, axis=-1, keepdims=True)

    total = lax.fori_loop(0, d // wide, square, jnp.zeros((tokens, 1), F32))
    inverse = lax.rsqrt(total * (1.0 / d) + 1e-05)
    rstd[...] = jnp.broadcast_to(inverse, rstd.shape)

    def turn(i, carry):
        at = pl.ds(pl.multiple_of(i * 256, 256), 256)
        x = hidden[:, at].astype(F32) * inverse * gain[:, at]
        turned[at, :] = x.astype(BF16).T
        return carry

    lax.fori_loop(0, d // 256, turn, 0)
    for k, (first, part) in enumerate(cuts(own)):
        for z in range(n):
            for a in range(m):
                start = (a * n + z) * own + first
                outs[k][z, a * part : (a + 1) * part, :] = turned[start : start + part, :]


def norm_rows(hidden, gain, after, n, m):
    tokens, d = hidden.shape
    parts = [jax.ShapeDtypeStruct((n, m * part, tokens), BF16) for _, part in cuts(d // (n * m))]
    got = pl.pallas_call(
        functools.partial(norm_kernel, n, m),
        in_specs=[VMEM, VMEM, pl.BlockSpec(memory_space=pl.ANY)],
        out_specs=[VMEM] * (len(parts) + 1),
        out_shape=parts + [jax.ShapeDtypeStruct((tokens, 128), F32)],
        scratch_shapes=[pltpu.VMEM((d, tokens), BF16)],
        compiler_params=PARAMS,
        cost_estimate=CHEAP,
        name="norm_rows",
    )(hidden, gain, after)
    return list(got[:-1]), got[-1]


def grad_kernel(n, m, count, me, rows, *refs):
    cots, outs = refs[:n], refs[n + count :]
    part = rows.shape[1] // m
    for which, out in enumerate(outs):
        owners = [lax.bitwise_xor(me[1], p) * 2 + me[2 + which] for p in range(m // 2)]
        lhs = []
        for s in range(n):
            source = lax.rem(me[0] + n - s, n)
            lhs.append(
                jnp.concatenate(
                    [rows[source, pl.ds(pl.multiple_of(o * part, part), part), :] for o in owners], axis=0
                )
            )
        for j in range(out.shape[1] // BLOCK):
            at = slice(j * BLOCK, (j + 1) * BLOCK)
            total = None
            for s in range(n):
                term = clipped(jnp.dot(lhs[s], cots[s][:, at], preferred_element_type=F32))
                total = term if total is None else total + term
            out[:, at] = clipped(total).astype(BF16)


def node_sum(z, chip, cores, rows, cots, m, after):
    n, count, tokens = rows.shape
    kv = cots[0].shape[1]
    return pl.pallas_call(
        functools.partial(grad_kernel, n, m, len(after)),
        grid=(1,),
        in_specs=[SMEM, VMEM]
        + [pl.BlockSpec((tokens, kv), lambda i: (0, 0))] * n
        + [pl.BlockSpec(memory_space=pl.ANY)] * len(after),
        out_specs=[VMEM] * len(cores),
        out_shape=[jax.ShapeDtypeStruct((count // 2, kv), BF16)] * len(cores),
        compiler_params=PARAMS,
        cost_estimate=CHEAP,
        name="node_sum",
    )(jnp.stack([z, chip, *cores]).astype(jnp.int32), rows, *cots, *after)


def project(starts, hidden, gain, rstd, cot, weights, values, gains, mean, keep):
    for which, (tile, count, load) in enumerate(weights):
        for j in range(count):
            w = load(j * tile, tile)
            at = pl.ds(pl.multiple_of(starts[which, j], 128), tile)
            g = gain[:, at]
            xhat = hidden[:, at].astype(F32) * rstd
            normed = (xhat * g).astype(BF16)
            values[...] += jnp.dot(normed, w, preferred_element_type=F32)
            grad = lax.dot_general(
                cot[...], w, (((1,), (1,)), ((), ())), preferred_element_type=F32
            ).astype(BF16)
            keep(which, j, tile, grad)
            product = grad.astype(F32) * xhat
            gains[:, at] = jnp.sum(product, axis=0, keepdims=True)
            mean[...] += jnp.sum(product * g, axis=-1, keepdims=True)


def own_kernel(starts, hidden, gain, rstd, cot, codes, scales, after, values, gains, mean, grads):
    values[...] = jnp.zeros_like(values)
    mean[...] = jnp.zeros_like(mean)
    gains[...] = jnp.zeros_like(gains)
    tile = 256
    count = codes.shape[0] // tile

    def load(first, size):
        return scaled(codes[first : first + size, :], scales[:, first : first + size].T)

    def keep(which, j, size, grad):
        grads[:, j * size : (j + 1) * size] = grad

    project(starts, hidden, gain, rstd[:, :1], cot, [(tile, count, load)], values, gains, mean, keep)


def part_shapes(tokens, kv, d, width):
    return [
        jax.ShapeDtypeStruct((tokens, kv), F32),
        jax.ShapeDtypeStruct((1, d), F32),
        jax.ShapeDtypeStruct((tokens, 128), F32),
        jax.ShapeDtypeStruct((tokens, width), BF16),
    ]


def own_part(starts, hidden, gain, rstd, cot, codes, scales, after):
    tokens, d = hidden.shape
    return pl.pallas_call(
        own_kernel,
        in_specs=[SMEM] + [VMEM] * 6 + [pl.BlockSpec(memory_space=pl.ANY)],
        out_specs=[VMEM] * 4,
        out_shape=part_shapes(tokens, cot.shape[1], d, codes.shape[0]),
        compiler_params=PARAMS,
        cost_estimate=CHEAP,
        name="own_part",
    )(starts, hidden, gain, rstd, cot, codes, scales, after)


def listed(weights, slot):
    return [
        (slot, w.shape[0] // slot, functools.partial(lambda w, first, size: w[first : first + size, :], w))
        for w in weights
    ]


def more_kernel(count, slot, starts, hidden, gain, rstd, cot, values_in, gains_in, mean_in, *refs):
    weights, (values, gains, mean, grads) = refs[:count], refs[count:]
    values[...] = values_in[...]
    gains[...] = gains_in[...]
    mean[...] = mean_in[...]
    width = weights[0].shape[0]

    def keep(which, j, size, grad):
        grads[:, which * width + j * size : which * width + (j + 1) * size] = grad

    project(starts, hidden, gain, rstd[:, :1], cot, listed(weights, slot), values, gains, mean, keep)


def more_part(starts, hidden, gain, rstd, cot, sums, weights, slot):
    tokens, d = hidden.shape
    count = len(weights)
    return pl.pallas_call(
        functools.partial(more_kernel, count, slot),
        in_specs=[SMEM] + [VMEM] * (7 + count),
        out_specs=[VMEM] * 4,
        out_shape=part_shapes(tokens, cot.shape[1], d, count * weights[0].shape[0]),
        compiler_params=PARAMS,
        cost_estimate=CHEAP,
        name="more_part",
    )(starts, hidden, gain, rstd, cot, *sums, *weights)


def last_kernel(count, kept, slot, *refs):
    starts, others, refs = refs[0], refs[1 : 1 + kept], refs[1 + kept :]
    hidden, gain, rstd, cot, values_in, gains_in, mean_in = refs[:7]
    olds, weights = refs[7 : 7 + kept], refs[7 + kept : 7 + kept + count]
    values, gains, result, total, mean, grads = refs[7 + kept + count :]
    total[...] = values_in[...]
    gains[...] = gains_in[...]
    mean[...] = mean_in[...]
    inverse = rstd[:, :1]
    width = weights[0].shape[0]

    def keep(which, j, size, grad):
        grads[:, which * width + j * size : which * width + (j + 1) * size] = grad

    project(starts, hidden, gain, inverse, cot, listed(weights, slot), total, gains, mean, keep)
    values[...] = total[...].astype(BF16)
    center = mean[:, :1] * (1.0 / hidden.shape[1])

    def finish(start, grad):
        at = pl.ds(pl.multiple_of(start, 128), grad.shape[1])
        xhat = hidden[:, at].astype(F32) * inverse
        t = gain[:, at] * grad.astype(F32)
        result[:, at] = (inverse * (t - xhat * center)).astype(BF16)

    for at, old in list(zip(others, olds)) + [(starts, grads)]:
        size = old.shape[1] // (at.shape[0] * at.shape[1])
        for i in range(at.shape[0]):
            for j in range(at.shape[1]):
                first = (i * at.shape[1] + j) * size
                finish(at[i, j], old[:, first : first + size])


def last_part(starts, others, hidden, gain, rstd, cot, sums, olds, weights, slot):
    tokens, d = hidden.shape
    kv = cot.shape[1]
    count, kept = len(weights), len(olds)
    return pl.pallas_call(
        functools.partial(last_kernel, count, kept, slot),
        in_specs=[SMEM] * (1 + kept) + [VMEM] * (7 + kept + count),
        out_specs=[VMEM] * 3,
        out_shape=[
            jax.ShapeDtypeStruct((tokens, kv), BF16),
            jax.ShapeDtypeStruct((1, d), F32),
            jax.ShapeDtypeStruct((tokens, d), BF16),
        ],
        scratch_shapes=[
            pltpu.VMEM((tokens, kv), F32),
            pltpu.VMEM((tokens, 128), F32),
            pltpu.VMEM((tokens, count * weights[0].shape[0]), BF16),
        ],
        compiler_params=PARAMS,
        cost_estimate=CHEAP,
        name="last_part",
    )(starts, *others, hidden, gain, rstd, cot, *sums, *olds, *weights)


def gate(arrays, after):
    count = len(arrays)
    anywhere = pl.BlockSpec(memory_space=pl.ANY)
    return pl.pallas_call(
        lambda *refs: None,
        in_specs=[anywhere] * (count + len(after)),
        out_specs=[anywhere] * count,
        out_shape=[jax.ShapeDtypeStruct(x.shape, x.dtype) for x in arrays],
        input_output_aliases={i: i for i in range(count)},
        name="gate",
    )(*arrays, *after)


def pair_sum(parts):
    while len(parts) > 1:
        parts = [parts[i] + parts[i + 1] for i in range(0, len(parts), 2)]
    return parts[0]


def exchange_sum(value, axis, size, first, last):
    for step in range(first, last):
        value = value + lax.ppermute(value, axis, [(i, i ^ (1 << step)) for i in range(size)])
    return value


def ring(value, n):
    def shift(x, by):
        return lax.ppermute(x, "node", [(i, (i + by) % n) for i in range(n)])

    slots, up, down = {}, value, value
    for s in range(1, n // 2 + 1):
        up = slots[s] = shift(up, 1)
        if n - s > s:
            down = slots[n - s] = shift(down, -1)
    return slots


def local(hidden, gain, codes, scales, cot):
    m, n = lax.axis_size("dp"), lax.axis_size("node")
    a, z = lax.axis_index("dp"), lax.axis_index("node")
    tokens, d = hidden.shape
    kv = cot.shape[1]
    own = d // (m * n)
    pieces = min(m, d // n // 128)
    size = d // n // pieces
    gain = gain.astype(F32).reshape(1, d)
    scales = scales.T
    here = lax.rem(a, pieces)
    chip, core = lax.div(a, 2), lax.rem(a, 2)

    def flip(value, bits):
        return lax.ppermute(value, "dp", [(i, i ^ bits[i % 2]) for i in range(m)])

    piece = weight_piece(here.reshape(1), codes, scales, cot, size)
    sends, rstd = norm_rows(hidden, gain, piece, n, m)
    own_start = (z * (d // n) + jnp.arange(d // n // 256, dtype=jnp.int32) * 256).reshape(1, -1)
    first = own_part(own_start, hidden, gain, rstd, cot, codes, scales, rstd)
    slots = ring(piece, n)
    cots = [cot] + [slots[s] for s in range(1, n)]

    def rows_to_owners(k, after):
        (rows,) = gate([sends[k]], after)
        return lax.all_to_all(rows, "node", split_axis=0, concat_axis=0, tiled=True)

    got = [rows_to_owners(0, [slots[1], slots[n - 1], first[2]])]

    mine = jnp.concatenate([slots[s][tokens:] for s in range(1, n)], axis=0)
    weights, bits, bit = [mine], [(0, 0)], 2
    if pieces >= 8:
        one, two = flip(mine, (2, 4)), flip(mine, (4, 2))
        weights += [one, two, flip(one, (4, 2))]
        bits += [(2, 4), (4, 2), (6, 6)]
        bit = 8
    while bit < pieces:
        weights += [flip(w, (bit, bit)) for w in weights]
        bits += [(e ^ bit, o ^ bit) for e, o in bits]
        bit *= 2
    if pieces > 1:
        weights = [x for w in weights for x in (w, flip(w, (1, 1)))]
        bits = [x for e, o in bits for x in ((e, o), (o ^ 1, e ^ 1))]
    at = [lax.bitwise_xor(here, jnp.where(core == 0, even, odd)) * size for even, odd in bits]
    slot_at = jnp.stack([lax.rem(z + n - s, n) * (d // n) for s in range(1, n)])
    starts = jnp.stack(at).astype(jnp.int32)[:, None] + slot_at.astype(jnp.int32)[None, :]

    got.append(rows_to_owners(1, [got[0], mine]))
    split = max(1, len(weights) - 2)
    more_start, last_start = starts[:split], starts[split:]
    chunks = cuts(own)
    theirs, ours, parts = [], [], []

    def node_sums(k, cores, after):
        return node_sum(z, chip, cores, got[k], cots, m, after)

    def to_owners(k):
        size = chunks[k][1]
        both = [
            ours[k][p * size : (p + 1) * size].astype(F32) + theirs[k][p * size : (p + 1) * size].astype(F32)
            for p in range(m // 2)
        ]
        return [both[0]] + [flip(both[p].astype(BF16), (2 * p, 2 * p)) for p in range(1, m // 2)]

    dp_steps = m.bit_length() - 1
    node_steps = n.bit_length() - 1
    after = [got[0]]
    for k in range(len(chunks)):
        if k < len(chunks) - 1:
            away, keep = node_sums(k, [1 - core, core], after)
            away = flip(away, (1, 1))
        else:
            (away,) = node_sums(k, [1 - core], after)
            away = flip(away, (1, 1))
            (keep,) = node_sums(k, [core], after)
        theirs.append(away)
        ours.append(keep)
        after = [keep]
        if k == 0:
            got.append(rows_to_owners(2, [got[1], keep]))
            weights[split - 1 : split] = gate(weights[split - 1 : split], [keep])
            more = more_part(more_start, hidden, gain, rstd, cot, first[:3], weights[:split], size)
            after = [more[2], away]
        if k == 1:
            got.append(rows_to_owners(3, [got[2], keep]))
            weights[split : split + 1] = gate(weights[split : split + 1], [keep, *parts[0][1:]])
            values, gains, input_gradient = last_part(
                last_start,
                [own_start, more_start],
                hidden,
                gain,
                rstd,
                cot,
                more[:3],
                [first[3], more[3]],
                weights[split:],
                size,
            )
            after = [gains, away]
        if k == 2:
            gains = exchange_sum(gains, "node", n, 0, node_steps)
            gains = exchange_sum(gains, "dp", m, 0, dp_steps)
            after += [*parts[1][1:]]
        parts.append(to_owners(k))
    scale = 1.0 / (m * n)
    gain_gradient_mean = gains.reshape(d) * scale
    done = [pair_sum([x.astype(F32) for x in part]) * scale for part in parts]
    weight_grad = jnp.concatenate(done, axis=0)
    return (values, input_gradient, weight_grad, gain_gradient_mean)


def solution(mesh):
    rows = P(("dp", "node"), None)
    return jax.shard_map(
        local,
        mesh=mesh,
        in_specs=(rows, P(), P("node", None), P("node", None), rows),
        out_specs=(rows, rows, rows, P()),
        check_vma=False,
    )
```

time: 327 us -> 244 us (0.75)
  waiting for transfers between devices: 164 us -> 82.4 us
  starting transfers between devices: 83.5 us -> 67.1 us
  Pallas kernels: 64.6 us -> 72.5 us
  other arithmetic: 7.78 us -> 11.4 us
  local copies, waits for them, and re-layouts: 5.69 us -> 8.97 us
    ppermute x43 -> x31, waiting for transfers between devices: 138 us -> 66.7 us  [the longest x23 32.1 us: flip(): return lax.ppermute(value, 'dp', [(i, i ^ bits[i % 2]) for i in range(m)])]
    ppermute x43 -> x31, starting transfers between devices: 75.4 us -> 30.1 us  [the longest x23 18.8 us: flip(): return lax.ppermute(value, 'dp', [(i, i ^ bits[i % 2]) for i in range(m)])]
    all_to_all x2 -> x4, starting transfers between devices: 8.1 us -> 36.9 us  [rows_to_owners(): return lax.all_to_all(rows, 'node', split_axis=0, concat_axis=0, tiled=True)]
    all_to_all x2 -> x4, waiting for transfers between devices: 25.5 us -> 15.7 us  [rows_to_owners(): return lax.all_to_all(rows, 'node', split_axis=0, concat_axis=0, tiled=True)]
    pallas_call x5 -> x15, Pallas kernels: 62.1 us -> 69.9 us  [the longest x5 27.9 us: node_sum(): pl.pallas_call(functools.partial(grad_kernel, n, m, len(after)), grid=(1,...]
    unnamed x45 -> x46, local copies, waits for them, and re-layouts: 2.18 us -> 6.48 us
  transfers between devices with their start and end apart: 45 -> 35, of which waited for: 13 -> 16; matrix products, arithmetic and copies ran while one was open for 3% -> 5% of each run, Pallas kernels for 19% -> 29%
where the time goes in v2:
time: 244 us; the launch traced here: 243 us
  waiting for transfers between devices  82.4 us (34%)
  Pallas kernels  72.5 us (30%)
  starting transfers between devices  67.1 us (27%)
  other arithmetic  11.4 us (5%)
  local copies, waits for them, and re-layouts  8.97 us (4%)
    all_to_all x4, starting transfers between devices, rows_to_owners(): return lax.all_to_all(rows, 'node', split_axis=0, concat_axis=0, tiled=True)  36.9 us
    ppermute x23, waiting for transfers between devices, flip(): return lax.ppermute(value, 'dp', [(i, i ^ bits[i % 2]) for i in range(m)])  32.1 us
    pallas_call x5, Pallas kernels, node_sum(): pl.pallas_call(functools.partial(grad_kernel, n, m, len(after)), grid=(1,...  27.9 us
    ppermute x3, waiting for transfers between devices, shift(): return lax.ppermute(x, 'node', [(i, (i + by) % n) for i in range(n)])  26.2 us
    ppermute x23, starting transfers between devices, flip(): return lax.ppermute(value, 'dp', [(i, i ^ bits[i % 2]) for i in range(m)])  18.8 us
    all_to_all x4, waiting for transfers between devices, rows_to_owners(): return lax.all_to_all(rows, 'node', split_axis=0, concat_axis=0, tiled=True)  15.7 us
    pallas_call x1, Pallas kernels, more_part(): pl.pallas_call(functools.partial(more_kernel, count, slot), in_specs=[SME...  12.5 us
    pallas_call x1, Pallas kernels, last_part(): pl.pallas_call(functools.partial(last_kernel, count, kept, slot), in_spec...  10.8 us
  transfers between devices with their start and end apart: 35, of which 16 were waited for; matrix products, arithmetic and copies ran while one was open for 5% of the time, Pallas kernels for 29%

profile of v2, /device:TPU:0, one launch (start us, length us, event | category | flops | bytes accessed | tf_op | source)
XLA Modules:
  0.0 243.2 jit_solution(2488983318799443508)
XLA Ops:
  0.6 2.6 %weight_piece.1.after = bf16[512,1024]{1,0:T(8,128)(2,1)} custom-call(s32[1]{0:T(128)} %bitcast.12.which, bf16[2048,1024]{1,0:T(8,128)(2,1)} %codes.3, f32[4,2048]{1,0:T(4,128)} %bitcast.24, bf16[256,1024]{1,0:T(8,128)(2,1)} %refs_0_.9), custom_call_target="tpu_custom_call" | custom-call | flops 1000 | bytes 1000 | tf_op jit(solution)/shard_map/weight_piece/pallas_call | solution.py:49
  3.2 3.0 %collective-permute-start = (bf16[512,1024]{1,0:T(8,128)(2,1)}, bf16[512,1024]{1,0:T(8,128)(2,1)}, u32[]{:S(2)}, u32[]{:S(2)}) collective-permute-start(bf16[512,1024]{1,0:T(8,128)(2,1)} %weight_piece.1.after), channel_id=1, source_target_pairs={{0,1},{1,2},{2,3},{3,0},{4,5},{5,6},{6,7},{7,4},{8,9},{9,10},{10,1... | collective-permute-start | bytes 3145736 | tf_op jit(solution)/shard_map/ppermute | solution.py:324
  6.2 2.0 collective-permute-start.2
  8.3 24.3 %collective-permute-done.refs_1_ = bf16[512,1024]{1,0:T(8,128)(2,1)} collective-permute-done((bf16[512,1024]{1,0:T(8,128)(2,1)}, bf16[512,1024]{1,0:T(8,128)(2,1)}, u32[]{:S(2)}, u32[]{:S(2)}) %collective-permute-start) | collective-permute-done | bytes 1048608 | tf_op jit(solution)/shard_map/ppermute | solution.py:324
  32.6 0.6 reshape.35
  33.2 9.3 %norm_rows.1 = (bf16[4,512,256]{2,1,0:T(8,128)(2,1)}, bf16[4,512,256]{2,1,0:T(8,128)(2,1)}, bf16[4,512,256]{2,1,0:T(8,128)(2,1)}, bf16[4,512,256]{2,1,0:T(8,128)(2,1)}, f32[256,128]{1,0:T(8,128)}) custom-call(bf16[256,8192]{1,0:T(8,128)(2,1)} %refs_3_.1, f32[1,8192]{1,0:T(1,128)} %bitcast.20, bf16[512,1024]{1,0:T(8,128)(2,1)} %weight_piece.1.after), custom_call_target="tpu_custom_call" | custom-call | flops 1000 | bytes 1000 | tf_op jit(solution)/shard_map/norm_rows/pallas_call | solution.py:99
  43.1 9.4 %own_part.1 = (f32[256,1024]{1,0:T(8,128)}, f32[1,8192]{1,0:T(1,128)}, f32[256,128]{1,0:T(8,128)}, bf16[256,2048]{1,0:T(8,128)(2,1)}) custom-call(s32[1,8]{1,0:T(1,128)} %multiply_add_fusion.starts.refs_1_, bf16[256,8192]{1,0:T(8,128)(2,1)} %refs_3_.1, f32[1,8192]{1,0:T(1,128)} %bitcast.21, f32[256,128]{1,0:T(8,128)} %get-tuple-element.26.rstd.after.refs_5_, ...), custom_call_target="tpu_custom_call" | custom-call | flops 1000 | bytes 1000 | tf_op jit(solution)/shard_map/own_part/pallas_call | solution.py:196
  52.5 1.3 collective-permute-done.2.refs_2_.refs_3_
  53.8 1.0 copy-done
  54.7 22.9 %all-to-all-start = ((bf16[4,512,256]{2,1,0:T(8,128)(2,1)}), bf16[4,512,256]{2,1,0:T(8,128)(2,1)S(1)}, u32[]{:S(2)}, u32[]{:S(2)}) async-start(bf16[4,512,256]{2,1,0:T(8,128)(2,1)} %gate.6), calls=%async_computation | async-start | bytes 2097152 | tf_op jit(solution)/shard_map/all_to_all | solution.py:359
  77.7 1.1 slice.148
  78.8 0.6 collective-permute-done.1.refs_2_
  79.5 1.4 pad_maximum_fusion.refs_0_.refs_2_
  81.0 1.5 collective-permute-start.4
  82.5 1.5 collective-permute-start.6
  84.0 15.1 %all-to-all-done.rows.refs_4_.refs_1_ = bf16[4,512,256]{2,1,0:T(8,128)(2,1)S(1)} async-done(((bf16[4,512,256]{2,1,0:T(8,128)(2,1)}), bf16[4,512,256]{2,1,0:T(8,128)(2,1)S(1)}, u32[]{:S(2)}, u32[]{:S(2)}) %all-to-all-start) | async-done | bytes 1048608 | tf_op jit(solution)/shard_map/all_to_all | solution.py:359
  99.1 1.0 copy-done.2
  100.1 3.5 %all-to-all-start.1 = ((bf16[4,512,256]{2,1,0:T(8,128)(2,1)}), bf16[4,512,256]{2,1,0:T(8,128)(2,1)S(1)}, u32[]{:S(2)}, u32[]{:S(2)}) async-start(bf16[4,512,256]{2,1,0:T(8,128)(2,1)} %gate.8), calls=%async_computation.1 | async-start | bytes 2097152 | tf_op jit(solution)/shard_map/all_to_all | solution.py:359
  103.6 15.0 %collective-permute-done.4.refs_2_ = bf16[768,1024]{1,0:T(8,128)(2,1)} collective-permute-done((bf16[768,1024]{1,0:T(8,128)(2,1)}, bf16[768,1024]{1,0:T(8,128)(2,1)}, u32[]{:S(2)}, u32[]{:S(2)}) %collective-permute-start.4) | collective-permute-done | bytes 1572896 | tf_op jit(solution)/shard_map/ppermute | solution.py:348
  119.7 6.2 %node_sum.5 = (bf16[256,1024]{1,0:T(8,128)(2,1)}, bf16[256,1024]{1,0:T(8,128)(2,1)}) custom-call(s32[4]{0:T(128)} %pad_add_fusion.1.me, bf16[4,512,256]{2,1,0:T(8,128)(2,1)} %copy-done.2, bf16[256,1024]{1,0:T(8,128)(2,1)} %refs_0_.9, bf16[512,1024]{1,0:T(8,128)(2,1)} %collective-permute-done.refs_1_, bf16[512,1024]{1,0:T(8,128)(2,1)} %copy-done.1, ...), custom_call_target="tpu_custom_call" | custom-call | flops 1000 | bytes 1000 | tf_op jit(solution)/shard_map/node_sum/pallas_call | solution.py:137
  125.9 0.6 all-to-all-done.1.rows.refs_1_
  126.6 1.0 copy-done.5
  127.6 4.9 %all-to-all-start.2 = ((bf16[4,512,256]{2,1,0:T(8,128)(2,1)}), bf16[4,512,256]{2,1,0:T(8,128)(2,1)S(1)}, u32[]{:S(2)}, u32[]{:S(2)}) async-start(bf16[4,512,256]{2,1,0:T(8,128)(2,1)} %gate.10), calls=%async_computation.2 | async-start | bytes 2097152 | tf_op jit(solution)/shard_map/all_to_all | solution.py:359
  132.5 6.9 %collective-permute-done.8.refs_0_ = bf16[768,1024]{1,0:T(8,128)(2,1)} collective-permute-done((bf16[768,1024]{1,0:T(8,128)(2,1)}, bf16[768,1024]{1,0:T(8,128)(2,1)}, u32[]{:S(2)}, u32[]{:S(2)}) %collective-permute-start.8) | collective-permute-done | bytes 1572896 | tf_op jit(solution)/shard_map/ppermute | solution.py:348
  140.0 0.7 broadcast_add_fusion
  140.7 12.5 %more_part.1 = (f32[256,1024]{1,0:T(8,128)}, f32[1,8192]{1,0:T(1,128)}, f32[256,128]{1,0:T(8,128)}, bf16[256,4608]{1,0:T(8,128)(2,1)}) custom-call(s32[6,3]{1,0:T(8,128)} %bitcast.26, bf16[256,8192]{1,0:T(8,128)(2,1)} %refs_3_.1, f32[1,8192]{1,0:T(1,128)} %bitcast.22, f32[256,128]{1,0:T(8,128)} %get-tuple-element.26.rstd.after.refs_5_, ...), custom_call_target="tpu_custom_call" | custom-call | flops 1000 | bytes 1000 | tf_op jit(solution)/shard_map/more_part/pallas_call | solution.py:230
  153.2 0.8 copy-done.9
  154.0 6.2 %node_sum.6 = (bf16[256,1024]{1,0:T(8,128)(2,1)}, bf16[256,1024]{1,0:T(8,128)(2,1)}) custom-call(s32[4]{0:T(128)} %pad_add_fusion.1.me, bf16[4,512,256]{2,1,0:T(8,128)(2,1)} %copy-done.5, bf16[256,1024]{1,0:T(8,128)(2,1)} %refs_0_.9, bf16[512,1024]{1,0:T(8,128)(2,1)} %collective-permute-done.refs_1_, bf16[512,1024]{1,0:T(8,128)(2,1)} %copy-done.1, ...), custom_call_target="tpu_custom_call" | custom-call | flops 1000 | bytes 1000 | tf_op jit(solution)/shard_map/node_sum/pallas_call | solution.py:137
  160.3 1.0 copy-done.4
  161.2 5.6 %all-to-all-start.3 = ((bf16[4,512,256]{2,1,0:T(8,128)(2,1)}), bf16[4,512,256]{2,1,0:T(8,128)(2,1)S(1)}, u32[]{:S(2)}, u32[]{:S(2)}) async-start(bf16[4,512,256]{2,1,0:T(8,128)(2,1)} %gate.11), calls=%async_computation.3 | async-start | bytes 2097152 | tf_op jit(solution)/shard_map/all_to_all | solution.py:359
  166.9 1.5 collective-permute-start.10
  168.5 2.0 collective-permute-start.12
  170.5 1.2 slice.111.refs_0_
  171.7 1.6 collective-permute-done.10.refs_2_
  173.3 3.6 %collective-permute-done.11.refs_3_ = bf16[64,1024]{1,0:T(8,128)(2,1)S(1)} collective-permute-done((bf16[64,1024]{1,0:T(8,128)(2,1)S(1)}, bf16[64,1024]{1,0:T(8,128)(2,1)S(1)}, u32[]{:S(2)}, u32[]{:S(2)}) %collective-permute-start.11) | collective-permute-done | bytes 131104 | tf_op jit(solution)/shard_map/ppermute | solution.py:348
  176.9 0.6 copy-done.17
  177.6 10.8 %last_part.1 = (bf16[256,1024]{1,0:T(8,128)(2,1)}, f32[1,8192]{1,0:T(1,128)}, bf16[256,8192]{1,0:T(8,128)(2,1)}) custom-call(s32[2,3]{1,0:T(2,128)} %slice.111.refs_0_, s32[1,8]{1,0:T(1,128)} %multiply_add_fusion.starts.refs_1_, s32[6,3]{1,0:T(8,128)} %bitcast.27, bf16[256,8192]{1,0:T(8,128)(2,1)} %refs_3_.1, f32[1,8192]{1,0:T(1,128)} %bitcast.23, ...), custom_call_target="tpu_custom_call" | custom-call | flops 1000 | bytes 1000 | tf_op jit(solution)/shard_map/last_part/pallas_call | solution.py:277
  188.4 2.1 collective-permute-start.26
  190.6 0.6 pad_add_fusion.2.me
  191.1 2.2 collective-permute-done.26
  193.4 0.8 add.170
  194.2 2.3 collective-permute-start.27
  196.4 0.6 pad_add_fusion.4.me
  197.0 2.0 collective-permute-done.27
  199.3 1.7 collective-permute-start.15
  201.0 1.8 collective-permute-start.17
  202.9 1.7 collective-permute-start.29
  204.7 4.1 %collective-permute-done.29 = f32[1,8192]{1,0:T(1,128)S(1)} collective-permute-done((f32[1,8192]{1,0:T(1,128)S(1)}, f32[1,8192]{1,0:T(1,128)S(1)}, u32[]{:S(2)}, u32[]{:S(2)}) %collective-permute-start.29) | collective-permute-done | bytes 32800 | tf_op jit(solution)/shard_map/ppermute | solution.py:318
  209.6 6.2 %node_sum.7 = (bf16[256,1024]{1,0:T(8,128)(2,1)}, bf16[256,1024]{1,0:T(8,128)(2,1)}) custom-call(s32[4]{0:T(128)} %pad_add_fusion.1.me, bf16[4,512,256]{2,1,0:T(8,128)(2,1)} %copy-done.4, bf16[256,1024]{1,0:T(8,128)(2,1)} %refs_0_.9, bf16[512,1024]{1,0:T(8,128)(2,1)} %collective-permute-done.refs_1_, bf16[512,1024]{1,0:T(8,128)(2,1)} %copy-done.1, ...), custom_call_target="tpu_custom_call" | custom-call | flops 1000 | bytes 1000 | tf_op jit(solution)/shard_map/node_sum/pallas_call | solution.py:137
  215.9 1.0 copy-done.3
  216.9 4.6 %node_sum.9 = bf16[256,1024]{1,0:T(8,128)(2,1)} custom-call(s32[3]{0:T(128)} %pad_add_fusion.4.me, bf16[4,512,256]{2,1,0:T(8,128)(2,1)} %copy-done.3, bf16[256,1024]{1,0:T(8,128)(2,1)} %refs_0_.9, bf16[512,1024]{1,0:T(8,128)(2,1)} %collective-permute-done.refs_1_, bf16[512,1024]{1,0:T(8,128)(2,1)} %copy-done.1, bf16[512,1024]{1,0:T(8,128)(2,1)} %copy-done, ...), custom_call_target="tpu_custom_call" | custom-call | flops 1000 | bytes 1000 | tf_op jit(solution)/shard_map/node_sum/pallas_call | solution.py:137
  222.0 0.7 add_multiply_fusion.4
  222.8 1.2 collective-permute-start.19
  224.0 2.0 collective-permute-start.20
  226.4 4.5 %node_sum.8 = bf16[256,1024]{1,0:T(8,128)(2,1)} custom-call(s32[3]{0:T(128)} %pad_add_fusion.2.me, bf16[4,512,256]{2,1,0:T(8,128)(2,1)} %copy-done.3, bf16[256,1024]{1,0:T(8,128)(2,1)} %refs_0_.9, bf16[512,1024]{1,0:T(8,128)(2,1)} %collective-permute-done.refs_1_, bf16[512,1024]{1,0:T(8,128)(2,1)} %copy-done.1, bf16[512,1024]{1,0:T(8,128)(2,1)} %copy-done, ...), custom_call_target="tpu_custom_call" | custom-call | flops 1000 | bytes 1000 | tf_op jit(solution)/shard_map/node_sum/pallas_call | solution.py:137
  230.9 1.2 add_convert_fusion.2
  232.1 1.2 collective-permute-start.23
  233.3 2.0 collective-permute-start.24
  235.7 1.0 add_multiply_fusion.1
  236.7 1.4 collective-permute-done.23
  238.0 1.9 collective-permute-done.24
  240.0 1.2 collective-permute-done.25
  241.2 1.0 add_multiply_fusion
  242.2 1.0 pad_maximum_fusion.1
  (96 shorter events, 5.1 us)
Async XLA Ops:
  0.6 32.0 %copy-start.21 = (bf16[8192]{0:T(1024)(128)(2,1)S(1)}, bf16[8192]{0:T(1024)(128)(2,1)}, u32[]{:S(2)}) copy-start(bf16[8192]{0:T(1024)(128)(2,1)} %param.6) | copy-start | bytes 49156
  3.2 29.4 %collective-permute-start = (bf16[512,1024]{1,0:T(8,128)(2,1)}, bf16[512,1024]{1,0:T(8,128)(2,1)}, u32[]{:S(2)}, u32[]{:S(2)}) collective-permute-start(bf16[512,1024]{1,0:T(8,128)(2,1)} %weight_piece.1.after), channel_id=1, source_target_pairs={{0,1},{1,2},{2,3},{3,0},{4,5},{5,6},{6,7},{7,4},{8,9},{9,10},{10,1... | collective-permute-start | bytes 3145736 | tf_op jit(solution)/shard_map/ppermute | solution.py:324
  6.2 47.5 %collective-permute-start.2 = (bf16[512,1024]{1,0:T(8,128)(2,1)}, bf16[512,1024]{1,0:T(8,128)(2,1)S(1)}, u32[]{:S(2)}, u32[]{:S(2)}) collective-permute-start(bf16[512,1024]{1,0:T(8,128)(2,1)} %weight_piece.1.after), channel_id=1, source_target_pairs={{0,3},{1,0},{2,1},{3,2},{4,7},{5,4},{6,5},{7,6},{8,11},{9,8},{10,9... | collective-permute-start | bytes 3145736 | tf_op jit(solution)/shard_map/ppermute | solution.py:324
  32.6 46.8 %collective-permute-start.1 = (bf16[512,1024]{1,0:T(8,128)(2,1)}, bf16[512,1024]{1,0:T(8,128)(2,1)S(1)}, u32[]{:S(2)}, u32[]{:S(2)}) collective-permute-start(bf16[512,1024]{1,0:T(8,128)(2,1)} %collective-permute-done.refs_1_), channel_id=1, source_target_pairs={{0,1},{1,2},{2,3},{3,0},{4,5},{5,6},{6,7},{7,4},{8,9},{9,10},{10,1... | collective-permute-start | bytes 3145736 | tf_op jit(solution)/shard_map/ppermute | solution.py:324
  53.8 1.0 copy-start
  54.7 44.4 %all-to-all-start = ((bf16[4,512,256]{2,1,0:T(8,128)(2,1)}), bf16[4,512,256]{2,1,0:T(8,128)(2,1)S(1)}, u32[]{:S(2)}, u32[]{:S(2)}) async-start(bf16[4,512,256]{2,1,0:T(8,128)(2,1)} %gate.6), calls=%async_computation | async-start | bytes 2097152 | tf_op jit(solution)/shard_map/all_to_all | solution.py:359
  77.7 1.8 slice-start
  79.4 1.6 copy-start.1
  81.0 37.6 %collective-permute-start.4 = (bf16[768,1024]{1,0:T(8,128)(2,1)}, bf16[768,1024]{1,0:T(8,128)(2,1)}, u32[]{:S(2)}, u32[]{:S(2)}) collective-permute-start(bf16[768,1024]{1,0:T(8,128)(2,1)} %pad_maximum_fusion.refs_0_.refs_2_), channel_id=1, source_target_pairs={{0,8},{4,20},{8,0},{12,28},{16,24},{20,4},{24,16},{28,12},{1,9},{5... | collective-permute-start | bytes 4718600 | tf_op jit(solution)/shard_map/ppermute | solution.py:348
  82.5 36.7 %collective-permute-start.6 = (bf16[768,1024]{1,0:T(8,128)(2,1)}, bf16[768,1024]{1,0:T(8,128)(2,1)}, u32[]{:S(2)}, u32[]{:S(2)}) collective-permute-start(bf16[768,1024]{1,0:T(8,128)(2,1)} %pad_maximum_fusion.refs_0_.refs_2_), channel_id=1, source_target_pairs={{0,16},{4,12},{8,24},{12,4},{16,0},{20,28},{24,8},{28,20},{1,17},{... | collective-permute-start | bytes 4718600 | tf_op jit(solution)/shard_map/ppermute | solution.py:348
  99.1 1.0 copy-start.2
  100.1 26.5 %all-to-all-start.1 = ((bf16[4,512,256]{2,1,0:T(8,128)(2,1)}), bf16[4,512,256]{2,1,0:T(8,128)(2,1)S(1)}, u32[]{:S(2)}, u32[]{:S(2)}) async-start(bf16[4,512,256]{2,1,0:T(8,128)(2,1)} %gate.8), calls=%async_computation.1 | async-start | bytes 2097152 | tf_op jit(solution)/shard_map/all_to_all | solution.py:359
  118.6 20.7 %collective-permute-start.8 = (bf16[768,1024]{1,0:T(8,128)(2,1)}, bf16[768,1024]{1,0:T(8,128)(2,1)}, u32[]{:S(2)}, u32[]{:S(2)}) collective-permute-start(bf16[768,1024]{1,0:T(8,128)(2,1)} %collective-permute-done.4.refs_2_), channel_id=1, source_target_pairs={{0,16},{4,12},{8,24},{12,4},{16,0},{20,28},{24,8},{28,20},{1,17},{... | collective-permute-start | bytes 4718600 | tf_op jit(solution)/shard_map/ppermute | solution.py:348
  118.6 22.1 %collective-permute-start.3 = (bf16[768,1024]{1,0:T(8,128)(2,1)}, bf16[768,1024]{1,0:T(8,128)(2,1)}, u32[]{:S(2)}, u32[]{:S(2)}) collective-permute-start(bf16[768,1024]{1,0:T(8,128)(2,1)} %pad_maximum_fusion.refs_0_.refs_2_), channel_id=1, source_target_pairs={{0,4},{4,0},{8,12},{12,8},{16,20},{20,16},{24,28},{28,24},{1,5},{5... | collective-permute-start | bytes 4718600 | tf_op jit(solution)/shard_map/ppermute | solution.py:348
  118.6 22.1 %collective-permute-start.5 = (bf16[768,1024]{1,0:T(8,128)(2,1)}, bf16[768,1024]{1,0:T(8,128)(2,1)}, u32[]{:S(2)}, u32[]{:S(2)}) collective-permute-start(bf16[768,1024]{1,0:T(8,128)(2,1)} %collective-permute-done.4.refs_2_), channel_id=1, source_target_pairs={{0,4},{4,0},{8,12},{12,8},{16,20},{20,16},{24,28},{28,24},{1,5},{5... | collective-permute-start | bytes 4718600 | tf_op jit(solution)/shard_map/ppermute | solution.py:348
  119.1 21.6 %collective-permute-start.7 = (bf16[768,1024]{1,0:T(8,128)(2,1)}, bf16[768,1024]{1,0:T(8,128)(2,1)}, u32[]{:S(2)}, u32[]{:S(2)}) collective-permute-start(bf16[768,1024]{1,0:T(8,128)(2,1)} %collective-permute-done.6.refs_4_), channel_id=1, source_target_pairs={{0,4},{4,0},{8,12},{12,8},{16,20},{20,16},{24,28},{28,24},{1,5},{5... | collective-permute-start | bytes 4718600 | tf_op jit(solution)/shard_map/ppermute | solution.py:348
  126.6 1.0 copy-start.5
  127.6 11.8 %copy-start.22 = (bf16[256,1024]{1,0:T(8,128)(2,1)S(1)}, bf16[256,1024]{1,0:T(8,128)(2,1)}, u32[]{:S(2)}) copy-start(bf16[256,1024]{1,0:T(8,128)(2,1)} %get-tuple-element.38) | copy-start | bytes 1572868
  127.6 32.7 %all-to-all-start.2 = ((bf16[4,512,256]{2,1,0:T(8,128)(2,1)}), bf16[4,512,256]{2,1,0:T(8,128)(2,1)S(1)}, u32[]{:S(2)}, u32[]{:S(2)}) async-start(bf16[4,512,256]{2,1,0:T(8,128)(2,1)} %gate.10), calls=%async_computation.2 | async-start | bytes 2097152 | tf_op jit(solution)/shard_map/all_to_all | solution.py:359
  139.3 37.6 %collective-permute-start.13 = (bf16[768,1024]{1,0:T(8,128)(2,1)}, bf16[768,1024]{1,0:T(8,128)(2,1)}, u32[]{:S(2)}, u32[]{:S(2)}) collective-permute-start(bf16[768,1024]{1,0:T(8,128)(2,1)} %collective-permute-done.8.refs_0_), channel_id=1, source_target_pairs={{0,4},{4,0},{8,12},{12,8},{16,20},{20,16},{24,28},{28,24},{1,5},{5... | collective-permute-start | bytes 4718600 | tf_op jit(solution)/shard_map/ppermute | solution.py:348
  139.4 13.9 %collective-permute-start.9 = (bf16[256,1024]{1,0:T(8,128)(2,1)S(1)}, bf16[256,1024]{1,0:T(8,128)(2,1)S(1)}, u32[]{:S(2)}, u32[]{:S(2)}) collective-permute-start(bf16[256,1024]{1,0:T(8,128)(2,1)S(1)} %copy-done.22), channel_id=1, source_target_pairs={{0,4},{4,0},{8,12},{12,8},{16,20},{20,16},{24,28},{28,24},{1,5},{5... | collective-permute-start | bytes 1572872 | tf_op jit(solution)/shard_map/ppermute | solution.py:348
  153.2 0.8 copy-start.9
  160.3 1.0 copy-start.4
  161.2 5.6 %copy-start.6 = (bf16[256,1024]{1,0:T(8,128)(2,1)S(1)}, bf16[256,1024]{1,0:T(8,128)(2,1)}, u32[]{:S(2)}) copy-start(bf16[256,1024]{1,0:T(8,128)(2,1)} %get-tuple-element.31.refs_1_.refs_2_) | copy-start | bytes 1572868
  161.2 5.6 %copy-start.10 = (bf16[256,1024]{1,0:T(8,128)(2,1)S(1)}, bf16[256,1024]{1,0:T(8,128)(2,1)}, u32[]{:S(2)}) copy-start(bf16[256,1024]{1,0:T(8,128)(2,1)} %copy-done.9) | copy-start | bytes 1572868
  161.2 54.7 %all-to-all-start.3 = ((bf16[4,512,256]{2,1,0:T(8,128)(2,1)}), bf16[4,512,256]{2,1,0:T(8,128)(2,1)S(1)}, u32[]{:S(2)}, u32[]{:S(2)}) async-start(bf16[4,512,256]{2,1,0:T(8,128)(2,1)} %gate.11), calls=%async_computation.3 | async-start | bytes 2097152 | tf_op jit(solution)/shard_map/all_to_all | solution.py:359
  166.8 32.4 %collective-permute-start.14 = (bf16[256,1024]{1,0:T(8,128)(2,1)}, bf16[256,1024]{1,0:T(8,128)(2,1)S(1)}, u32[]{:S(2)}, u32[]{:S(2)}) collective-permute-start(bf16[256,1024]{1,0:T(8,128)(2,1)} %get-tuple-element.42), channel_id=1, source_target_pairs={{0,4},{4,0},{8,12},{12,8},{16,20},{20,16},{24,28},{28,24},{1,5},{5... | collective-permute-start | bytes 1572872 | tf_op jit(solution)/shard_map/ppermute | solution.py:348
  166.9 6.4 %collective-permute-start.10 = (bf16[64,1024]{1,0:T(8,128)(2,1)S(1)}, bf16[64,1024]{1,0:T(8,128)(2,1)S(1)}, u32[]{:S(2)}, u32[]{:S(2)}) collective-permute-start(bf16[64,1024]{1,0:T(8,128)(2,1)S(1)} %get-tuple-element.59), channel_id=1, source_target_pairs={{0,8},{4,12},{8,0},{12,4},{16,24},{20,28},{24,16},{28,20},{1,9},{5... | collective-permute-start | bytes 393224 | tf_op jit(solution)/shard_map/ppermute | solution.py:348
  168.5 8.4 %collective-permute-start.11 = (bf16[64,1024]{1,0:T(8,128)(2,1)S(1)}, bf16[64,1024]{1,0:T(8,128)(2,1)S(1)}, u32[]{:S(2)}, u32[]{:S(2)}) collective-permute-start(bf16[64,1024]{1,0:T(8,128)(2,1)S(1)} %get-tuple-element.58), channel_id=1, source_target_pairs={{0,16},{4,20},{8,24},{12,28},{16,0},{20,4},{24,8},{28,12},{1,17},{... | collective-permute-start | bytes 393224 | tf_op jit(solution)/shard_map/ppermute | solution.py:348
  168.5 8.4 %collective-permute-start.12 = (bf16[64,1024]{1,0:T(8,128)(2,1)S(1)}, bf16[64,1024]{1,0:T(8,128)(2,1)S(1)}, u32[]{:S(2)}, u32[]{:S(2)}) collective-permute-start(bf16[64,1024]{1,0:T(8,128)(2,1)S(1)} %get-tuple-element.57), channel_id=1, source_target_pairs={{0,24},{4,28},{8,16},{12,20},{16,8},{20,12},{24,0},{28,4},{1,25},{... | collective-permute-start | bytes 393224 | tf_op jit(solution)/shard_map/ppermute | solution.py:348
  173.3 3.6 %copy-start.15 = (bf16[64,1024]{1,0:T(8,128)(2,1)}, bf16[64,1024]{1,0:T(8,128)(2,1)S(1)}, u32[]{:S(2)}) copy-start(bf16[64,1024]{1,0:T(8,128)(2,1)S(1)} %collective-permute-done.10.refs_2_) | copy-start | bytes 393220
  176.9 0.7 copy-start.17
  176.9 0.7 copy-start.19
  177.6 21.5 %copy-start.8 = (bf16[256,1024]{1,0:T(8,128)(2,1)S(1)}, bf16[256,1024]{1,0:T(8,128)(2,1)}, u32[]{:S(2)}) copy-start(bf16[256,1024]{1,0:T(8,128)(2,1)} %get-tuple-element.39.refs_1_.refs_2_) | copy-start | bytes 1572868
  188.4 16.2 %copy-start.16 = (bf16[64,1024]{1,0:T(8,128)(2,1)S(1)}, bf16[64,1024]{1,0:T(8,128)(2,1)}, u32[]{:S(2)}) copy-start(bf16[64,1024]{1,0:T(8,128)(2,1)} %copy-done.15) | copy-start | bytes 393220
  188.4 16.2 %copy-start.18 = (bf16[64,1024]{1,0:T(8,128)(2,1)S(1)}, bf16[64,1024]{1,0:T(8,128)(2,1)}, u32[]{:S(2)}) copy-start(bf16[64,1024]{1,0:T(8,128)(2,1)} %copy-done.17) | copy-start | bytes 393220
  188.4 16.2 %copy-start.20 = (bf16[64,1024]{1,0:T(8,128)(2,1)S(1)}, bf16[64,1024]{1,0:T(8,128)(2,1)}, u32[]{:S(2)}) copy-start(bf16[64,1024]{1,0:T(8,128)(2,1)} %copy-done.19) | copy-start | bytes 393220
  188.4 4.9 %collective-permute-start.26 = (f32[1,8192]{1,0:T(1,128)}, f32[1,8192]{1,0:T(1,128)S(1)}, u32[]{:S(2)}, u32[]{:S(2)}) collective-permute-start(f32[1,8192]{1,0:T(1,128)} %get-tuple-element.44.refs_4_), channel_id=1, source_target_pairs={{0,1},{1,0},{2,3},{3,2},{4,5},{5,4},{6,7},{7,6},{8,9},{9,8},{10,11... | collective-permute-start | bytes 98312 | tf_op jit(solution)/shard_map/ppermute | solution.py:318
  194.2 4.9 %collective-permute-start.27 = (f32[1,8192]{1,0:T(1,128)S(1)}, f32[1,8192]{1,0:T(1,128)S(1)}, u32[]{:S(2)}, u32[]{:S(2)}) collective-permute-start(f32[1,8192]{1,0:T(1,128)S(1)} %add.170), channel_id=1, source_target_pairs={{0,2},{1,3},{2,0},{3,1},{4,6},{5,7},{6,4},{7,5},{8,10},{9,11},{10,... | collective-permute-start | bytes 98312 | tf_op jit(solution)/shard_map/ppermute | solution.py:318
  199.1 3.8 %collective-permute-start.28 = (f32[1,8192]{1,0:T(1,128)S(1)}, f32[1,8192]{1,0:T(1,128)S(1)}, u32[]{:S(2)}, u32[]{:S(2)}) collective-permute-start(f32[1,8192]{1,0:T(1,128)S(1)} %add.171), channel_id=1, source_target_pairs={{0,4},{4,0},{8,12},{12,8},{16,20},{20,16},{24,28},{28,24},{1,5},{5... | collective-permute-start | bytes 98312 | tf_op jit(solution)/shard_map/ppermute | solution.py:318
  199.2 10.4 %copy-start.11 = (bf16[256,1024]{1,0:T(8,128)(2,1)}, bf16[256,1024]{1,0:T(8,128)(2,1)S(1)}, u32[]{:S(2)}) copy-start(bf16[256,1024]{1,0:T(8,128)(2,1)S(1)} %collective-permute-done.14.refs_5_) | copy-start | bytes 1572868
  199.3 9.6 %collective-permute-start.15 = (bf16[64,1024]{1,0:T(8,128)(2,1)S(1)}, bf16[64,1024]{1,0:T(8,128)(2,1)S(1)}, u32[]{:S(2)}, u32[]{:S(2)}) collective-permute-start(bf16[64,1024]{1,0:T(8,128)(2,1)S(1)} %get-tuple-element.56), channel_id=1, source_target_pairs={{0,8},{4,12},{8,0},{12,4},{16,24},{20,28},{24,16},{28,20},{1,9},{5... | collective-permute-start | bytes 393224 | tf_op jit(solution)/shard_map/ppermute | solution.py:348
  201.0 8.4 %collective-permute-start.16 = (bf16[64,1024]{1,0:T(8,128)(2,1)S(1)}, bf16[64,1024]{1,0:T(8,128)(2,1)S(1)}, u32[]{:S(2)}, u32[]{:S(2)}) collective-permute-start(bf16[64,1024]{1,0:T(8,128)(2,1)S(1)} %get-tuple-element.55), channel_id=1, source_target_pairs={{0,16},{4,20},{8,24},{12,28},{16,0},{20,4},{24,8},{28,12},{1,17},{... | collective-permute-start | bytes 393224 | tf_op jit(solution)/shard_map/ppermute | solution.py:348
  201.0 8.4 %collective-permute-start.17 = (bf16[64,1024]{1,0:T(8,128)(2,1)S(1)}, bf16[64,1024]{1,0:T(8,128)(2,1)S(1)}, u32[]{:S(2)}, u32[]{:S(2)}) collective-permute-start(bf16[64,1024]{1,0:T(8,128)(2,1)S(1)} %get-tuple-element.54), channel_id=1, source_target_pairs={{0,24},{4,28},{8,16},{12,20},{16,8},{20,12},{24,0},{28,4},{1,25},{... | collective-permute-start | bytes 393224 | tf_op jit(solution)/shard_map/ppermute | solution.py:348
  202.9 5.9 %collective-permute-start.29 = (f32[1,8192]{1,0:T(1,128)S(1)}, f32[1,8192]{1,0:T(1,128)S(1)}, u32[]{:S(2)}, u32[]{:S(2)}) collective-permute-start(f32[1,8192]{1,0:T(1,128)S(1)} %add.172), channel_id=1, source_target_pairs={{0,8},{4,12},{8,0},{12,4},{16,24},{20,28},{24,16},{28,20},{1,9},{5... | collective-permute-start | bytes 98312 | tf_op jit(solution)/shard_map/ppermute | solution.py:318
  208.9 13.2 %collective-permute-start.30 = (f32[1,8192]{1,0:T(1,128)S(1)}, f32[1,8192]{1,0:T(1,128)S(1)}, u32[]{:S(2)}, u32[]{:S(2)}) collective-permute-start(f32[1,8192]{1,0:T(1,128)S(1)} %add.173), channel_id=1, source_target_pairs={{0,16},{4,20},{8,24},{12,28},{16,0},{20,4},{24,8},{28,12},{1,17},{... | collective-permute-start | bytes 98312 | tf_op jit(solution)/shard_map/ppermute | solution.py:318
  209.0 6.8 %copy-start.12 = (bf16[64,1024]{1,0:T(8,128)(2,1)}, bf16[64,1024]{1,0:T(8,128)(2,1)S(1)}, u32[]{:S(2)}) copy-start(bf16[64,1024]{1,0:T(8,128)(2,1)S(1)} %collective-permute-done.15.refs_5_) | copy-start | bytes 393220
  209.4 6.4 %copy-start.13 = (bf16[64,1024]{1,0:T(8,128)(2,1)}, bf16[64,1024]{1,0:T(8,128)(2,1)S(1)}, u32[]{:S(2)}) copy-start(bf16[64,1024]{1,0:T(8,128)(2,1)S(1)} %collective-permute-done.16.refs_6_) | copy-start | bytes 393220
  209.5 6.4 %copy-start.14 = (bf16[64,1024]{1,0:T(8,128)(2,1)}, bf16[64,1024]{1,0:T(8,128)(2,1)S(1)}, u32[]{:S(2)}) copy-start(bf16[64,1024]{1,0:T(8,128)(2,1)S(1)} %collective-permute-done.17.refs_7_) | copy-start | bytes 393220
  215.8 6.9 %collective-permute-start.18 = (bf16[256,1024]{1,0:T(8,128)(2,1)}, bf16[256,1024]{1,0:T(8,128)(2,1)S(1)}, u32[]{:S(2)}, u32[]{:S(2)}) collective-permute-start(bf16[256,1024]{1,0:T(8,128)(2,1)} %get-tuple-element.46), channel_id=1, source_target_pairs={{0,4},{4,0},{8,12},{12,8},{16,20},{20,16},{24,28},{28,24},{1,5},{5... | collective-permute-start | bytes 1572872 | tf_op jit(solution)/shard_map/ppermute | solution.py:348
  215.9 1.0 copy-start.3
  216.9 5.8 %copy-start.7 = (bf16[256,1024]{1,0:T(8,128)(2,1)S(1)}, bf16[256,1024]{1,0:T(8,128)(2,1)}, u32[]{:S(2)}) copy-start(bf16[256,1024]{1,0:T(8,128)(2,1)} %get-tuple-element.45.refs_4_) | copy-start | bytes 1572868
  221.5 9.4 %collective-permute-start.22 = (bf16[256,1024]{1,0:T(8,128)(2,1)}, bf16[256,1024]{1,0:T(8,128)(2,1)S(1)}, u32[]{:S(2)}, u32[]{:S(2)}) collective-permute-start(bf16[256,1024]{1,0:T(8,128)(2,1)} %node_sum.9), channel_id=1, source_target_pairs={{0,4},{4,0},{8,12},{12,8},{16,20},{20,16},{24,28},{28,24},{1,5},{5... | collective-permute-start | bytes 1572872 | tf_op jit(solution)/shard_map/ppermute | solution.py:348
  222.8 12.5 %collective-permute-start.19 = (bf16[64,1024]{1,0:T(8,128)(2,1)S(1)}, bf16[64,1024]{1,0:T(8,128)(2,1)S(1)}, u32[]{:S(2)}, u32[]{:S(2)}) collective-permute-start(bf16[64,1024]{1,0:T(8,128)(2,1)S(1)} %get-tuple-element.48), channel_id=1, source_target_pairs={{0,8},{4,12},{8,0},{12,4},{16,24},{20,28},{24,16},{28,20},{1,9},{5... | collective-permute-start | bytes 393224 | tf_op jit(solution)/shard_map/ppermute | solution.py:348
  224.0 11.6 %collective-permute-start.20 = (bf16[64,1024]{1,0:T(8,128)(2,1)S(1)}, bf16[64,1024]{1,0:T(8,128)(2,1)S(1)}, u32[]{:S(2)}, u32[]{:S(2)}) collective-permute-start(bf16[64,1024]{1,0:T(8,128)(2,1)S(1)} %get-tuple-element.50), channel_id=1, source_target_pairs={{0,16},{4,20},{8,24},{12,28},{16,0},{20,4},{24,8},{28,12},{1,17},{... | collective-permute-start | bytes 393224 | tf_op jit(solution)/shard_map/ppermute | solution.py:348
  226.0 9.6 %collective-permute-start.21 = (bf16[64,1024]{1,0:T(8,128)(2,1)S(1)}, bf16[64,1024]{1,0:T(8,128)(2,1)S(1)}, u32[]{:S(2)}, u32[]{:S(2)}) collective-permute-start(bf16[64,1024]{1,0:T(8,128)(2,1)S(1)} %get-tuple-element.49), channel_id=1, source_target_pairs={{0,24},{4,28},{8,16},{12,20},{16,8},{20,12},{24,0},{28,4},{1,25},{... | collective-permute-start | bytes 393224 | tf_op jit(solution)/shard_map/ppermute | solution.py:348
  232.1 6.0 %collective-permute-start.23 = (bf16[64,1024]{1,0:T(8,128)(2,1)S(1)}, bf16[64,1024]{1,0:T(8,128)(2,1)S(1)}, u32[]{:S(2)}, u32[]{:S(2)}) collective-permute-start(bf16[64,1024]{1,0:T(8,128)(2,1)S(1)} %get-tuple-element.51), channel_id=1, source_target_pairs={{0,8},{4,12},{8,0},{12,4},{16,24},{20,28},{24,16},{28,20},{1,9},{5... | collective-permute-start | bytes 393224 | tf_op jit(solution)/shard_map/ppermute | solution.py:348
  233.3 6.7 %collective-permute-start.24 = (bf16[64,1024]{1,0:T(8,128)(2,1)S(1)}, bf16[64,1024]{1,0:T(8,128)(2,1)S(1)}, u32[]{:S(2)}, u32[]{:S(2)}) collective-permute-start(bf16[64,1024]{1,0:T(8,128)(2,1)S(1)} %get-tuple-element.53), channel_id=1, source_target_pairs={{0,16},{4,20},{8,24},{12,28},{16,0},{20,4},{24,8},{28,12},{1,17},{... | collective-permute-start | bytes 393224 | tf_op jit(solution)/shard_map/ppermute | solution.py:348
  235.3 5.9 %collective-permute-start.25 = (bf16[64,1024]{1,0:T(8,128)(2,1)S(1)}, bf16[64,1024]{1,0:T(8,128)(2,1)S(1)}, u32[]{:S(2)}, u32[]{:S(2)}) collective-permute-start(bf16[64,1024]{1,0:T(8,128)(2,1)S(1)} %get-tuple-element.52), channel_id=1, source_target_pairs={{0,24},{4,28},{8,16},{12,20},{16,8},{20,12},{24,0},{28,4},{1,25},{... | collective-permute-start | bytes 393224 | tf_op jit(solution)/shard_map/ppermute | solution.py:348

commit v3 on v2

--- a/solution.py
+++ b/solution.py
@@ -8,7 +8,6 @@
 from jax.sharding import PartitionSpec as P
 
 BLOCK = 256
-CUTS = (2, 2, 2, 2)
 F32 = jnp.float32
 BF16 = jnp.bfloat16
 VMEM = pl.BlockSpec(memory_space=pltpu.VMEM)
@@ -18,9 +17,9 @@
 
 
 def cuts(own):
-    unit = own // sum(CUTS)
-    sizes = [unit * c for c in CUTS]
-    sizes = [x for x in sizes if x]
+    units = own // 16
+    last = max(1, units // 8)
+    sizes = [16 * (units // 2), 16 * (units - units // 2 - last), 16 * last]
     return [(sum(sizes[:k]), size) for k, size in enumerate(sizes)]
 
 
@@ -38,10 +37,9 @@
     return jnp.clip(block, -limit, limit)
 
 
-def piece_kernel(which, codes, scales, cot, out):
-    tokens = cot.shape[0]
-    out[:tokens, :] = cot[...]
-    out[tokens:, :] = scaled(codes[...], scales[...].T)
+def piece_kernel(which, codes, scales, cot, out, copy):
+    out[...] = scaled(codes[...], scales[...].T)
+    copy[...] = cot[...]
 
 
 def weight_piece(which, codes, scales, cot, rows):
@@ -56,9 +54,12 @@
                 pl.BlockSpec((scales.shape[0], rows), lambda i, w: (0, w[0])),
                 pl.BlockSpec((tokens, kv), lambda i, w: (0, 0)),
             ],
-            out_specs=pl.BlockSpec((tokens + rows, kv), lambda i, w: (0, 0)),
+            out_specs=[
+                pl.BlockSpec((rows, kv), lambda i, w: (0, 0)),
+                pl.BlockSpec((tokens, kv), lambda i, w: (0, 0)),
+            ],
         ),
-        out_shape=jax.ShapeDtypeStruct((tokens + rows, kv), BF16),
+        out_shape=[jax.ShapeDtypeStruct((rows, kv), BF16), jax.ShapeDtypeStruct((tokens, kv), BF16)],
         compiler_params=PARAMS,
         cost_estimate=CHEAP,
         name="weight_piece",
@@ -136,9 +137,8 @@
     kv = cots[0].shape[1]
     return pl.pallas_call(
         functools.partial(grad_kernel, n, m, len(after)),
-        grid=(1,),
         in_specs=[SMEM, VMEM]
-        + [pl.BlockSpec((tokens, kv), lambda i: (0, 0))] * n
+        + [VMEM] * n
         + [pl.BlockSpec(memory_space=pl.ANY)] * len(after),
         out_specs=[VMEM] * len(cores),
         out_shape=[jax.ShapeDtypeStruct((count // 2, kv), BF16)] * len(cores),
@@ -319,13 +319,16 @@
     return value
 
 
-def ring(value, n):
+def ring(value, n, after):
     def shift(x, by):
         return lax.ppermute(x, "node", [(i, (i + by) % n) for i in range(n)])
 
     slots, up, down = {}, value, value
     for s in range(1, n // 2 + 1):
-        up = slots[s] = shift(up, 1)
+        up = shift(up, 1)
+        if s == 1 and after:
+            (up,) = gate([up], after)
+        slots[s] = up
         if n - s > s:
             down = slots[n - s] = shift(down, -1)
     return slots
@@ -347,20 +350,22 @@
     def flip(value, bits):
         return lax.ppermute(value, "dp", [(i, i ^ bits[i % 2]) for i in range(m)])
 
-    piece = weight_piece(here.reshape(1), codes, scales, cot, size)
+    piece, cot_copy = weight_piece(here.reshape(1), codes, scales, cot, size)
     sends, rstd = norm_rows(hidden, gain, piece, n, m)
     own_start = (z * (d // n) + jnp.arange(d // n // 256, dtype=jnp.int32) * 256).reshape(1, -1)
     first = own_part(own_start, hidden, gain, rstd, cot, codes, scales, rstd)
-    slots = ring(piece, n)
-    cots = [cot] + [slots[s] for s in range(1, n)]
+    slots = ring(piece, n, [rstd])
+    (cot_copy,) = gate([cot_copy], [slots[1], slots[n - 1], first[2]])
+    cot_slots = ring(cot_copy, n, [])
+    cots = [cot] + [cot_slots[s] for s in range(1, n)]
 
     def rows_to_owners(k, after):
         (rows,) = gate([sends[k]], after)
         return lax.all_to_all(rows, "node", split_axis=0, concat_axis=0, tiled=True)
 
-    got = [rows_to_owners(0, [slots[1], slots[n - 1], first[2]])]
-
-    mine = jnp.concatenate([slots[s][tokens:] for s in range(1, n)], axis=0)
+    (near,) = gate([slots[1]], [first[2]])
+    mine = jnp.concatenate([near] + [slots[s] for s in range(2, n)], axis=0)
+    got = [rows_to_owners(0, [mine, *cots])]
     weights, bits, bit = [mine], [(0, 0)], 2
     if pieces >= 8:
         one, two = flip(mine, (2, 4)), flip(mine, (4, 2))
@@ -378,7 +383,6 @@
     slot_at = jnp.stack([lax.rem(z + n - s, n) * (d // n) for s in range(1, n)])
     starts = jnp.stack(at).astype(jnp.int32)[:, None] + slot_at.astype(jnp.int32)[None, :]
 
-    got.append(rows_to_owners(1, [got[0], mine]))
     split = max(1, len(weights) - 2)
     more_start, last_start = starts[:split], starts[split:]
     chunks = cuts(own)
@@ -397,44 +401,38 @@
 
     dp_steps = m.bit_length() - 1
     node_steps = n.bit_length() - 1
-    after = [got[0]]
-    for k in range(len(chunks)):
-        if k < len(chunks) - 1:
-            away, keep = node_sums(k, [1 - core, core], after)
-            away = flip(away, (1, 1))
-        else:
-            (away,) = node_sums(k, [1 - core], after)
-            away = flip(away, (1, 1))
-            (keep,) = node_sums(k, [core], after)
-        theirs.append(away)
-        ours.append(keep)
-        after = [keep]
-        if k == 0:
-            got.append(rows_to_owners(2, [got[1], keep]))
-            weights[split - 1 : split] = gate(weights[split - 1 : split], [keep])
-            more = more_part(more_start, hidden, gain, rstd, cot, first[:3], weights[:split], size)
-            after = [more[2], away]
-        if k == 1:
-            got.append(rows_to_owners(3, [got[2], keep]))
-            weights[split : split + 1] = gate(weights[split : split + 1], [keep, *parts[0][1:]])
-            values, gains, input_gradient = last_part(
-                last_start,
-                [own_start, more_start],
-                hidden,
-                gain,
-                rstd,
-                cot,
-                more[:3],
-                [first[3], more[3]],
-                weights[split:],
-                size,
-            )
-            after = [gains, away]
-        if k == 2:
-            gains = exchange_sum(gains, "node", n, 0, node_steps)
-            gains = exchange_sum(gains, "dp", m, 0, dp_steps)
-            after += [*parts[1][1:]]
-        parts.append(to_owners(k))
+    more = more_part(more_start, hidden, gain, rstd, cot, first[:3], weights[:split], size)
+    weights[split : split + 1] = gate(weights[split : split + 1], [more[2]])
+    values, gains, input_gradient = last_part(
+        last_start,
+        [own_start, more_start],
+        hidden,
+        gain,
+        rstd,
+        cot,
+        more[:3],
+        [first[3], more[3]],
+        weights[split:],
+        size,
+    )
+    got.append(rows_to_owners(1, [got[0], gains]))
+    away, keep = node_sums(0, [1 - core, core], [gains])
+    theirs.append(flip(away, (1, 1)))
+    ours.append(keep)
+    parts.append(to_owners(0))
+    gains = exchange_sum(gains, "dp", m, 0, dp_steps)
+    got.append(rows_to_owners(2, [got[1], keep, gains, *parts[0][1:]]))
+    away, keep = node_sums(1, [1 - core, core], [keep])
+    (gains,) = gate([gains], [got[2]])
+    gains = exchange_sum(gains, "node", n, 0, node_steps)
+    theirs.append(flip(away, (1, 1)))
+    ours.append(keep)
+    parts.append(to_owners(1))
+    (away,) = node_sums(2, [1 - core], [keep])
+    theirs.append(flip(away, (1, 1)))
+    (keep,) = node_sums(2, [core], [away])
+    ours.append(keep)
+    parts.append(to_owners(2))
     scale = 1.0 / (m * n)
     gain_gradient_mean = gains.reshape(d) * scale
     done = [pair_sum([x.astype(F32) for x in part]) * scale for part in parts]

time: 244 us -> 217 us (0.89)
  starting transfers between devices: 67.1 us -> 44.2 us
  Pallas kernels: 72.5 us -> 69.7 us
  local copies, waits for them, and re-layouts: 8.97 us -> 6.45 us
    all_to_all x4 -> x3, starting transfers between devices: 36.9 us -> 11.3 us  [rows_to_owners(): return lax.all_to_all(rows, 'node', split_axis=0, concat_axis=0, tiled=True)]
    all_to_all x4 -> x3, waiting for transfers between devices: 15.7 us -> 10.4 us  [rows_to_owners(): return lax.all_to_all(rows, 'node', split_axis=0, concat_axis=0, tiled=True)]
    ppermute x3 -> x6, waiting for transfers between devices: 26.2 us -> 31.1 us  [shift(): return lax.ppermute(x, 'node', [(i, (i + by) % n) for i in range(n)])]
    ppermute x5, waiting for transfers between devices: 8.3 us -> 13.1 us  [exchange_sum(): lax.ppermute(value, axis, [(i, i ^ 1 << step) for i in range(size)])]
    ppermute x23 -> x19, waiting for transfers between devices: 32.1 us -> 28.1 us  [flip(): return lax.ppermute(value, 'dp', [(i, i ^ bits[i % 2]) for i in range(m)])]
    ppermute x3 -> x6, starting transfers between devices: 5.05 us -> 8.88 us  [shift(): return lax.ppermute(x, 'node', [(i, (i + by) % n) for i in range(n)])]
    pallas_call x5 -> x4, Pallas kernels: 27.9 us -> 25 us  [node_sum(): pl.pallas_call(functools.partial(grad_kernel, n, m, len(after)), in_specs...]
    ppermute x23 -> x19, starting transfers between devices: 18.8 us -> 19.8 us  [flip(): return lax.ppermute(value, 'dp', [(i, i ^ bits[i % 2]) for i in range(m)])]
  transfers between devices with their start and end apart: 35 -> 33, of which waited for: 16 -> 17; matrix products, arithmetic and copies ran while one was open for 5% -> 4% of each run, Pallas kernels for 29% -> 31%
where the time goes in v3:
time: 217 us
  waiting for transfers between devices  82.7 us (38%)
  Pallas kernels  69.7 us (32%)
  starting transfers between devices  44.2 us (20%)
  other arithmetic  12.9 us (6%)
  local copies, waits for them, and re-layouts  6.45 us (3%)
    ppermute x6, waiting for transfers between devices, shift(): return lax.ppermute(x, 'node', [(i, (i + by) % n) for i in range(n)])  31.1 us
    ppermute x19, waiting for transfers between devices, flip(): return lax.ppermute(value, 'dp', [(i, i ^ bits[i % 2]) for i in range(m)])  28.1 us
    pallas_call x4, Pallas kernels, node_sum(): pl.pallas_call(functools.partial(grad_kernel, n, m, len(after)), in_specs...  25 us
    ppermute x19, starting transfers between devices, flip(): return lax.ppermute(value, 'dp', [(i, i ^ bits[i % 2]) for i in range(m)])  19.8 us
    ppermute x5, waiting for transfers between devices, exchange_sum(): lax.ppermute(value, axis, [(i, i ^ 1 << step) for i in range(size)])  13.1 us
    pallas_call x1, Pallas kernels, more_part(): pl.pallas_call(functools.partial(more_kernel, count, slot), in_specs=[SME...  12.5 us
    all_to_all x3, starting transfers between devices, rows_to_owners(): return lax.all_to_all(rows, 'node', split_axis=0, concat_axis=0, tiled=True)  11.3 us
    pallas_call x1, Pallas kernels, last_part(): pl.pallas_call(functools.partial(last_kernel, count, kept, slot), in_spec...  10.8 us
  transfers between devices with their start and end apart: 33, of which 17 were waited for; matrix products, arithmetic and copies ran while one was open for 4% of the time, Pallas kernels for 31%

profile of v3, /device:TPU:0, one launch (start us, length us, event | category | flops | bytes accessed | tf_op | source)
XLA Modules:
  0.0 216.9 jit_solution(17223680103873075404)
XLA Ops:
  0.6 2.5 %weight_piece.1 = (bf16[256,1024]{1,0:T(8,128)(2,1)}, bf16[256,1024]{1,0:T(8,128)(2,1)}) custom-call(s32[1]{0:T(128)} %bitcast.12.which, bf16[2048,1024]{1,0:T(8,128)(2,1)} %codes.3, f32[4,2048]{1,0:T(4,128)} %bitcast.24, bf16[256,1024]{1,0:T(8,128)(2,1)} %refs_0_.7), custom_call_target="tpu_custom_call" | custom-call | flops 1000 | bytes 1000 | tf_op jit(solution)/shard_map/weight_piece/pallas_call | solution.py:47
  3.2 3.0 %collective-permute-start = (bf16[256,1024]{1,0:T(8,128)(2,1)}, bf16[256,1024]{1,0:T(8,128)(2,1)S(1)}, u32[]{:S(2)}, u32[]{:S(2)}) collective-permute-start(bf16[256,1024]{1,0:T(8,128)(2,1)} %get-tuple-element.25.after), channel_id=1, source_target_pairs={{0,1},{1,2},{2,3},{3,0},{4,5},{5,6},{6,7},{7,4},{8,9},{9,10},{10,1... | collective-permute-start | bytes 1572872 | tf_op jit(solution)/shard_map/ppermute | solution.py:324
  6.2 2.0 collective-permute-start.2
  8.2 0.6 reshape.35
  8.8 9.5 %norm_rows.1 = (bf16[4,1024,256]{2,1,0:T(8,128)(2,1)}, bf16[4,768,256]{2,1,0:T(8,128)(2,1)}, bf16[4,256,256]{2,1,0:T(8,128)(2,1)}, f32[256,128]{1,0:T(8,128)}) custom-call(bf16[256,8192]{1,0:T(8,128)(2,1)} %refs_3_.1, f32[1,8192]{1,0:T(1,128)} %bitcast.20, bf16[256,1024]{1,0:T(8,128)(2,1)} %get-tuple-element.25.after), custom_call_target="tpu_custom_call" | custom-call | flops 1000 | bytes 1000 | tf_op jit(solution)/shard_map/norm_rows/pallas_call | solution.py:100
  18.4 2.9 %collective-permute-done.refs_0_ = bf16[256,1024]{1,0:T(8,128)(2,1)S(1)} collective-permute-done((bf16[256,1024]{1,0:T(8,128)(2,1)}, bf16[256,1024]{1,0:T(8,128)(2,1)S(1)}, u32[]{:S(2)}, u32[]{:S(2)}) %collective-permute-start) | collective-permute-done | bytes 524320 | tf_op jit(solution)/shard_map/ppermute | solution.py:324
  21.2 0.8 copy-done.5
  22.0 0.6 multiply_add_fusion.starts.refs_1_
  22.6 9.4 %own_part.1 = (f32[256,1024]{1,0:T(8,128)}, f32[1,8192]{1,0:T(1,128)}, f32[256,128]{1,0:T(8,128)}, bf16[256,2048]{1,0:T(8,128)(2,1)}) custom-call(s32[1,8]{1,0:T(1,128)} %multiply_add_fusion.starts.refs_1_, bf16[256,8192]{1,0:T(8,128)(2,1)} %refs_3_.1, f32[1,8192]{1,0:T(1,128)} %bitcast.21, f32[256,128]{1,0:T(8,128)} %get-tuple-element.26.rstd.after.refs_1_.refs_5_, ...), custom_call_target="tpu_custom_call" | custom-call | flops 1000 | bytes 1000 | tf_op jit(solution)/shard_map/own_part/pallas_call | solution.py:196
  32.0 0.8 copy-done.8
  32.8 10.0 %collective-permute-done.1 = bf16[256,1024]{1,0:T(8,128)(2,1)S(1)} collective-permute-done((bf16[256,1024]{1,0:T(8,128)(2,1)}, bf16[256,1024]{1,0:T(8,128)(2,1)S(1)}, u32[]{:S(2)}, u32[]{:S(2)}) %collective-permute-start.1) | collective-permute-done | bytes 524320 | tf_op jit(solution)/shard_map/ppermute | solution.py:324
  42.9 2.5 %pad_maximum_fusion.refs_0_.refs_1_ = bf16[768,1024]{1,0:T(8,128)(2,1)} fusion(bf16[256,1024]{1,0:T(8,128)(2,1)} %copy-done.8, bf16[256,1024]{1,0:T(8,128)(2,1)S(1)} %collective-permute-done.1, bf16[256,1024]{1,0:T(8,128)(2,1)} %gate.9), kind=kLoop, calls=%fused_computation | loop fusion | flops 4718592 | bytes 3145728 | tf_op jit(solution)/shard_map/concatenate | solution.py:367
  45.4 1.5 collective-permute-start.4
  46.9 0.5 collective-permute-start.10
  47.4 3.3 %collective-permute-start.12 = (bf16[256,1024]{1,0:T(8,128)(2,1)S(1)}, bf16[256,1024]{1,0:T(8,128)(2,1)S(1)}, u32[]{:S(2)}, u32[]{:S(2)}) collective-permute-start(bf16[256,1024]{1,0:T(8,128)(2,1)S(1)} %copy-done.16), channel_id=1, source_target_pairs={{0,3},{1,0},{2,1},{3,2},{4,7},{5,4},{6,5},{7,6},{8,11},{9,8},{10,9... | collective-permute-start | bytes 1572872 | tf_op jit(solution)/shard_map/ppermute | solution.py:324
  50.7 12.8 %collective-permute-done.10.refs_3_.refs_1_ = bf16[256,1024]{1,0:T(8,128)(2,1)S(1)} collective-permute-done((bf16[256,1024]{1,0:T(8,128)(2,1)S(1)}, bf16[256,1024]{1,0:T(8,128)(2,1)S(1)}, u32[]{:S(2)}, u32[]{:S(2)}) %collective-permute-start.10) | collective-permute-done | bytes 524320 | tf_op jit(solution)/shard_map/ppermute | solution.py:324
  63.5 3.4 %collective-permute-start.6 = (bf16[768,1024]{1,0:T(8,128)(2,1)}, bf16[768,1024]{1,0:T(8,128)(2,1)}, u32[]{:S(2)}, u32[]{:S(2)}) collective-permute-start(bf16[768,1024]{1,0:T(8,128)(2,1)} %pad_maximum_fusion.refs_0_.refs_1_), channel_id=1, source_target_pairs={{0,16},{4,12},{8,24},{12,4},{16,0},{20,28},{24,8},{28,20},{1,17},{... | collective-permute-start | bytes 4718600 | tf_op jit(solution)/shard_map/ppermute | solution.py:351
  67.0 5.6 %collective-permute-done.4.refs_2_ = bf16[768,1024]{1,0:T(8,128)(2,1)} collective-permute-done((bf16[768,1024]{1,0:T(8,128)(2,1)}, bf16[768,1024]{1,0:T(8,128)(2,1)}, u32[]{:S(2)}, u32[]{:S(2)}) %collective-permute-start.4) | collective-permute-done | bytes 1572896 | tf_op jit(solution)/shard_map/ppermute | solution.py:351
  72.6 3.5 %collective-permute-start.8 = (bf16[768,1024]{1,0:T(8,128)(2,1)}, bf16[768,1024]{1,0:T(8,128)(2,1)}, u32[]{:S(2)}, u32[]{:S(2)}) collective-permute-start(bf16[768,1024]{1,0:T(8,128)(2,1)} %collective-permute-done.4.refs_2_), channel_id=1, source_target_pairs={{0,16},{4,12},{8,24},{12,4},{16,0},{20,28},{24,8},{28,20},{1,17},{... | collective-permute-start | bytes 4718600 | tf_op jit(solution)/shard_map/ppermute | solution.py:351
  76.2 5.4 %collective-permute-done.11.refs_4_.refs_2_ = bf16[256,1024]{1,0:T(8,128)(2,1)S(1)} collective-permute-done((bf16[256,1024]{1,0:T(8,128)(2,1)S(1)}, bf16[256,1024]{1,0:T(8,128)(2,1)S(1)}, u32[]{:S(2)}, u32[]{:S(2)}) %collective-permute-start.11) | collective-permute-done | bytes 524320 | tf_op jit(solution)/shard_map/ppermute | solution.py:324
  81.5 0.8 copy-done.4
  82.3 3.8 %all-to-all-start = ((bf16[4,1024,256]{2,1,0:T(8,128)(2,1)}), bf16[4,1024,256]{2,1,0:T(8,128)(2,1)S(1)}, u32[]{:S(2)}, u32[]{:S(2)}) async-start(bf16[4,1024,256]{2,1,0:T(8,128)(2,1)} %gate.12), calls=%async_computation | async-start | bytes 4194304 | tf_op jit(solution)/shard_map/all_to_all | solution.py:364
  86.8 15.8 %collective-permute-done.8.refs_0_ = bf16[768,1024]{1,0:T(8,128)(2,1)} collective-permute-done((bf16[768,1024]{1,0:T(8,128)(2,1)}, bf16[768,1024]{1,0:T(8,128)(2,1)}, u32[]{:S(2)}, u32[]{:S(2)}) %collective-permute-start.8) | collective-permute-done | bytes 1572896 | tf_op jit(solution)/shard_map/ppermute | solution.py:351
  102.8 0.6 slice.78.refs_0_
  103.4 12.5 %more_part.1 = (f32[256,1024]{1,0:T(8,128)}, f32[1,8192]{1,0:T(1,128)}, f32[256,128]{1,0:T(8,128)}, bf16[256,4608]{1,0:T(8,128)(2,1)}) custom-call(s32[6,3]{1,0:T(8,128)} %bitcast.26, bf16[256,8192]{1,0:T(8,128)(2,1)} %refs_3_.1, f32[1,8192]{1,0:T(1,128)} %bitcast.22, f32[256,128]{1,0:T(8,128)} %get-tuple-element.26.rstd.after.refs_1_.refs_5_, ...), custom_call_target="tpu_custom_call" | custom-call | flops 1000 | bytes 1000 | tf_op jit(solution)/shard_map/more_part/pallas_call | solution.py:230
  115.9 10.8 %last_part.1 = (bf16[256,1024]{1,0:T(8,128)(2,1)}, f32[1,8192]{1,0:T(1,128)}, bf16[256,8192]{1,0:T(8,128)(2,1)}) custom-call(s32[2,3]{1,0:T(2,128)} %slice.78.refs_0_, s32[1,8]{1,0:T(1,128)} %multiply_add_fusion.starts.refs_1_, s32[6,3]{1,0:T(8,128)} %bitcast.27, bf16[256,8192]{1,0:T(8,128)(2,1)} %refs_3_.1, f32[1,8192]{1,0:T(1,128)} %bitcast.23, ...), custom_call_target="tpu_custom_call" | custom-call | flops 1000 | bytes 1000 | tf_op jit(solution)/shard_map/last_part/pallas_call | solution.py:277
  126.7 4.1 %all-to-all-done.rows.refs_1_ = bf16[4,1024,256]{2,1,0:T(8,128)(2,1)S(1)} async-done(((bf16[4,1024,256]{2,1,0:T(8,128)(2,1)}), bf16[4,1024,256]{2,1,0:T(8,128)(2,1)S(1)}, u32[]{:S(2)}, u32[]{:S(2)}) %all-to-all-start) | async-done | bytes 2097184 | tf_op jit(solution)/shard_map/all_to_all | solution.py:364
  130.8 1.3 copy-done
  132.1 3.8 %all-to-all-start.1 = ((bf16[4,768,256]{2,1,0:T(8,128)(2,1)}), bf16[4,768,256]{2,1,0:T(8,128)(2,1)S(1)}, u32[]{:S(2)}, u32[]{:S(2)}) async-start(bf16[4,768,256]{2,1,0:T(8,128)(2,1)} %gate.13), calls=%async_computation.1 | async-start | bytes 3145728 | tf_op jit(solution)/shard_map/all_to_all | solution.py:364
  135.9 0.6 pad_add_fusion.1.me
  136.5 9.9 %node_sum.4 = (bf16[512,1024]{1,0:T(8,128)(2,1)}, bf16[512,1024]{1,0:T(8,128)(2,1)}) custom-call(s32[4]{0:T(128)} %pad_add_fusion.1.me, bf16[4,1024,256]{2,1,0:T(8,128)(2,1)} %copy-done, bf16[256,1024]{1,0:T(8,128)(2,1)} %refs_0_.7, bf16[256,1024]{1,0:T(8,128)(2,1)} %copy-done.2, bf16[256,1024]{1,0:T(8,128)(2,1)} %copy-done.4, bf16[256,1024]{1,0:T(8,128)(2,1)} %copy-done.3, ...), custom_call_target="tpu_custom_call" | custom-call | flops 1000 | bytes 1000 | tf_op jit(solution)/shard_map/node_sum/pallas_call | solution.py:138
  146.4 2.9 %collective-permute-done.13 = bf16[512,1024]{1,0:T(8,128)(2,1)S(1)} collective-permute-done((bf16[512,1024]{1,0:T(8,128)(2,1)}, bf16[512,1024]{1,0:T(8,128)(2,1)S(1)}, u32[]{:S(2)}, u32[]{:S(2)}) %collective-permute-start.13) | collective-permute-done | bytes 1048608 | tf_op jit(solution)/shard_map/ppermute | solution.py:351
  149.2 1.4 add_convert_fusion
  150.7 1.9 collective-permute-start.14
  152.7 1.5 collective-permute-start.16
  154.2 1.2 collective-permute-done.21
  155.5 1.9 collective-permute-start.22
  157.4 8.2 %collective-permute-done.22 = f32[1,8192]{1,0:T(1,128)S(1)} collective-permute-done((f32[1,8192]{1,0:T(1,128)S(1)}, f32[1,8192]{1,0:T(1,128)S(1)}, u32[]{:S(2)}, u32[]{:S(2)}) %collective-permute-start.22) | collective-permute-done | bytes 32800 | tf_op jit(solution)/shard_map/ppermute | solution.py:318
  165.8 3.8 %collective-permute-done.23 = f32[1,8192]{1,0:T(1,128)S(1)} collective-permute-done((f32[1,8192]{1,0:T(1,128)S(1)}, f32[1,8192]{1,0:T(1,128)S(1)}, u32[]{:S(2)}, u32[]{:S(2)}) %collective-permute-start.23) | collective-permute-done | bytes 32800 | tf_op jit(solution)/shard_map/ppermute | solution.py:318
  169.6 0.6 add.137.refs_3_.refs_0_
  170.2 2.0 all-to-all-done.1.rows.refs_1_
  172.3 1.2 copy-done.1
  173.4 3.7 %all-to-all-start.2 = ((bf16[4,256,256]{2,1,0:T(8,128)(2,1)}), bf16[4,256,256]{2,1,0:T(8,128)(2,1)S(1)}, u32[]{:S(2)}, u32[]{:S(2)}) async-start(bf16[4,256,256]{2,1,0:T(8,128)(2,1)} %gate.14), calls=%async_computation.2 | async-start | bytes 1048576 | tf_op jit(solution)/shard_map/all_to_all | solution.py:364
  177.2 8.1 %node_sum.5 = (bf16[384,1024]{1,0:T(8,128)(2,1)}, bf16[384,1024]{1,0:T(8,128)(2,1)}) custom-call(s32[4]{0:T(128)} %pad_add_fusion.1.me, bf16[4,768,256]{2,1,0:T(8,128)(2,1)} %copy-done.1, bf16[256,1024]{1,0:T(8,128)(2,1)} %refs_0_.7, bf16[256,1024]{1,0:T(8,128)(2,1)} %copy-done.2, bf16[256,1024]{1,0:T(8,128)(2,1)} %copy-done.4, bf16[256,1024]{1,0:T(8,128)(2,1)} %copy-done.3, ...), custom_call_target="tpu_custom_call" | custom-call | flops 1000 | bytes 1000 | tf_op jit(solution)/shard_map/node_sum/pallas_call | solution.py:138
  185.3 0.6 pad_add_fusion.4.me
  185.9 0.6 pad_add_fusion.2.me
  186.5 4.4 %all-to-all-done.2.rows.refs_1_ = bf16[4,256,256]{2,1,0:T(8,128)(2,1)S(1)} async-done(((bf16[4,256,256]{2,1,0:T(8,128)(2,1)}), bf16[4,256,256]{2,1,0:T(8,128)(2,1)S(1)}, u32[]{:S(2)}, u32[]{:S(2)}) %all-to-all-start.2) | async-done | bytes 524320 | tf_op jit(solution)/shard_map/all_to_all | solution.py:364
  190.9 0.8 copy-done.6
  191.7 1.2 add_multiply_fusion
  192.9 3.5 %node_sum.6.refs_4_ = bf16[128,1024]{1,0:T(8,128)(2,1)} custom-call(s32[3]{0:T(128)} %pad_add_fusion.4.me, bf16[4,256,256]{2,1,0:T(8,128)(2,1)} %copy-done.6, bf16[256,1024]{1,0:T(8,128)(2,1)} %refs_0_.7, bf16[256,1024]{1,0:T(8,128)(2,1)} %copy-done.2, bf16[256,1024]{1,0:T(8,128)(2,1)} %copy-done.4, bf16[256,1024]{1,0:T(8,128)(2,1)} %copy-done.3, ...), custom_call_target="tpu_custom_call" | custom-call | flops 1000 | bytes 1000 | tf_op jit(solution)/shard_map/node_sum/pallas_call | solution.py:138
  196.5 2.1 collective-permute-start.29
  198.8 1.5 collective-permute-start.20
  200.3 1.7 collective-permute-start.19
  202.3 3.5 %node_sum.7 = bf16[128,1024]{1,0:T(8,128)(2,1)} custom-call(s32[3]{0:T(128)} %pad_add_fusion.2.me, bf16[4,256,256]{2,1,0:T(8,128)(2,1)} %copy-done.6, bf16[256,1024]{1,0:T(8,128)(2,1)} %refs_0_.7, bf16[256,1024]{1,0:T(8,128)(2,1)} %copy-done.2, bf16[256,1024]{1,0:T(8,128)(2,1)} %copy-done.4, bf16[256,1024]{1,0:T(8,128)(2,1)} %copy-done.3, ...), custom_call_target="tpu_custom_call" | custom-call | flops 1000 | bytes 1000 | tf_op jit(solution)/shard_map/node_sum/pallas_call | solution.py:138
  205.8 0.7 add_multiply_fusion.3
  206.5 1.0 add_convert_fusion.8
  207.4 1.5 collective-permute-start.27
  209.0 1.7 collective-permute-start.26
  211.0 0.7 collective-permute-done.19
  211.8 1.4 collective-permute-done.27
  213.2 0.6 collective-permute-done.26
  213.8 1.1 collective-permute-done.25
  214.9 0.9 add_multiply_fusion.2
  215.8 1.1 pad_maximum_fusion.1
  (81 shorter events, 2.5 us)
Async XLA Ops:
  0.6 7.6 %copy-start.19 = (bf16[8192]{0:T(1024)(128)(2,1)S(1)}, bf16[8192]{0:T(1024)(128)(2,1)}, u32[]{:S(2)}) copy-start(bf16[8192]{0:T(1024)(128)(2,1)} %param.6) | copy-start | bytes 49156
  3.2 18.1 %collective-permute-start = (bf16[256,1024]{1,0:T(8,128)(2,1)}, bf16[256,1024]{1,0:T(8,128)(2,1)S(1)}, u32[]{:S(2)}, u32[]{:S(2)}) collective-permute-start(bf16[256,1024]{1,0:T(8,128)(2,1)} %get-tuple-element.25.after), channel_id=1, source_target_pairs={{0,1},{1,2},{2,3},{3,0},{4,5},{5,6},{6,7},{7,4},{8,9},{9,10},{10,1... | collective-permute-start | bytes 1572872 | tf_op jit(solution)/shard_map/ppermute | solution.py:324
  6.2 25.9 %collective-permute-start.2 = (bf16[256,1024]{1,0:T(8,128)(2,1)}, bf16[256,1024]{1,0:T(8,128)(2,1)S(1)}, u32[]{:S(2)}, u32[]{:S(2)}) collective-permute-start(bf16[256,1024]{1,0:T(8,128)(2,1)} %get-tuple-element.25.after), channel_id=1, source_target_pairs={{0,3},{1,0},{2,1},{3,2},{4,7},{5,4},{6,5},{7,6},{8,11},{9,8},{10,9... | collective-permute-start | bytes 1572872 | tf_op jit(solution)/shard_map/ppermute | solution.py:324
  21.2 0.8 copy-start.5
  22.0 20.8 %collective-permute-start.1 = (bf16[256,1024]{1,0:T(8,128)(2,1)}, bf16[256,1024]{1,0:T(8,128)(2,1)S(1)}, u32[]{:S(2)}, u32[]{:S(2)}) collective-permute-start(bf16[256,1024]{1,0:T(8,128)(2,1)} %gate.8.refs_0_.refs_1_), channel_id=1, source_target_pairs={{0,1},{1,2},{2,3},{3,0},{4,5},{5,6},{6,7},{7,4},{8,9},{9,10},{10,1... | collective-permute-start | bytes 1572872 | tf_op jit(solution)/shard_map/ppermute | solution.py:324
  32.0 0.8 copy-start.8
  42.9 4.0 %copy-start.16 = (bf16[256,1024]{1,0:T(8,128)(2,1)S(1)}, bf16[256,1024]{1,0:T(8,128)(2,1)}, u32[]{:S(2)}) copy-start(bf16[256,1024]{1,0:T(8,128)(2,1)} %gate.11) | copy-start | bytes 1572868
  45.4 27.2 %collective-permute-start.4 = (bf16[768,1024]{1,0:T(8,128)(2,1)}, bf16[768,1024]{1,0:T(8,128)(2,1)}, u32[]{:S(2)}, u32[]{:S(2)}) collective-permute-start(bf16[768,1024]{1,0:T(8,128)(2,1)} %pad_maximum_fusion.refs_0_.refs_1_), channel_id=1, source_target_pairs={{0,8},{4,20},{8,0},{12,28},{16,24},{20,4},{24,16},{28,12},{1,9},{5... | collective-permute-start | bytes 4718600 | tf_op jit(solution)/shard_map/ppermute | solution.py:351
  46.9 16.7 %collective-permute-start.10 = (bf16[256,1024]{1,0:T(8,128)(2,1)S(1)}, bf16[256,1024]{1,0:T(8,128)(2,1)S(1)}, u32[]{:S(2)}, u32[]{:S(2)}) collective-permute-start(bf16[256,1024]{1,0:T(8,128)(2,1)S(1)} %copy-done.16), channel_id=1, source_target_pairs={{0,1},{1,2},{2,3},{3,0},{4,5},{5,6},{6,7},{7,4},{8,9},{9,10},{10,1... | collective-permute-start | bytes 1572872 | tf_op jit(solution)/shard_map/ppermute | solution.py:324
  47.4 28.7 %collective-permute-start.12 = (bf16[256,1024]{1,0:T(8,128)(2,1)S(1)}, bf16[256,1024]{1,0:T(8,128)(2,1)S(1)}, u32[]{:S(2)}, u32[]{:S(2)}) collective-permute-start(bf16[256,1024]{1,0:T(8,128)(2,1)S(1)} %copy-done.16), channel_id=1, source_target_pairs={{0,3},{1,0},{2,1},{3,2},{4,7},{5,4},{6,5},{7,6},{8,11},{9,8},{10,9... | collective-permute-start | bytes 1572872 | tf_op jit(solution)/shard_map/ppermute | solution.py:324
  63.5 18.0 %copy-start.2 = (bf16[256,1024]{1,0:T(8,128)(2,1)}, bf16[256,1024]{1,0:T(8,128)(2,1)S(1)}, u32[]{:S(2)}) copy-start(bf16[256,1024]{1,0:T(8,128)(2,1)S(1)} %collective-permute-done.10.refs_3_.refs_1_) | copy-start | bytes 1572868
  63.5 18.0 %collective-permute-start.11 = (bf16[256,1024]{1,0:T(8,128)(2,1)S(1)}, bf16[256,1024]{1,0:T(8,128)(2,1)S(1)}, u32[]{:S(2)}, u32[]{:S(2)}) collective-permute-start(bf16[256,1024]{1,0:T(8,128)(2,1)S(1)} %collective-permute-done.10.refs_3_.refs_1_), channel_id=1, source_target_pairs={{0,1},{1,2},{2,3},{3,0},{4,5},{5,6},{6,7},{7,4},{8,9},{9,10},{10,1... | collective-permute-start | bytes 1572872 | tf_op jit(solution)/shard_map/ppermute | solution.py:324
  63.5 23.2 %collective-permute-start.6 = (bf16[768,1024]{1,0:T(8,128)(2,1)}, bf16[768,1024]{1,0:T(8,128)(2,1)}, u32[]{:S(2)}, u32[]{:S(2)}) collective-permute-start(bf16[768,1024]{1,0:T(8,128)(2,1)} %pad_maximum_fusion.refs_0_.refs_1_), channel_id=1, source_target_pairs={{0,16},{4,12},{8,24},{12,4},{16,0},{20,28},{24,8},{28,20},{1,17},{... | collective-permute-start | bytes 4718600 | tf_op jit(solution)/shard_map/ppermute | solution.py:351
  72.6 29.9 %collective-permute-start.8 = (bf16[768,1024]{1,0:T(8,128)(2,1)}, bf16[768,1024]{1,0:T(8,128)(2,1)}, u32[]{:S(2)}, u32[]{:S(2)}) collective-permute-start(bf16[768,1024]{1,0:T(8,128)(2,1)} %collective-permute-done.4.refs_2_), channel_id=1, source_target_pairs={{0,16},{4,12},{8,24},{12,4},{16,0},{20,28},{24,8},{28,20},{1,17},{... | collective-permute-start | bytes 4718600 | tf_op jit(solution)/shard_map/ppermute | solution.py:351
  76.1 5.4 %copy-start.3 = (bf16[256,1024]{1,0:T(8,128)(2,1)}, bf16[256,1024]{1,0:T(8,128)(2,1)S(1)}, u32[]{:S(2)}) copy-start(bf16[256,1024]{1,0:T(8,128)(2,1)S(1)} %collective-permute-done.12.refs_5_.refs_3_) | copy-start | bytes 1572868
  81.5 0.8 copy-start.4
  82.3 48.5 %all-to-all-start = ((bf16[4,1024,256]{2,1,0:T(8,128)(2,1)}), bf16[4,1024,256]{2,1,0:T(8,128)(2,1)S(1)}, u32[]{:S(2)}, u32[]{:S(2)}) async-start(bf16[4,1024,256]{2,1,0:T(8,128)(2,1)} %gate.12), calls=%async_computation | async-start | bytes 4194304 | tf_op jit(solution)/shard_map/all_to_all | solution.py:364
  86.1 17.2 %collective-permute-start.3 = (bf16[768,1024]{1,0:T(8,128)(2,1)}, bf16[768,1024]{1,0:T(8,128)(2,1)}, u32[]{:S(2)}, u32[]{:S(2)}) collective-permute-start(bf16[768,1024]{1,0:T(8,128)(2,1)} %pad_maximum_fusion.refs_0_.refs_1_), channel_id=1, source_target_pairs={{0,4},{4,0},{8,12},{12,8},{16,20},{20,16},{24,28},{28,24},{1,5},{5... | collective-permute-start | bytes 4718600 | tf_op jit(solution)/shard_map/ppermute | solution.py:351
  86.2 17.2 %collective-permute-start.5 = (bf16[768,1024]{1,0:T(8,128)(2,1)}, bf16[768,1024]{1,0:T(8,128)(2,1)}, u32[]{:S(2)}, u32[]{:S(2)}) collective-permute-start(bf16[768,1024]{1,0:T(8,128)(2,1)} %collective-permute-done.4.refs_2_), channel_id=1, source_target_pairs={{0,4},{4,0},{8,12},{12,8},{16,20},{20,16},{24,28},{28,24},{1,5},{5... | collective-permute-start | bytes 4718600 | tf_op jit(solution)/shard_map/ppermute | solution.py:351
  86.7 16.7 %collective-permute-start.7 = (bf16[768,1024]{1,0:T(8,128)(2,1)}, bf16[768,1024]{1,0:T(8,128)(2,1)}, u32[]{:S(2)}, u32[]{:S(2)}) collective-permute-start(bf16[768,1024]{1,0:T(8,128)(2,1)} %collective-permute-done.6.refs_4_), channel_id=1, source_target_pairs={{0,4},{4,0},{8,12},{12,8},{16,20},{20,16},{24,28},{28,24},{1,5},{5... | collective-permute-start | bytes 4718600 | tf_op jit(solution)/shard_map/ppermute | solution.py:351
  102.5 13.4 %collective-permute-start.9 = (bf16[768,1024]{1,0:T(8,128)(2,1)}, bf16[768,1024]{1,0:T(8,128)(2,1)}, u32[]{:S(2)}, u32[]{:S(2)}) collective-permute-start(bf16[768,1024]{1,0:T(8,128)(2,1)} %collective-permute-done.8.refs_0_), channel_id=1, source_target_pairs={{0,4},{4,0},{8,12},{12,8},{16,20},{20,16},{24,28},{28,24},{1,5},{5... | collective-permute-start | bytes 4718600 | tf_op jit(solution)/shard_map/ppermute | solution.py:351
  102.8 0.6 copy-start.18
  130.8 1.3 copy-start
  132.1 40.1 %all-to-all-start.1 = ((bf16[4,768,256]{2,1,0:T(8,128)(2,1)}), bf16[4,768,256]{2,1,0:T(8,128)(2,1)S(1)}, u32[]{:S(2)}, u32[]{:S(2)}) async-start(bf16[4,768,256]{2,1,0:T(8,128)(2,1)} %gate.13), calls=%async_computation.1 | async-start | bytes 3145728 | tf_op jit(solution)/shard_map/all_to_all | solution.py:364
  146.4 7.8 %copy-start.17 = (f32[1,8192]{1,0:T(1,128)S(1)}, f32[1,8192]{1,0:T(1,128)}, u32[]{:S(2)}) copy-start(f32[1,8192]{1,0:T(1,128)} %get-tuple-element.39.refs_4_.refs_2_) | copy-start | bytes 98308
  146.4 2.9 %collective-permute-start.13 = (bf16[512,1024]{1,0:T(8,128)(2,1)}, bf16[512,1024]{1,0:T(8,128)(2,1)S(1)}, u32[]{:S(2)}, u32[]{:S(2)}) collective-permute-start(bf16[512,1024]{1,0:T(8,128)(2,1)} %get-tuple-element.41), channel_id=1, source_target_pairs={{0,4},{4,0},{8,12},{12,8},{16,20},{20,16},{24,28},{28,24},{1,5},{5... | collective-permute-start | bytes 3145736 | tf_op jit(solution)/shard_map/ppermute | solution.py:351
  150.7 19.6 %collective-permute-start.14 = (bf16[128,1024]{1,0:T(8,128)(2,1)S(1)}, bf16[128,1024]{1,0:T(8,128)(2,1)S(1)}, u32[]{:S(2)}, u32[]{:S(2)}) collective-permute-start(bf16[128,1024]{1,0:T(8,128)(2,1)S(1)} %get-tuple-element.48), channel_id=1, source_target_pairs={{0,8},{4,12},{8,0},{12,4},{16,24},{20,28},{24,16},{28,20},{1,9},{5... | collective-permute-start | bytes 786440 | tf_op jit(solution)/shard_map/ppermute | solution.py:351
  152.6 17.6 %collective-permute-start.15 = (bf16[128,1024]{1,0:T(8,128)(2,1)S(1)}, bf16[128,1024]{1,0:T(8,128)(2,1)S(1)}, u32[]{:S(2)}, u32[]{:S(2)}) collective-permute-start(bf16[128,1024]{1,0:T(8,128)(2,1)S(1)} %get-tuple-element.47), channel_id=1, source_target_pairs={{0,16},{4,20},{8,24},{12,28},{16,0},{20,4},{24,8},{28,12},{1,17},{... | collective-permute-start | bytes 786440 | tf_op jit(solution)/shard_map/ppermute | solution.py:351
  152.7 17.5 %collective-permute-start.16 = (bf16[128,1024]{1,0:T(8,128)(2,1)S(1)}, bf16[128,1024]{1,0:T(8,128)(2,1)S(1)}, u32[]{:S(2)}, u32[]{:S(2)}) collective-permute-start(bf16[128,1024]{1,0:T(8,128)(2,1)S(1)} %get-tuple-element.46), channel_id=1, source_target_pairs={{0,24},{4,28},{8,16},{12,20},{16,8},{20,12},{24,0},{28,4},{1,25},{... | collective-permute-start | bytes 786440 | tf_op jit(solution)/shard_map/ppermute | solution.py:351
  154.2 1.2 collective-permute-start.21
  155.5 10.1 %collective-permute-start.22 = (f32[1,8192]{1,0:T(1,128)S(1)}, f32[1,8192]{1,0:T(1,128)S(1)}, u32[]{:S(2)}, u32[]{:S(2)}) collective-permute-start(f32[1,8192]{1,0:T(1,128)S(1)} %add.135), channel_id=1, source_target_pairs={{0,8},{4,12},{8,0},{12,4},{16,24},{20,28},{24,16},{28,20},{1,9},{5... | collective-permute-start | bytes 98312 | tf_op jit(solution)/shard_map/ppermute | solution.py:318
  165.6 4.0 %collective-permute-start.23 = (f32[1,8192]{1,0:T(1,128)S(1)}, f32[1,8192]{1,0:T(1,128)S(1)}, u32[]{:S(2)}, u32[]{:S(2)}) collective-permute-start(f32[1,8192]{1,0:T(1,128)S(1)} %add.136), channel_id=1, source_target_pairs={{0,16},{4,20},{8,24},{12,28},{16,0},{20,4},{24,8},{28,12},{1,17},{... | collective-permute-start | bytes 98312 | tf_op jit(solution)/shard_map/ppermute | solution.py:318
  170.2 2.0 copy-start.9
  170.2 2.0 copy-start.11
  170.2 2.0 copy-start.13
  172.2 1.2 copy-start.1
  173.4 17.4 %all-to-all-start.2 = ((bf16[4,256,256]{2,1,0:T(8,128)(2,1)}), bf16[4,256,256]{2,1,0:T(8,128)(2,1)S(1)}, u32[]{:S(2)}, u32[]{:S(2)}) async-start(bf16[4,256,256]{2,1,0:T(8,128)(2,1)} %gate.14), calls=%async_computation.2 | async-start | bytes 1048576 | tf_op jit(solution)/shard_map/all_to_all | solution.py:364
  177.2 14.5 %copy-start.10 = (bf16[128,1024]{1,0:T(8,128)(2,1)S(1)}, bf16[128,1024]{1,0:T(8,128)(2,1)}, u32[]{:S(2)}) copy-start(bf16[128,1024]{1,0:T(8,128)(2,1)} %copy-done.9) | copy-start | bytes 786436
  177.2 14.5 %copy-start.12 = (bf16[128,1024]{1,0:T(8,128)(2,1)S(1)}, bf16[128,1024]{1,0:T(8,128)(2,1)}, u32[]{:S(2)}) copy-start(bf16[128,1024]{1,0:T(8,128)(2,1)} %copy-done.11) | copy-start | bytes 786436
  177.2 14.5 %copy-start.14 = (bf16[128,1024]{1,0:T(8,128)(2,1)S(1)}, bf16[128,1024]{1,0:T(8,128)(2,1)}, u32[]{:S(2)}) copy-start(bf16[128,1024]{1,0:T(8,128)(2,1)} %copy-done.13) | copy-start | bytes 786436
  185.3 13.3 %collective-permute-start.17 = (bf16[384,1024]{1,0:T(8,128)(2,1)}, bf16[384,1024]{1,0:T(8,128)(2,1)S(1)}, u32[]{:S(2)}, u32[]{:S(2)}) collective-permute-start(bf16[384,1024]{1,0:T(8,128)(2,1)} %get-tuple-element.44), channel_id=1, source_target_pairs={{0,4},{4,0},{8,12},{12,8},{16,20},{20,16},{24,28},{28,24},{1,5},{5... | collective-permute-start | bytes 2359304 | tf_op jit(solution)/shard_map/ppermute | solution.py:351
  190.9 0.8 copy-start.6
  191.7 4.8 %collective-permute-start.28 = (f32[1,8192]{1,0:T(1,128)}, f32[1,8192]{1,0:T(1,128)S(1)}, u32[]{:S(2)}, u32[]{:S(2)}) collective-permute-start(f32[1,8192]{1,0:T(1,128)} %gate.15), channel_id=1, source_target_pairs={{0,1},{1,0},{2,3},{3,2},{4,5},{5,4},{6,7},{7,6},{8,9},{9,8},{10,11... | collective-permute-start | bytes 98312 | tf_op jit(solution)/shard_map/ppermute | solution.py:318
  192.9 3.6 %copy-start.15 = (f32[1,8192]{1,0:T(1,128)S(1)}, f32[1,8192]{1,0:T(1,128)}, u32[]{:S(2)}) copy-start(f32[1,8192]{1,0:T(1,128)} %gate.15) | copy-start | bytes 98308
  192.9 5.7 %copy-start.7 = (bf16[384,1024]{1,0:T(8,128)(2,1)S(1)}, bf16[384,1024]{1,0:T(8,128)(2,1)}, u32[]{:S(2)}) copy-start(bf16[384,1024]{1,0:T(8,128)(2,1)} %get-tuple-element.43.refs_4_) | copy-start | bytes 2359300
  196.4 10.1 %collective-permute-start.24 = (bf16[128,1024]{1,0:T(8,128)(2,1)}, bf16[128,1024]{1,0:T(8,128)(2,1)S(1)}, u32[]{:S(2)}, u32[]{:S(2)}) collective-permute-start(bf16[128,1024]{1,0:T(8,128)(2,1)} %node_sum.6.refs_4_), channel_id=1, source_target_pairs={{0,4},{4,0},{8,12},{12,8},{16,20},{20,16},{24,28},{28,24},{1,5},{5... | collective-permute-start | bytes 786440 | tf_op jit(solution)/shard_map/ppermute | solution.py:351
  196.5 9.3 %collective-permute-start.29 = (f32[1,8192]{1,0:T(1,128)S(1)}, f32[1,8192]{1,0:T(1,128)S(1)}, u32[]{:S(2)}, u32[]{:S(2)}) collective-permute-start(f32[1,8192]{1,0:T(1,128)S(1)} %add.145), channel_id=1, source_target_pairs={{0,2},{1,3},{2,0},{3,1},{4,6},{5,7},{6,4},{7,5},{8,10},{9,11},{10,... | collective-permute-start | bytes 98312 | tf_op jit(solution)/shard_map/ppermute | solution.py:318
  198.8 11.9 %collective-permute-start.20 = (bf16[96,1024]{1,0:T(8,128)(2,1)S(1)}, bf16[96,1024]{1,0:T(8,128)(2,1)S(1)}, u32[]{:S(2)}, u32[]{:S(2)}) collective-permute-start(bf16[96,1024]{1,0:T(8,128)(2,1)S(1)} %get-tuple-element.50), channel_id=1, source_target_pairs={{0,24},{4,28},{8,16},{12,20},{16,8},{20,12},{24,0},{28,4},{1,25},{... | collective-permute-start | bytes 589832 | tf_op jit(solution)/shard_map/ppermute | solution.py:351
  200.3 11.4 %collective-permute-start.19 = (bf16[96,1024]{1,0:T(8,128)(2,1)S(1)}, bf16[96,1024]{1,0:T(8,128)(2,1)S(1)}, u32[]{:S(2)}, u32[]{:S(2)}) collective-permute-start(bf16[96,1024]{1,0:T(8,128)(2,1)S(1)} %get-tuple-element.51), channel_id=1, source_target_pairs={{0,16},{4,20},{8,24},{12,28},{16,0},{20,4},{24,8},{28,12},{1,17},{... | collective-permute-start | bytes 589832 | tf_op jit(solution)/shard_map/ppermute | solution.py:351
  202.0 9.7 %collective-permute-start.18 = (bf16[96,1024]{1,0:T(8,128)(2,1)S(1)}, bf16[96,1024]{1,0:T(8,128)(2,1)S(1)}, u32[]{:S(2)}, u32[]{:S(2)}) collective-permute-start(bf16[96,1024]{1,0:T(8,128)(2,1)S(1)} %get-tuple-element.49), channel_id=1, source_target_pairs={{0,8},{4,12},{8,0},{12,4},{16,24},{20,28},{24,16},{28,20},{1,9},{5... | collective-permute-start | bytes 589832 | tf_op jit(solution)/shard_map/ppermute | solution.py:351
  207.4 5.8 %collective-permute-start.27 = (bf16[32,1024]{1,0:T(8,128)(2,1)S(1)}, bf16[32,1024]{1,0:T(8,128)(2,1)S(1)}, u32[]{:S(2)}, u32[]{:S(2)}) collective-permute-start(bf16[32,1024]{1,0:T(8,128)(2,1)S(1)} %get-tuple-element.53), channel_id=1, source_target_pairs={{0,24},{4,28},{8,16},{12,20},{16,8},{20,12},{24,0},{28,4},{1,25},{... | collective-permute-start | bytes 196616 | tf_op jit(solution)/shard_map/ppermute | solution.py:351
  209.0 4.8 %collective-permute-start.26 = (bf16[32,1024]{1,0:T(8,128)(2,1)S(1)}, bf16[32,1024]{1,0:T(8,128)(2,1)S(1)}, u32[]{:S(2)}, u32[]{:S(2)}) collective-permute-start(bf16[32,1024]{1,0:T(8,128)(2,1)S(1)} %get-tuple-element.54), channel_id=1, source_target_pairs={{0,16},{4,20},{8,24},{12,28},{16,0},{20,4},{24,8},{28,12},{1,17},{... | collective-permute-start | bytes 196616 | tf_op jit(solution)/shard_map/ppermute | solution.py:351
  210.7 4.3 %collective-permute-start.25 = (bf16[32,1024]{1,0:T(8,128)(2,1)S(1)}, bf16[32,1024]{1,0:T(8,128)(2,1)S(1)}, u32[]{:S(2)}, u32[]{:S(2)}) collective-permute-start(bf16[32,1024]{1,0:T(8,128)(2,1)S(1)} %get-tuple-element.52), channel_id=1, source_target_pairs={{0,8},{4,12},{8,0},{12,4},{16,24},{20,28},{24,16},{28,20},{1,9},{5... | collective-permute-start | bytes 196616 | tf_op jit(solution)/shard_map/ppermute | solution.py:351

commit v4 on v3

--- a/solution.py
+++ b/solution.py
@@ -37,13 +37,12 @@
     return jnp.clip(block, -limit, limit)
 
 
-def piece_kernel(which, codes, scales, cot, out, copy):
+def piece_kernel(which, codes, scales, out):
     out[...] = scaled(codes[...], scales[...].T)
-    copy[...] = cot[...]
-
-
-def weight_piece(which, codes, scales, cot, rows):
-    tokens, kv = cot.shape
+
+
+def weight_piece(which, codes, scales, rows):
+    kv = codes.shape[1]
     return pl.pallas_call(
         piece_kernel,
         grid_spec=pltpu.PrefetchScalarGridSpec(
@@ -52,22 +51,19 @@
             in_specs=[
                 pl.BlockSpec((rows, kv), lambda i, w: (w[0], 0)),
                 pl.BlockSpec((scales.shape[0], rows), lambda i, w: (0, w[0])),
-                pl.BlockSpec((tokens, kv), lambda i, w: (0, 0)),
             ],
-            out_specs=[
-                pl.BlockSpec((rows, kv), lambda i, w: (0, 0)),
-                pl.BlockSpec((tokens, kv), lambda i, w: (0, 0)),
-            ],
+            out_specs=pl.BlockSpec((rows, kv), lambda i, w: (0, 0)),
         ),
-        out_shape=[jax.ShapeDtypeStruct((rows, kv), BF16), jax.ShapeDtypeStruct((tokens, kv), BF16)],
+        out_shape=jax.ShapeDtypeStruct((rows, kv), BF16),
         compiler_params=PARAMS,
         cost_estimate=CHEAP,
         name="weight_piece",
-    )(which, codes, scales, cot)
-
-
-def norm_kernel(n, m, hidden, gain, after, *rest):
-    outs, rstd, turned = rest[:-2], rest[-2], rest[-1]
+    )(which, codes, scales)
+
+
+def norm_kernel(n, m, hidden, gain, cot, after, *rest):
+    outs, rstd, copy, turned = rest[:-3], rest[-3], rest[-2], rest[-1]
+    copy[...] = cot[...]
     tokens, d = hidden.shape
     own = d // (n * m)
     wide = 512
@@ -94,20 +90,20 @@
                 outs[k][z, a * part : (a + 1) * part, :] = turned[start : start + part, :]
 
 
-def norm_rows(hidden, gain, after, n, m):
+def norm_rows(hidden, gain, cot, after, n, m):
     tokens, d = hidden.shape
     parts = [jax.ShapeDtypeStruct((n, m * part, tokens), BF16) for _, part in cuts(d // (n * m))]
     got = pl.pallas_call(
         functools.partial(norm_kernel, n, m),
-        in_specs=[VMEM, VMEM, pl.BlockSpec(memory_space=pl.ANY)],
-        out_specs=[VMEM] * (len(parts) + 1),
-        out_shape=parts + [jax.ShapeDtypeStruct((tokens, 128), F32)],
+        in_specs=[VMEM, VMEM, VMEM, pl.BlockSpec(memory_space=pl.ANY)],
+        out_specs=[VMEM] * (len(parts) + 2),
+        out_shape=parts + [jax.ShapeDtypeStruct((tokens, 128), F32), jax.ShapeDtypeStruct(cot.shape, BF16)],
         scratch_shapes=[pltpu.VMEM((d, tokens), BF16)],
         compiler_params=PARAMS,
         cost_estimate=CHEAP,
         name="norm_rows",
-    )(hidden, gain, after)
-    return list(got[:-1]), got[-1]
+    )(hidden, gain, cot, after)
+    return list(got[:-2]), got[-2], got[-1]
 
 
 def grad_kernel(n, m, count, me, rows, *refs):
@@ -350,8 +346,8 @@
     def flip(value, bits):
         return lax.ppermute(value, "dp", [(i, i ^ bits[i % 2]) for i in range(m)])
 
-    piece, cot_copy = weight_piece(here.reshape(1), codes, scales, cot, size)
-    sends, rstd = norm_rows(hidden, gain, piece, n, m)
+    piece = weight_piece(here.reshape(1), codes, scales, size)
+    sends, rstd, cot_copy = norm_rows(hidden, gain, cot, piece, n, m)
     own_start = (z * (d // n) + jnp.arange(d // n // 256, dtype=jnp.int32) * 256).reshape(1, -1)
     first = own_part(own_start, hidden, gain, rstd, cot, codes, scales, rstd)
     slots = ring(piece, n, [rstd])
@@ -428,9 +424,8 @@
     theirs.append(flip(away, (1, 1)))
     ours.append(keep)
     parts.append(to_owners(1))
-    (away,) = node_sums(2, [1 - core], [keep])
+    away, keep = node_sums(2, [1 - core, core], [keep])
     theirs.append(flip(away, (1, 1)))
-    (keep,) = node_sums(2, [core], [away])
     ours.append(keep)
     parts.append(to_owners(2))
     scale = 1.0 / (m * n)

time: 217 us -> 216 us (level)
  other arithmetic: 12.9 us -> 10.1 us
  waiting for transfers between devices: 82.7 us -> 85.5 us
  Pallas kernels: 69.7 us -> 67.1 us
    pallas_call x4 -> x3, Pallas kernels: 25 us -> 22.5 us  [node_sum(): pl.pallas_call(functools.partial(grad_kernel, n, m, len(after)), in_specs...]
    unnamed x40 -> x42, local copies, waits for them, and re-layouts: 5.78 us -> 5.75 us
  transfers between devices with their start and end apart: 33 -> 33, of which waited for: 17 -> 17; matrix products, arithmetic and copies ran while one was open for 4% -> 3% of each run, Pallas kernels for 31% -> 30%
where the time goes in v4:
time: 216 us
  waiting for transfers between devices  85.5 us (40%)
  Pallas kernels  67.1 us (31%)
  starting transfers between devices  45.6 us (21%)
  other arithmetic  10.1 us (5%)
  local copies, waits for them, and re-layouts  6.42 us (3%)
    ppermute x6, waiting for transfers between devices, shift(): return lax.ppermute(x, 'node', [(i, (i + by) % n) for i in range(n)])  30.9 us
    ppermute x19, waiting for transfers between devices, flip(): return lax.ppermute(value, 'dp', [(i, i ^ bits[i % 2]) for i in range(m)])  29.9 us
    pallas_call x3, Pallas kernels, node_sum(): pl.pallas_call(functools.partial(grad_kernel, n, m, len(after)), in_specs...  22.5 us
    ppermute x19, starting transfers between devices, flip(): return lax.ppermute(value, 'dp', [(i, i ^ bits[i % 2]) for i in range(m)])  21.2 us
    ppermute x5, waiting for transfers between devices, exchange_sum(): lax.ppermute(value, axis, [(i, i ^ 1 << step) for i in range(size)])  13.1 us
    pallas_call x1, Pallas kernels, more_part(): pl.pallas_call(functools.partial(more_kernel, count, slot), in_specs=[SME...  12.5 us
    all_to_all x3, waiting for transfers between devices, rows_to_owners(): return lax.all_to_all(rows, 'node', split_axis=0, concat_axis=0, tiled=True)  11.6 us
    all_to_all x3, starting transfers between devices, rows_to_owners(): return lax.all_to_all(rows, 'node', split_axis=0, concat_axis=0, tiled=True)  11.3 us
  transfers between devices with their start and end apart: 33, of which 17 were waited for; matrix products, arithmetic and copies ran while one was open for 3% of the time, Pallas kernels for 30%

profile of v4, /device:TPU:0, one launch (start us, length us, event | category | flops | bytes accessed | tf_op | source)
XLA Modules:
  0.0 215.6 jit_solution(4077831576521876394)
XLA Ops:
  0.6 2.2 %weight_piece.1.after = bf16[256,1024]{1,0:T(8,128)(2,1)} custom-call(s32[1]{0:T(128)} %bitcast.12.which, bf16[2048,1024]{1,0:T(8,128)(2,1)} %codes.3, f32[4,2048]{1,0:T(4,128)} %bitcast.24), custom_call_target="tpu_custom_call" | custom-call | flops 1000 | bytes 1000 | tf_op jit(solution)/shard_map/weight_piece/pallas_call | solution.py:46
  2.9 3.0 %collective-permute-start = (bf16[256,1024]{1,0:T(8,128)(2,1)}, bf16[256,1024]{1,0:T(8,128)(2,1)S(1)}, u32[]{:S(2)}, u32[]{:S(2)}) collective-permute-start(bf16[256,1024]{1,0:T(8,128)(2,1)} %weight_piece.1.after), channel_id=1, source_target_pairs={{0,1},{1,2},{2,3},{3,0},{4,5},{5,6},{6,7},{7,4},{8,9},{9,10},{10,1... | collective-permute-start | bytes 1572872 | tf_op jit(solution)/shard_map/ppermute | solution.py:320
  5.9 2.0 collective-permute-start.2
  7.9 0.6 reshape.35
  8.5 9.7 %norm_rows.1 = (bf16[4,1024,256]{2,1,0:T(8,128)(2,1)}, bf16[4,768,256]{2,1,0:T(8,128)(2,1)}, bf16[4,256,256]{2,1,0:T(8,128)(2,1)}, f32[256,128]{1,0:T(8,128)}, bf16[256,1024]{1,0:T(8,128)(2,1)}) custom-call(bf16[256,8192]{1,0:T(8,128)(2,1)} %refs_3_.1, f32[1,8192]{1,0:T(1,128)} %bitcast.20, bf16[256,1024]{1,0:T(8,128)(2,1)} %refs_0_.5, ...), custom_call_target="tpu_custom_call" | custom-call | flops 1000 | bytes 1000 | tf_op jit(solution)/shard_map/norm_rows/pallas_call | solution.py:96
  18.3 2.6 %collective-permute-done.refs_0_ = bf16[256,1024]{1,0:T(8,128)(2,1)S(1)} collective-permute-done((bf16[256,1024]{1,0:T(8,128)(2,1)}, bf16[256,1024]{1,0:T(8,128)(2,1)S(1)}, u32[]{:S(2)}, u32[]{:S(2)}) %collective-permute-start) | collective-permute-done | bytes 524320 | tf_op jit(solution)/shard_map/ppermute | solution.py:320
  20.9 0.8 copy-done.2
  21.7 0.6 multiply_add_fusion.starts.refs_1_
  22.3 9.4 %own_part.1 = (f32[256,1024]{1,0:T(8,128)}, f32[1,8192]{1,0:T(1,128)}, f32[256,128]{1,0:T(8,128)}, bf16[256,2048]{1,0:T(8,128)(2,1)}) custom-call(s32[1,8]{1,0:T(1,128)} %multiply_add_fusion.starts.refs_1_, bf16[256,8192]{1,0:T(8,128)(2,1)} %refs_3_.1, f32[1,8192]{1,0:T(1,128)} %bitcast.21, f32[256,128]{1,0:T(8,128)} %get-tuple-element.26.rstd.after.refs_1_.refs_5_, ...), custom_call_target="tpu_custom_call" | custom-call | flops 1000 | bytes 1000 | tf_op jit(solution)/shard_map/own_part/pallas_call | solution.py:192
  31.7 0.8 copy-done.8
  32.5 10.0 %collective-permute-done.1 = bf16[256,1024]{1,0:T(8,128)(2,1)S(1)} collective-permute-done((bf16[256,1024]{1,0:T(8,128)(2,1)}, bf16[256,1024]{1,0:T(8,128)(2,1)S(1)}, u32[]{:S(2)}, u32[]{:S(2)}) %collective-permute-start.1) | collective-permute-done | bytes 524320 | tf_op jit(solution)/shard_map/ppermute | solution.py:320
  42.6 2.5 %pad_maximum_fusion.refs_0_.refs_1_ = bf16[768,1024]{1,0:T(8,128)(2,1)} fusion(bf16[256,1024]{1,0:T(8,128)(2,1)} %copy-done.8, bf16[256,1024]{1,0:T(8,128)(2,1)S(1)} %collective-permute-done.1, bf16[256,1024]{1,0:T(8,128)(2,1)} %gate.9), kind=kLoop, calls=%fused_computation | loop fusion | flops 4718592 | bytes 3145728 | tf_op jit(solution)/shard_map/concatenate | solution.py:363
  45.1 1.5 collective-permute-start.4
  46.6 0.5 collective-permute-start.10
  47.1 3.3 %collective-permute-start.12 = (bf16[256,1024]{1,0:T(8,128)(2,1)S(1)}, bf16[256,1024]{1,0:T(8,128)(2,1)S(1)}, u32[]{:S(2)}, u32[]{:S(2)}) collective-permute-start(bf16[256,1024]{1,0:T(8,128)(2,1)S(1)} %copy-done.16), channel_id=1, source_target_pairs={{0,3},{1,0},{2,1},{3,2},{4,7},{5,4},{6,5},{7,6},{8,11},{9,8},{10,9... | collective-permute-start | bytes 1572872 | tf_op jit(solution)/shard_map/ppermute | solution.py:320
  50.4 12.8 %collective-permute-done.10.refs_3_.refs_1_ = bf16[256,1024]{1,0:T(8,128)(2,1)S(1)} collective-permute-done((bf16[256,1024]{1,0:T(8,128)(2,1)S(1)}, bf16[256,1024]{1,0:T(8,128)(2,1)S(1)}, u32[]{:S(2)}, u32[]{:S(2)}) %collective-permute-start.10) | collective-permute-done | bytes 524320 | tf_op jit(solution)/shard_map/ppermute | solution.py:320
  63.2 3.4 %collective-permute-start.6 = (bf16[768,1024]{1,0:T(8,128)(2,1)}, bf16[768,1024]{1,0:T(8,128)(2,1)}, u32[]{:S(2)}, u32[]{:S(2)}) collective-permute-start(bf16[768,1024]{1,0:T(8,128)(2,1)} %pad_maximum_fusion.refs_0_.refs_1_), channel_id=1, source_target_pairs={{0,16},{4,12},{8,24},{12,4},{16,0},{20,28},{24,8},{28,20},{1,17},{... | collective-permute-start | bytes 4718600 | tf_op jit(solution)/shard_map/ppermute | solution.py:347
  66.7 5.6 %collective-permute-done.4.refs_2_ = bf16[768,1024]{1,0:T(8,128)(2,1)} collective-permute-done((bf16[768,1024]{1,0:T(8,128)(2,1)}, bf16[768,1024]{1,0:T(8,128)(2,1)}, u32[]{:S(2)}, u32[]{:S(2)}) %collective-permute-start.4) | collective-permute-done | bytes 1572896 | tf_op jit(solution)/shard_map/ppermute | solution.py:347
  72.3 3.5 %collective-permute-start.8 = (bf16[768,1024]{1,0:T(8,128)(2,1)}, bf16[768,1024]{1,0:T(8,128)(2,1)}, u32[]{:S(2)}, u32[]{:S(2)}) collective-permute-start(bf16[768,1024]{1,0:T(8,128)(2,1)} %collective-permute-done.4.refs_2_), channel_id=1, source_target_pairs={{0,16},{4,12},{8,24},{12,4},{16,0},{20,28},{24,8},{28,20},{1,17},{... | collective-permute-start | bytes 4718600 | tf_op jit(solution)/shard_map/ppermute | solution.py:347
  75.9 5.4 %collective-permute-done.11.refs_4_.refs_2_ = bf16[256,1024]{1,0:T(8,128)(2,1)S(1)} collective-permute-done((bf16[256,1024]{1,0:T(8,128)(2,1)S(1)}, bf16[256,1024]{1,0:T(8,128)(2,1)S(1)}, u32[]{:S(2)}, u32[]{:S(2)}) %collective-permute-start.11) | collective-permute-done | bytes 524320 | tf_op jit(solution)/shard_map/ppermute | solution.py:320
  81.2 0.8 copy-done.5
  82.0 3.8 %all-to-all-start = ((bf16[4,1024,256]{2,1,0:T(8,128)(2,1)}), bf16[4,1024,256]{2,1,0:T(8,128)(2,1)S(1)}, u32[]{:S(2)}, u32[]{:S(2)}) async-start(bf16[4,1024,256]{2,1,0:T(8,128)(2,1)} %gate.12), calls=%async_computation | async-start | bytes 4194304 | tf_op jit(solution)/shard_map/all_to_all | solution.py:360
  85.9 0.5 collective-permute-start.5
  86.5 15.8 %collective-permute-done.8.refs_0_ = bf16[768,1024]{1,0:T(8,128)(2,1)} collective-permute-done((bf16[768,1024]{1,0:T(8,128)(2,1)}, bf16[768,1024]{1,0:T(8,128)(2,1)}, u32[]{:S(2)}, u32[]{:S(2)}) %collective-permute-start.8) | collective-permute-done | bytes 1572896 | tf_op jit(solution)/shard_map/ppermute | solution.py:347
  102.5 0.6 slice.78.refs_0_
  103.1 12.5 %more_part.1 = (f32[256,1024]{1,0:T(8,128)}, f32[1,8192]{1,0:T(1,128)}, f32[256,128]{1,0:T(8,128)}, bf16[256,4608]{1,0:T(8,128)(2,1)}) custom-call(s32[6,3]{1,0:T(8,128)} %bitcast.26, bf16[256,8192]{1,0:T(8,128)(2,1)} %refs_3_.1, f32[1,8192]{1,0:T(1,128)} %bitcast.22, f32[256,128]{1,0:T(8,128)} %get-tuple-element.26.rstd.after.refs_1_.refs_5_, ...), custom_call_target="tpu_custom_call" | custom-call | flops 1000 | bytes 1000 | tf_op jit(solution)/shard_map/more_part/pallas_call | solution.py:226
  115.6 10.8 %last_part.1 = (bf16[256,1024]{1,0:T(8,128)(2,1)}, f32[1,8192]{1,0:T(1,128)}, bf16[256,8192]{1,0:T(8,128)(2,1)}) custom-call(s32[2,3]{1,0:T(2,128)} %slice.78.refs_0_, s32[1,8]{1,0:T(1,128)} %multiply_add_fusion.starts.refs_1_, s32[6,3]{1,0:T(8,128)} %bitcast.27, bf16[256,8192]{1,0:T(8,128)(2,1)} %refs_3_.1, f32[1,8192]{1,0:T(1,128)} %bitcast.23, ...), custom_call_target="tpu_custom_call" | custom-call | flops 1000 | bytes 1000 | tf_op jit(solution)/shard_map/last_part/pallas_call | solution.py:273
  126.4 4.1 %all-to-all-done.rows.refs_1_ = bf16[4,1024,256]{2,1,0:T(8,128)(2,1)S(1)} async-done(((bf16[4,1024,256]{2,1,0:T(8,128)(2,1)}), bf16[4,1024,256]{2,1,0:T(8,128)(2,1)S(1)}, u32[]{:S(2)}, u32[]{:S(2)}) %all-to-all-start) | async-done | bytes 2097184 | tf_op jit(solution)/shard_map/all_to_all | solution.py:360
  130.5 1.3 copy-done
  131.8 3.8 %all-to-all-start.1 = ((bf16[4,768,256]{2,1,0:T(8,128)(2,1)}), bf16[4,768,256]{2,1,0:T(8,128)(2,1)S(1)}, u32[]{:S(2)}, u32[]{:S(2)}) async-start(bf16[4,768,256]{2,1,0:T(8,128)(2,1)} %gate.13), calls=%async_computation.1 | async-start | bytes 3145728 | tf_op jit(solution)/shard_map/all_to_all | solution.py:360
  135.6 0.7 pad_add_fusion.1.me
  136.3 9.9 %node_sum.3 = (bf16[512,1024]{1,0:T(8,128)(2,1)}, bf16[512,1024]{1,0:T(8,128)(2,1)}) custom-call(s32[4]{0:T(128)} %pad_add_fusion.1.me, bf16[4,1024,256]{2,1,0:T(8,128)(2,1)} %copy-done, bf16[256,1024]{1,0:T(8,128)(2,1)} %refs_0_.5, bf16[256,1024]{1,0:T(8,128)(2,1)} %copy-done.3, bf16[256,1024]{1,0:T(8,128)(2,1)} %copy-done.5, bf16[256,1024]{1,0:T(8,128)(2,1)} %copy-done.4, ...), custom_call_target="tpu_custom_call" | custom-call | flops 1000 | bytes 1000 | tf_op jit(solution)/shard_map/node_sum/pallas_call | solution.py:134
  146.2 2.9 %collective-permute-done.13 = bf16[512,1024]{1,0:T(8,128)(2,1)S(1)} collective-permute-done((bf16[512,1024]{1,0:T(8,128)(2,1)}, bf16[512,1024]{1,0:T(8,128)(2,1)S(1)}, u32[]{:S(2)}, u32[]{:S(2)}) %collective-permute-start.13) | collective-permute-done | bytes 1048608 | tf_op jit(solution)/shard_map/ppermute | solution.py:347
  149.0 1.4 add_convert_fusion
  150.4 1.9 collective-permute-start.14
  152.5 1.5 collective-permute-start.16
  154.0 1.2 collective-permute-done.21
  155.2 1.9 collective-permute-start.22
  157.2 8.2 %collective-permute-done.22 = f32[1,8192]{1,0:T(1,128)S(1)} collective-permute-done((f32[1,8192]{1,0:T(1,128)S(1)}, f32[1,8192]{1,0:T(1,128)S(1)}, u32[]{:S(2)}, u32[]{:S(2)}) %collective-permute-start.22) | collective-permute-done | bytes 32800 | tf_op jit(solution)/shard_map/ppermute | solution.py:314
  165.4 0.2 collective-permute-start.23
  165.6 3.8 %collective-permute-done.23 = f32[1,8192]{1,0:T(1,128)S(1)} collective-permute-done((f32[1,8192]{1,0:T(1,128)S(1)}, f32[1,8192]{1,0:T(1,128)S(1)}, u32[]{:S(2)}, u32[]{:S(2)}) %collective-permute-start.23) | collective-permute-done | bytes 32800 | tf_op jit(solution)/shard_map/ppermute | solution.py:314
  169.3 0.6 add.137.refs_3_.refs_0_
  170.0 1.9 all-to-all-done.1.rows.refs_1_
  172.0 1.2 copy-done.1
  173.1 3.7 %all-to-all-start.2 = ((bf16[4,256,256]{2,1,0:T(8,128)(2,1)}), bf16[4,256,256]{2,1,0:T(8,128)(2,1)S(1)}, u32[]{:S(2)}, u32[]{:S(2)}) async-start(bf16[4,256,256]{2,1,0:T(8,128)(2,1)} %gate.14), calls=%async_computation.2 | async-start | bytes 1048576 | tf_op jit(solution)/shard_map/all_to_all | solution.py:360
  176.9 8.1 %node_sum.4 = (bf16[384,1024]{1,0:T(8,128)(2,1)}, bf16[384,1024]{1,0:T(8,128)(2,1)}) custom-call(s32[4]{0:T(128)} %pad_add_fusion.1.me, bf16[4,768,256]{2,1,0:T(8,128)(2,1)} %copy-done.1, bf16[256,1024]{1,0:T(8,128)(2,1)} %refs_0_.5, bf16[256,1024]{1,0:T(8,128)(2,1)} %copy-done.3, bf16[256,1024]{1,0:T(8,128)(2,1)} %copy-done.5, bf16[256,1024]{1,0:T(8,128)(2,1)} %copy-done.4, ...), custom_call_target="tpu_custom_call" | custom-call | flops 1000 | bytes 1000 | tf_op jit(solution)/shard_map/node_sum/pallas_call | solution.py:134
  185.0 5.6 %all-to-all-done.2.rows.refs_1_ = bf16[4,256,256]{2,1,0:T(8,128)(2,1)S(1)} async-done(((bf16[4,256,256]{2,1,0:T(8,128)(2,1)}), bf16[4,256,256]{2,1,0:T(8,128)(2,1)S(1)}, u32[]{:S(2)}, u32[]{:S(2)}) %all-to-all-start.2) | async-done | bytes 524320 | tf_op jit(solution)/shard_map/all_to_all | solution.py:360
  190.5 0.8 copy-done.6
  191.4 1.2 add_multiply_fusion
  192.6 4.5 %node_sum.5 = (bf16[128,1024]{1,0:T(8,128)(2,1)}, bf16[128,1024]{1,0:T(8,128)(2,1)}) custom-call(s32[4]{0:T(128)} %pad_add_fusion.1.me, bf16[4,256,256]{2,1,0:T(8,128)(2,1)} %copy-done.6, bf16[256,1024]{1,0:T(8,128)(2,1)} %refs_0_.5, bf16[256,1024]{1,0:T(8,128)(2,1)} %copy-done.3, bf16[256,1024]{1,0:T(8,128)(2,1)} %copy-done.5, bf16[256,1024]{1,0:T(8,128)(2,1)} %copy-done.4, ...), custom_call_target="tpu_custom_call" | custom-call | flops 1000 | bytes 1000 | tf_op jit(solution)/shard_map/node_sum/pallas_call | solution.py:134
  197.1 2.1 collective-permute-start.29
  199.2 0.2 add_convert_fusion.5
  199.4 1.5 collective-permute-start.20
  200.9 1.7 collective-permute-start.19
  202.7 0.3 collective-permute-start.18
  203.0 0.7 add_multiply_fusion.3
  203.7 1.5 collective-permute-start.27
  205.2 1.7 collective-permute-start.26
  207.0 1.2 collective-permute-done.20
  208.2 1.7 collective-permute-start.25
  209.9 2.6 %collective-permute-done.19 = bf16[96,1024]{1,0:T(8,128)(2,1)S(1)} collective-permute-done((bf16[96,1024]{1,0:T(8,128)(2,1)S(1)}, bf16[96,1024]{1,0:T(8,128)(2,1)S(1)}, u32[]{:S(2)}, u32[]{:S(2)}) %collective-permute-start.19) | collective-permute-done | bytes 196640 | tf_op jit(solution)/shard_map/ppermute | solution.py:347
  212.6 1.3 collective-permute-done.27
  213.9 0.6 collective-permute-done.26
  214.5 1.1 pad_maximum_fusion.1
  (80 shorter events, 1.0 us)
Async XLA Ops:
  0.6 7.3 %copy-start.20 = (bf16[8192]{0:T(1024)(128)(2,1)S(1)}, bf16[8192]{0:T(1024)(128)(2,1)}, u32[]{:S(2)}) copy-start(bf16[8192]{0:T(1024)(128)(2,1)} %param.6) | copy-start | bytes 49156
  2.9 18.1 %collective-permute-start = (bf16[256,1024]{1,0:T(8,128)(2,1)}, bf16[256,1024]{1,0:T(8,128)(2,1)S(1)}, u32[]{:S(2)}, u32[]{:S(2)}) collective-permute-start(bf16[256,1024]{1,0:T(8,128)(2,1)} %weight_piece.1.after), channel_id=1, source_target_pairs={{0,1},{1,2},{2,3},{3,0},{4,5},{5,6},{6,7},{7,4},{8,9},{9,10},{10,1... | collective-permute-start | bytes 1572872 | tf_op jit(solution)/shard_map/ppermute | solution.py:320
  5.9 25.9 %collective-permute-start.2 = (bf16[256,1024]{1,0:T(8,128)(2,1)}, bf16[256,1024]{1,0:T(8,128)(2,1)S(1)}, u32[]{:S(2)}, u32[]{:S(2)}) collective-permute-start(bf16[256,1024]{1,0:T(8,128)(2,1)} %weight_piece.1.after), channel_id=1, source_target_pairs={{0,3},{1,0},{2,1},{3,2},{4,7},{5,4},{6,5},{7,6},{8,11},{9,8},{10,9... | collective-permute-start | bytes 1572872 | tf_op jit(solution)/shard_map/ppermute | solution.py:320
  20.9 0.8 copy-start.2
  21.7 20.8 %collective-permute-start.1 = (bf16[256,1024]{1,0:T(8,128)(2,1)}, bf16[256,1024]{1,0:T(8,128)(2,1)S(1)}, u32[]{:S(2)}, u32[]{:S(2)}) collective-permute-start(bf16[256,1024]{1,0:T(8,128)(2,1)} %gate.8.refs_0_.refs_1_), channel_id=1, source_target_pairs={{0,1},{1,2},{2,3},{3,0},{4,5},{5,6},{6,7},{7,4},{8,9},{9,10},{10,1... | collective-permute-start | bytes 1572872 | tf_op jit(solution)/shard_map/ppermute | solution.py:320
  31.7 0.8 copy-start.8
  42.6 4.0 %copy-start.16 = (bf16[256,1024]{1,0:T(8,128)(2,1)S(1)}, bf16[256,1024]{1,0:T(8,128)(2,1)}, u32[]{:S(2)}) copy-start(bf16[256,1024]{1,0:T(8,128)(2,1)} %gate.11) | copy-start | bytes 1572868
  45.1 27.2 %collective-permute-start.4 = (bf16[768,1024]{1,0:T(8,128)(2,1)}, bf16[768,1024]{1,0:T(8,128)(2,1)}, u32[]{:S(2)}, u32[]{:S(2)}) collective-permute-start(bf16[768,1024]{1,0:T(8,128)(2,1)} %pad_maximum_fusion.refs_0_.refs_1_), channel_id=1, source_target_pairs={{0,8},{4,20},{8,0},{12,28},{16,24},{20,4},{24,16},{28,12},{1,9},{5... | collective-permute-start | bytes 4718600 | tf_op jit(solution)/shard_map/ppermute | solution.py:347
  46.6 16.7 %collective-permute-start.10 = (bf16[256,1024]{1,0:T(8,128)(2,1)S(1)}, bf16[256,1024]{1,0:T(8,128)(2,1)S(1)}, u32[]{:S(2)}, u32[]{:S(2)}) collective-permute-start(bf16[256,1024]{1,0:T(8,128)(2,1)S(1)} %copy-done.16), channel_id=1, source_target_pairs={{0,1},{1,2},{2,3},{3,0},{4,5},{5,6},{6,7},{7,4},{8,9},{9,10},{10,1... | collective-permute-start | bytes 1572872 | tf_op jit(solution)/shard_map/ppermute | solution.py:320
  47.1 28.7 %collective-permute-start.12 = (bf16[256,1024]{1,0:T(8,128)(2,1)S(1)}, bf16[256,1024]{1,0:T(8,128)(2,1)S(1)}, u32[]{:S(2)}, u32[]{:S(2)}) collective-permute-start(bf16[256,1024]{1,0:T(8,128)(2,1)S(1)} %copy-done.16), channel_id=1, source_target_pairs={{0,3},{1,0},{2,1},{3,2},{4,7},{5,4},{6,5},{7,6},{8,11},{9,8},{10,9... | collective-permute-start | bytes 1572872 | tf_op jit(solution)/shard_map/ppermute | solution.py:320
  63.2 18.0 %copy-start.3 = (bf16[256,1024]{1,0:T(8,128)(2,1)}, bf16[256,1024]{1,0:T(8,128)(2,1)S(1)}, u32[]{:S(2)}) copy-start(bf16[256,1024]{1,0:T(8,128)(2,1)S(1)} %collective-permute-done.10.refs_3_.refs_1_) | copy-start | bytes 1572868
  63.2 18.0 %collective-permute-start.11 = (bf16[256,1024]{1,0:T(8,128)(2,1)S(1)}, bf16[256,1024]{1,0:T(8,128)(2,1)S(1)}, u32[]{:S(2)}, u32[]{:S(2)}) collective-permute-start(bf16[256,1024]{1,0:T(8,128)(2,1)S(1)} %collective-permute-done.10.refs_3_.refs_1_), channel_id=1, source_target_pairs={{0,1},{1,2},{2,3},{3,0},{4,5},{5,6},{6,7},{7,4},{8,9},{9,10},{10,1... | collective-permute-start | bytes 1572872 | tf_op jit(solution)/shard_map/ppermute | solution.py:320
  63.2 23.2 %collective-permute-start.6 = (bf16[768,1024]{1,0:T(8,128)(2,1)}, bf16[768,1024]{1,0:T(8,128)(2,1)}, u32[]{:S(2)}, u32[]{:S(2)}) collective-permute-start(bf16[768,1024]{1,0:T(8,128)(2,1)} %pad_maximum_fusion.refs_0_.refs_1_), channel_id=1, source_target_pairs={{0,16},{4,12},{8,24},{12,4},{16,0},{20,28},{24,8},{28,20},{1,17},{... | collective-permute-start | bytes 4718600 | tf_op jit(solution)/shard_map/ppermute | solution.py:347
  72.3 29.9 %collective-permute-start.8 = (bf16[768,1024]{1,0:T(8,128)(2,1)}, bf16[768,1024]{1,0:T(8,128)(2,1)}, u32[]{:S(2)}, u32[]{:S(2)}) collective-permute-start(bf16[768,1024]{1,0:T(8,128)(2,1)} %collective-permute-done.4.refs_2_), channel_id=1, source_target_pairs={{0,16},{4,12},{8,24},{12,4},{16,0},{20,28},{24,8},{28,20},{1,17},{... | collective-permute-start | bytes 4718600 | tf_op jit(solution)/shard_map/ppermute | solution.py:347
  75.8 5.4 %copy-start.4 = (bf16[256,1024]{1,0:T(8,128)(2,1)}, bf16[256,1024]{1,0:T(8,128)(2,1)S(1)}, u32[]{:S(2)}) copy-start(bf16[256,1024]{1,0:T(8,128)(2,1)S(1)} %collective-permute-done.12.refs_5_.refs_3_) | copy-start | bytes 1572868
  81.2 0.8 copy-start.5
  82.0 48.4 %all-to-all-start = ((bf16[4,1024,256]{2,1,0:T(8,128)(2,1)}), bf16[4,1024,256]{2,1,0:T(8,128)(2,1)S(1)}, u32[]{:S(2)}, u32[]{:S(2)}) async-start(bf16[4,1024,256]{2,1,0:T(8,128)(2,1)} %gate.12), calls=%async_computation | async-start | bytes 4194304 | tf_op jit(solution)/shard_map/all_to_all | solution.py:360
  85.8 17.3 %collective-permute-start.3 = (bf16[768,1024]{1,0:T(8,128)(2,1)}, bf16[768,1024]{1,0:T(8,128)(2,1)}, u32[]{:S(2)}, u32[]{:S(2)}) collective-permute-start(bf16[768,1024]{1,0:T(8,128)(2,1)} %pad_maximum_fusion.refs_0_.refs_1_), channel_id=1, source_target_pairs={{0,4},{4,0},{8,12},{12,8},{16,20},{20,16},{24,28},{28,24},{1,5},{5... | collective-permute-start | bytes 4718600 | tf_op jit(solution)/shard_map/ppermute | solution.py:347
  85.9 17.2 %collective-permute-start.5 = (bf16[768,1024]{1,0:T(8,128)(2,1)}, bf16[768,1024]{1,0:T(8,128)(2,1)}, u32[]{:S(2)}, u32[]{:S(2)}) collective-permute-start(bf16[768,1024]{1,0:T(8,128)(2,1)} %collective-permute-done.4.refs_2_), channel_id=1, source_target_pairs={{0,4},{4,0},{8,12},{12,8},{16,20},{20,16},{24,28},{28,24},{1,5},{5... | collective-permute-start | bytes 4718600 | tf_op jit(solution)/shard_map/ppermute | solution.py:347
  86.4 16.7 %collective-permute-start.7 = (bf16[768,1024]{1,0:T(8,128)(2,1)}, bf16[768,1024]{1,0:T(8,128)(2,1)}, u32[]{:S(2)}, u32[]{:S(2)}) collective-permute-start(bf16[768,1024]{1,0:T(8,128)(2,1)} %collective-permute-done.6.refs_4_), channel_id=1, source_target_pairs={{0,4},{4,0},{8,12},{12,8},{16,20},{20,16},{24,28},{28,24},{1,5},{5... | collective-permute-start | bytes 4718600 | tf_op jit(solution)/shard_map/ppermute | solution.py:347
  102.2 13.4 %collective-permute-start.9 = (bf16[768,1024]{1,0:T(8,128)(2,1)}, bf16[768,1024]{1,0:T(8,128)(2,1)}, u32[]{:S(2)}, u32[]{:S(2)}) collective-permute-start(bf16[768,1024]{1,0:T(8,128)(2,1)} %collective-permute-done.8.refs_0_), channel_id=1, source_target_pairs={{0,4},{4,0},{8,12},{12,8},{16,20},{20,16},{24,28},{28,24},{1,5},{5... | collective-permute-start | bytes 4718600 | tf_op jit(solution)/shard_map/ppermute | solution.py:347
  102.5 0.6 copy-start.19
  130.5 1.3 copy-start
  131.8 40.1 %all-to-all-start.1 = ((bf16[4,768,256]{2,1,0:T(8,128)(2,1)}), bf16[4,768,256]{2,1,0:T(8,128)(2,1)S(1)}, u32[]{:S(2)}, u32[]{:S(2)}) async-start(bf16[4,768,256]{2,1,0:T(8,128)(2,1)} %gate.13), calls=%async_computation.1 | async-start | bytes 3145728 | tf_op jit(solution)/shard_map/all_to_all | solution.py:360
  146.2 7.8 %copy-start.17 = (f32[1,8192]{1,0:T(1,128)S(1)}, f32[1,8192]{1,0:T(1,128)}, u32[]{:S(2)}) copy-start(f32[1,8192]{1,0:T(1,128)} %get-tuple-element.39.refs_4_.refs_2_) | copy-start | bytes 98308
  146.2 2.9 %collective-permute-start.13 = (bf16[512,1024]{1,0:T(8,128)(2,1)}, bf16[512,1024]{1,0:T(8,128)(2,1)S(1)}, u32[]{:S(2)}, u32[]{:S(2)}) collective-permute-start(bf16[512,1024]{1,0:T(8,128)(2,1)} %get-tuple-element.41), channel_id=1, source_target_pairs={{0,4},{4,0},{8,12},{12,8},{16,20},{20,16},{24,28},{28,24},{1,5},{5... | collective-permute-start | bytes 3145736 | tf_op jit(solution)/shard_map/ppermute | solution.py:347
  150.4 19.6 %collective-permute-start.14 = (bf16[128,1024]{1,0:T(8,128)(2,1)S(1)}, bf16[128,1024]{1,0:T(8,128)(2,1)S(1)}, u32[]{:S(2)}, u32[]{:S(2)}) collective-permute-start(bf16[128,1024]{1,0:T(8,128)(2,1)S(1)} %get-tuple-element.50), channel_id=1, source_target_pairs={{0,8},{4,12},{8,0},{12,4},{16,24},{20,28},{24,16},{28,20},{1,9},{5... | collective-permute-start | bytes 786440 | tf_op jit(solution)/shard_map/ppermute | solution.py:347
  152.4 17.6 %collective-permute-start.15 = (bf16[128,1024]{1,0:T(8,128)(2,1)S(1)}, bf16[128,1024]{1,0:T(8,128)(2,1)S(1)}, u32[]{:S(2)}, u32[]{:S(2)}) collective-permute-start(bf16[128,1024]{1,0:T(8,128)(2,1)S(1)} %get-tuple-element.49), channel_id=1, source_target_pairs={{0,16},{4,20},{8,24},{12,28},{16,0},{20,4},{24,8},{28,12},{1,17},{... | collective-permute-start | bytes 786440 | tf_op jit(solution)/shard_map/ppermute | solution.py:347
  152.5 17.5 %collective-permute-start.16 = (bf16[128,1024]{1,0:T(8,128)(2,1)S(1)}, bf16[128,1024]{1,0:T(8,128)(2,1)S(1)}, u32[]{:S(2)}, u32[]{:S(2)}) collective-permute-start(bf16[128,1024]{1,0:T(8,128)(2,1)S(1)} %get-tuple-element.48), channel_id=1, source_target_pairs={{0,24},{4,28},{8,16},{12,20},{16,8},{20,12},{24,0},{28,4},{1,25},{... | collective-permute-start | bytes 786440 | tf_op jit(solution)/shard_map/ppermute | solution.py:347
  154.0 1.2 collective-permute-start.21
  155.2 10.1 %collective-permute-start.22 = (f32[1,8192]{1,0:T(1,128)S(1)}, f32[1,8192]{1,0:T(1,128)S(1)}, u32[]{:S(2)}, u32[]{:S(2)}) collective-permute-start(f32[1,8192]{1,0:T(1,128)S(1)} %add.135), channel_id=1, source_target_pairs={{0,8},{4,12},{8,0},{12,4},{16,24},{20,28},{24,16},{28,20},{1,9},{5... | collective-permute-start | bytes 98312 | tf_op jit(solution)/shard_map/ppermute | solution.py:314
  165.4 4.0 %collective-permute-start.23 = (f32[1,8192]{1,0:T(1,128)S(1)}, f32[1,8192]{1,0:T(1,128)S(1)}, u32[]{:S(2)}, u32[]{:S(2)}) collective-permute-start(f32[1,8192]{1,0:T(1,128)S(1)} %add.136), channel_id=1, source_target_pairs={{0,16},{4,20},{8,24},{12,28},{16,0},{20,4},{24,8},{28,12},{1,17},{... | collective-permute-start | bytes 98312 | tf_op jit(solution)/shard_map/ppermute | solution.py:314
  170.0 1.9 copy-start.9
  170.0 1.9 copy-start.11
  170.0 1.9 copy-start.13
  171.9 1.2 copy-start.1
  173.1 17.4 %all-to-all-start.2 = ((bf16[4,256,256]{2,1,0:T(8,128)(2,1)}), bf16[4,256,256]{2,1,0:T(8,128)(2,1)S(1)}, u32[]{:S(2)}, u32[]{:S(2)}) async-start(bf16[4,256,256]{2,1,0:T(8,128)(2,1)} %gate.14), calls=%async_computation.2 | async-start | bytes 1048576 | tf_op jit(solution)/shard_map/all_to_all | solution.py:360
  176.9 14.5 %copy-start.10 = (bf16[128,1024]{1,0:T(8,128)(2,1)S(1)}, bf16[128,1024]{1,0:T(8,128)(2,1)}, u32[]{:S(2)}) copy-start(bf16[128,1024]{1,0:T(8,128)(2,1)} %copy-done.9) | copy-start | bytes 786436
  176.9 14.5 %copy-start.12 = (bf16[128,1024]{1,0:T(8,128)(2,1)S(1)}, bf16[128,1024]{1,0:T(8,128)(2,1)}, u32[]{:S(2)}) copy-start(bf16[128,1024]{1,0:T(8,128)(2,1)} %copy-done.11) | copy-start | bytes 786436
  176.9 14.5 %copy-start.14 = (bf16[128,1024]{1,0:T(8,128)(2,1)S(1)}, bf16[128,1024]{1,0:T(8,128)(2,1)}, u32[]{:S(2)}) copy-start(bf16[128,1024]{1,0:T(8,128)(2,1)} %copy-done.13) | copy-start | bytes 786436
  185.0 14.2 %collective-permute-start.17 = (bf16[384,1024]{1,0:T(8,128)(2,1)}, bf16[384,1024]{1,0:T(8,128)(2,1)S(1)}, u32[]{:S(2)}, u32[]{:S(2)}) collective-permute-start(bf16[384,1024]{1,0:T(8,128)(2,1)} %get-tuple-element.44), channel_id=1, source_target_pairs={{0,4},{4,0},{8,12},{12,8},{16,20},{20,16},{24,28},{28,24},{1,5},{5... | collective-permute-start | bytes 2359304 | tf_op jit(solution)/shard_map/ppermute | solution.py:347
  190.5 0.8 copy-start.6
  191.3 5.7 %collective-permute-start.28 = (f32[1,8192]{1,0:T(1,128)}, f32[1,8192]{1,0:T(1,128)S(1)}, u32[]{:S(2)}, u32[]{:S(2)}) collective-permute-start(f32[1,8192]{1,0:T(1,128)} %gate.15), channel_id=1, source_target_pairs={{0,1},{1,0},{2,3},{3,2},{4,5},{5,4},{6,7},{7,6},{8,9},{9,8},{10,11... | collective-permute-start | bytes 98312 | tf_op jit(solution)/shard_map/ppermute | solution.py:314
  192.5 4.5 %copy-start.15 = (f32[1,8192]{1,0:T(1,128)S(1)}, f32[1,8192]{1,0:T(1,128)}, u32[]{:S(2)}) copy-start(f32[1,8192]{1,0:T(1,128)} %gate.15) | copy-start | bytes 98308
  192.5 6.7 %copy-start.7 = (bf16[384,1024]{1,0:T(8,128)(2,1)S(1)}, bf16[384,1024]{1,0:T(8,128)(2,1)}, u32[]{:S(2)}) copy-start(bf16[384,1024]{1,0:T(8,128)(2,1)} %get-tuple-element.43.refs_4_) | copy-start | bytes 2359300
  197.1 6.6 %copy-start.18 = (bf16[128,1024]{1,0:T(8,128)(2,1)S(1)}, bf16[128,1024]{1,0:T(8,128)(2,1)}, u32[]{:S(2)}) copy-start(bf16[128,1024]{1,0:T(8,128)(2,1)} %get-tuple-element.46) | copy-start | bytes 786436
  197.1 6.6 %collective-permute-start.24 = (bf16[128,1024]{1,0:T(8,128)(2,1)}, bf16[128,1024]{1,0:T(8,128)(2,1)S(1)}, u32[]{:S(2)}, u32[]{:S(2)}) collective-permute-start(bf16[128,1024]{1,0:T(8,128)(2,1)} %get-tuple-element.47), channel_id=1, source_target_pairs={{0,4},{4,0},{8,12},{12,8},{16,20},{20,16},{24,28},{28,24},{1,5},{5... | collective-permute-start | bytes 786440 | tf_op jit(solution)/shard_map/ppermute | solution.py:347
  197.1 5.9 %collective-permute-start.29 = (f32[1,8192]{1,0:T(1,128)S(1)}, f32[1,8192]{1,0:T(1,128)S(1)}, u32[]{:S(2)}, u32[]{:S(2)}) collective-permute-start(f32[1,8192]{1,0:T(1,128)S(1)} %add.145), channel_id=1, source_target_pairs={{0,2},{1,3},{2,0},{3,1},{4,6},{5,7},{6,4},{7,5},{8,10},{9,11},{10,... | collective-permute-start | bytes 98312 | tf_op jit(solution)/shard_map/ppermute | solution.py:314
  199.4 8.7 %collective-permute-start.20 = (bf16[96,1024]{1,0:T(8,128)(2,1)S(1)}, bf16[96,1024]{1,0:T(8,128)(2,1)S(1)}, u32[]{:S(2)}, u32[]{:S(2)}) collective-permute-start(bf16[96,1024]{1,0:T(8,128)(2,1)S(1)} %get-tuple-element.52), channel_id=1, source_target_pairs={{0,24},{4,28},{8,16},{12,20},{16,8},{20,12},{24,0},{28,4},{1,25},{... | collective-permute-start | bytes 589832 | tf_op jit(solution)/shard_map/ppermute | solution.py:347
  200.9 11.5 %collective-permute-start.19 = (bf16[96,1024]{1,0:T(8,128)(2,1)S(1)}, bf16[96,1024]{1,0:T(8,128)(2,1)S(1)}, u32[]{:S(2)}, u32[]{:S(2)}) collective-permute-start(bf16[96,1024]{1,0:T(8,128)(2,1)S(1)} %get-tuple-element.53), channel_id=1, source_target_pairs={{0,16},{4,20},{8,24},{12,28},{16,0},{20,4},{24,8},{28,12},{1,17},{... | collective-permute-start | bytes 589832 | tf_op jit(solution)/shard_map/ppermute | solution.py:347
  202.7 9.8 %collective-permute-start.18 = (bf16[96,1024]{1,0:T(8,128)(2,1)S(1)}, bf16[96,1024]{1,0:T(8,128)(2,1)S(1)}, u32[]{:S(2)}, u32[]{:S(2)}) collective-permute-start(bf16[96,1024]{1,0:T(8,128)(2,1)S(1)} %get-tuple-element.51), channel_id=1, source_target_pairs={{0,8},{4,12},{8,0},{12,4},{16,24},{20,28},{24,16},{28,20},{1,9},{5... | collective-permute-start | bytes 589832 | tf_op jit(solution)/shard_map/ppermute | solution.py:347
  203.7 10.2 %collective-permute-start.27 = (bf16[32,1024]{1,0:T(8,128)(2,1)S(1)}, bf16[32,1024]{1,0:T(8,128)(2,1)S(1)}, u32[]{:S(2)}, u32[]{:S(2)}) collective-permute-start(bf16[32,1024]{1,0:T(8,128)(2,1)S(1)} %get-tuple-element.55), channel_id=1, source_target_pairs={{0,24},{4,28},{8,16},{12,20},{16,8},{20,12},{24,0},{28,4},{1,25},{... | collective-permute-start | bytes 196616 | tf_op jit(solution)/shard_map/ppermute | solution.py:347
  205.2 9.2 %collective-permute-start.26 = (bf16[32,1024]{1,0:T(8,128)(2,1)S(1)}, bf16[32,1024]{1,0:T(8,128)(2,1)S(1)}, u32[]{:S(2)}, u32[]{:S(2)}) collective-permute-start(bf16[32,1024]{1,0:T(8,128)(2,1)S(1)} %get-tuple-element.56), channel_id=1, source_target_pairs={{0,16},{4,20},{8,24},{12,28},{16,0},{20,4},{24,8},{28,12},{1,17},{... | collective-permute-start | bytes 196616 | tf_op jit(solution)/shard_map/ppermute | solution.py:347
  208.2 6.3 %collective-permute-start.25 = (bf16[32,1024]{1,0:T(8,128)(2,1)S(1)}, bf16[32,1024]{1,0:T(8,128)(2,1)S(1)}, u32[]{:S(2)}, u32[]{:S(2)}) collective-permute-start(bf16[32,1024]{1,0:T(8,128)(2,1)S(1)} %get-tuple-element.54), channel_id=1, source_target_pairs={{0,8},{4,12},{8,0},{12,4},{16,24},{20,28},{24,16},{28,20},{1,9},{5... | collective-permute-start | bytes 196616 | tf_op jit(solution)/shard_map/ppermute | solution.py:347
